TPU v7x, 128 devices: a whole 4x4x4 slice. The times are simulated.
128 devices in a mesh: dp: 4 (over z), ctx: 32 (over y, x, core).
Axes of the slice: x: 4, y: 4, z: 4, core: 2. Of those that a mesh axis runs over, the one named last changes fastest.
Arguments:
- generated_input: bfloat16 [4, 4096, 8192], P('dp', 'ctx'), may hold values from -6 to 6
- frozen_query: bfloat16 [4, 4096, 4096], P('dp', 'ctx'), may hold values from -12 to 12
- frozen_key_value: bfloat16 [4, 4096, 1024], P('dp', 'ctx'), may hold values from -6 to 6
- adapter_down_weight: bfloat16 [8192, 128], replicated, may hold values from -0.0625 to 0.0625
- query_up_weight: bfloat16 [64, 4096], replicated, may hold values from -0.75 to 0.75
- value_up_weight: bfloat16 [64, 512], replicated, may hold values from -0.75 to 0.75
- response_numbers: int32 [4, 4096], P('dp', 'ctx'), may hold values from 0 to 3, never falling along the last dimension, each value on 1 to 3072 neighbouring positions
- target_replica: int32 [32, 4, 4], P('ctx'), may hold values from 0 to 3, as said below
- output_gradient: bfloat16 [4, 4096, 4096], P('dp', 'ctx'), may hold values from -6 to 6
Outputs:
- attn_out: bfloat16 [4, 4096, 4096], P('dp', 'ctx')
- grad_a: float32 [8192, 128], replicated
- query_up_gradient: float32 [64, 4096], replicated
- value_up_gradient: float32 [64, 512], replicated
Inputs may be any that keep to these rules, and one draw needn't show every extreme that they name: `target_replica`: for each block c and generator replica g, the 4 quarters go to 4 different trainer replicas; for each block c and quarter k, the 4 generator replicas send to 4 different trainer replicas. `response_numbers`: never falls along a pack; every response number appears; a response has at most 3072 positions (rounded down), and one has exactly that many.
All inputs are finite; a program needn't handle non-finite values.
Results may differ from a plain program's by a relative error of at most 0.017.
Values may be sent and summed in bfloat16 or wider, within the bound.
No kernel may reach another device: no remote copies, remote signals or barrier semaphores. Data moves between devices by JAX's collectives and lax.ppermute only.
A program may use at most 128 MiB of HBM per device.

v0:
```python
import math

import jax
import jax.numpy as jnp
from jax import lax
from jax.sharding import PartitionSpec as P

HEAD_SIZE = 128


ADAPTER_SCALE = 0.5
MASKED = -1e30


def blockwise(step_fn, carry, pieces):
    piece_len = pieces[0].shape[0]
    block_length = math.gcd(piece_len, 512)

    def turn(step_index, running):
        first_row = step_index * block_length
        sub_pieces = tuple(
            (lax.dynamic_slice_in_dim(member, first_row, block_length, 0) for member in pieces)
        )
        return step_fn(running, sub_pieces, first_row)

    return lax.fori_loop(0, piece_len // block_length, turn, carry)


def inverse_of(order, places):
    return jnp.sum(places[None, :] * (order[None, :] == places[:, None]).astype(jnp.int32), axis=1)


def on_device(
    generated_input,
    frozen_query,
    frozen_key_value,
    adapter_down_weight,
    query_up_weight,
    value_up_weight,
    response_numbers,
    target_replica,
    output_gradient,
):
    replicas = lax.axis_size("dp")
    my_replica = lax.axis_index("dp")
    my_shard = lax.axis_index("ctx")
    tok_rows = generated_input.shape[1]
    quarter_len = tok_rows // replicas
    adapter_rank_size = query_up_weight.shape[0]
    q_width = query_up_weight.shape[1]
    key_value_width = value_up_weight.shape[1]
    heads_kv = key_value_width // HEAD_SIZE
    groups = q_width // key_value_width
    inverse = 1.0 / math.sqrt(HEAD_SIZE)
    highest_precision = lax.Precision.HIGHEST
    route = target_replica[0]
    places = jnp.arange(replicas, dtype=jnp.int32)
    outgoing = lax.dynamic_index_in_dim(route, my_replica, 0, keepdims=False)
    send_order = inverse_of(outgoing, places)
    incoming = jnp.sum(places[:, None] * (route == my_replica).astype(jnp.int32), axis=0)
    back_order = inverse_of(incoming, places)
    input_rows = generated_input[0]
    reduced_rows = jnp.dot(
        input_rows, adapter_down_weight, preferred_element_type=jnp.float32
    ).astype(jnp.bfloat16)

    def quarters(rows, order):
        return jnp.take(rows.reshape(replicas, quarter_len, rows.shape[-1]), order, axis=0)

    def joined(slots, order):
        return jnp.take(slots, order, axis=0).reshape(tok_rows, slots.shape[-1])

    q_got, kv_got, low_got = (
        lax.all_to_all(
            quarters(frozen_query[0], send_order), "dp", split_axis=0, concat_axis=0, tiled=True
        ),
        lax.all_to_all(
            quarters(frozen_key_value[0], send_order), "dp", split_axis=0, concat_axis=0, tiled=True
        ),
        lax.all_to_all(
            quarters(reduced_rows, send_order), "dp", split_axis=0, concat_axis=0, tiled=True
        ),
    )
    query_input = joined(q_got, incoming)
    key_value_input = joined(kv_got, incoming)
    reduced_input = joined(low_got, incoming)
    reduced_query = reduced_input[:, :adapter_rank_size]
    reduced_value = reduced_input[:, adapter_rank_size:]
    query_rows = (
        query_input.astype(jnp.float32)
        + ADAPTER_SCALE
        * jnp.dot(reduced_query, query_up_weight, preferred_element_type=jnp.float32)
    ).astype(jnp.bfloat16)
    value_rows = (
        key_value_input[:, key_value_width:].astype(jnp.float32)
        + ADAPTER_SCALE
        * jnp.dot(reduced_value, value_up_weight, preferred_element_type=jnp.float32)
    ).astype(jnp.bfloat16)
    key_value = jnp.concatenate([key_value_input[:, :key_value_width], value_rows], axis=1)
    seg_own = response_numbers[0].astype(jnp.bfloat16)
    q_position = my_shard * tok_rows + jnp.arange(tok_rows, dtype=jnp.int32)
    last_row = my_shard * tok_rows + tok_rows - 1
    query_head_rows = query_rows.reshape(tok_rows, heads_kv, groups, HEAD_SIZE)
    head_gradients = output_gradient[0].reshape(tok_rows, heads_kv, groups, HEAD_SIZE)

    def split_piece(kv_piece, seg_piece, offset):
        piece_len = kv_piece.shape[0]
        key_heads = kv_piece[:, :key_value_width].reshape(piece_len, heads_kv, HEAD_SIZE)
        val_heads = kv_piece[:, key_value_width:].reshape(piece_len, heads_kv, HEAD_SIZE)
        k_position = offset + jnp.arange(piece_len, dtype=jnp.int32)
        visible = (seg_own[:, None] == seg_piece[None, :]) & (
            k_position[None, :] <= q_position[:, None]
        )
        raw_scores = (
            jnp.einsum(
                "rkgd,tkd->kgrt", query_head_rows, key_heads, preferred_element_type=jnp.float32
            )
            * inverse
        )
        return (key_heads, val_heads, visible, raw_scores)

    def forward_step(carry, pieces, offset):
        kv_piece, seg_piece = pieces

        def forward_compute(running):
            run_max, run_sum, accumulated = running
            key_heads, val_heads, visible, raw_scores = split_piece(kv_piece, seg_piece, offset)
            masked = jnp.where(visible, raw_scores, MASKED)
            new_max = jnp.maximum(run_max, jnp.max(masked, axis=-1))
            weight = jnp.where(visible, jnp.exp(raw_scores - new_max[..., None]), 0.0)
            factor = jnp.exp(run_max - new_max)
            run_sum = run_sum * factor + jnp.sum(weight, axis=-1)
            update = jnp.einsum(
                "kgrt,tkd->rkgd",
                weight.astype(jnp.bfloat16),
                val_heads,
                preferred_element_type=jnp.float32,
            )
            accumulated = accumulated * jnp.transpose(factor, (2, 0, 1))[..., None] + update
            return (new_max, run_sum, accumulated)

        return lax.cond(offset <= last_row, forward_compute, lambda running: running, carry)

    forward_init = (
        jnp.full((heads_kv, groups, tok_rows), MASKED, jnp.float32),
        jnp.zeros((heads_kv, groups, tok_rows), jnp.float32),
        jnp.zeros((tok_rows, heads_kv, groups, HEAD_SIZE), jnp.float32),
    )
    run_max, run_sum, accumulated = blockwise(
        forward_step,
        forward_init,
        (
            lax.all_gather(key_value, "ctx", axis=0, tiled=True),
            lax.all_gather(seg_own, "ctx", axis=0, tiled=True),
        ),
    )
    attn_low = (accumulated / jnp.transpose(run_sum, (2, 0, 1))[..., None]).astype(jnp.bfloat16)
    log_total = run_max + jnp.log(run_sum)
    row_delta = jnp.transpose(
        jnp.sum(head_gradients.astype(jnp.float32) * attn_low.astype(jnp.float32), axis=-1),
        (1, 2, 0),
    )
    all_keys = tok_rows * lax.axis_size("ctx")

    def backward_step(carry, pieces, offset):
        kv_piece, seg_piece = pieces

        def backward_compute(running):
            dq_acc, dv_full = running
            key_heads, val_heads, visible, raw_scores = split_piece(kv_piece, seg_piece, offset)
            piece_len = kv_piece.shape[0]
            prob_rows = jnp.where(visible, jnp.exp(raw_scores - log_total[..., None]), 0.0)
            prob_grad = jnp.einsum(
                "rkgd,tkd->kgrt", head_gradients, val_heads, preferred_element_type=jnp.float32
            )
            score_grad = (prob_rows * (prob_grad - row_delta[..., None])).astype(jnp.bfloat16)
            dq_acc = (
                dq_acc
                + jnp.einsum(
                    "kgrt,tkd->rkgd", score_grad, key_heads, preferred_element_type=jnp.float32
                )
                * inverse
            )
            grad_piece = jnp.einsum(
                "kgrt,rkgd->tkd",
                prob_rows.astype(jnp.bfloat16),
                head_gradients,
                preferred_element_type=jnp.float32,
            ).reshape(piece_len, key_value_width)
            current = lax.dynamic_slice_in_dim(dv_full, offset, piece_len, 0)
            dv_full = lax.dynamic_update_slice_in_dim(dv_full, current + grad_piece, offset, 0)
            return (dq_acc, dv_full)

        return lax.cond(offset <= last_row, backward_compute, lambda running: running, carry)

    backward_init = (
        jnp.zeros((tok_rows, heads_kv, groups, HEAD_SIZE), jnp.float32),
        jnp.zeros((all_keys, key_value_width), jnp.float32),
    )
    dq_acc, dv_full = blockwise(
        backward_step,
        backward_init,
        (
            lax.all_gather(key_value, "ctx", axis=0, tiled=True),
            lax.all_gather(seg_own, "ctx", axis=0, tiled=True),
        ),
    )
    query_low_gradient = dq_acc.reshape(tok_rows, q_width).astype(jnp.bfloat16)
    b_v_wide = jnp.transpose(value_up_weight).astype(jnp.float32)
    dv_own = lax.psum_scatter(dv_full, "ctx", scatter_dimension=0, tiled=True)
    value_up_gradient = ADAPTER_SCALE * jnp.dot(
        jnp.transpose(reduced_value).astype(jnp.float32),
        dv_own,
        precision=highest_precision,
        preferred_element_type=jnp.float32,
    )
    reduced_value_gradient = ADAPTER_SCALE * jnp.dot(
        dv_own, b_v_wide, precision=highest_precision, preferred_element_type=jnp.float32
    )
    query_up_gradient = ADAPTER_SCALE * jnp.dot(
        jnp.transpose(reduced_query), query_low_gradient, preferred_element_type=jnp.float32
    )
    reduced_gradient = jnp.concatenate(
        [
            ADAPTER_SCALE
            * jnp.dot(
                query_low_gradient,
                jnp.transpose(query_up_weight),
                preferred_element_type=jnp.float32,
            ),
            reduced_value_gradient,
        ],
        axis=1,
    ).astype(jnp.bfloat16)
    returned = lax.all_to_all(
        quarters(reduced_gradient, back_order), "dp", split_axis=0, concat_axis=0, tiled=True
    )
    low_back = joined(returned, outgoing)
    grad_a = jnp.dot(jnp.transpose(input_rows), low_back, preferred_element_type=jnp.float32)
    grad_a, query_up_gradient, value_up_gradient = lax.psum(
        (grad_a, query_up_gradient, value_up_gradient), ("dp", "ctx")
    )
    attn_out = attn_low.reshape(tok_rows, q_width)[None]
    return (attn_out, grad_a, query_up_gradient, value_up_gradient)


def solution(mesh):
    return jax.shard_map(
        on_device,
        mesh=mesh,
        in_specs=(
            P("dp", "ctx", None),
            P("dp", "ctx", None),
            P("dp", "ctx", None),
            P(),
            P(),
            P(),
            P("dp", "ctx"),
            P("ctx", None, None),
            P("dp", "ctx", None),
        ),
        out_specs=(P("dp", "ctx", None), P(), P(), P()),
        check_vma=False,
    )
```

profile of v0, /device:TPU:1, one launch (start us, length us, event | category | flops | bytes accessed | tf_op | source)
XLA Modules:
  0.0 660.7 jit_solution(17623773270615458516)
XLA Ops:
  9.3 2.3 fusion.47
  12.9 5.9 all-to-all-start.1
  20.1 2.9 all-to-all-done.1
  23.0 3.4 all-to-all-start
  27.1 4.8 all-to-all-done
  33.6 1.8 gather_fusion.4
  36.6 4.3 all-to-all-start.2
  40.9 2.3 copy.33
  43.2 24.9 %all-gather = bf16[1,4096]{1,0:T(2,128)(2,1)S(1)} all-gather(bf16[1,128]{1,0:T(2,128)(2,1)S(1)} %get-tuple-element.808), channel_id=2, replica_groups=mesh['dp'=4,'ctx'=32] {'ctx'}, dimensions={1}, use_global_device_ids=true | all-gather | bytes 8448 | tf_op jit(solution)/shard_map/all_gather | solution.py:154
  68.1 1.8 gather_fusion.5
  72.3 16.7 %all-gather.3.cloned.1.call-done = bf16[4096,1024]{1,0:T(8,128)(2,1)} async-done(((bf16[128,1024]{1,0:T(8,128)(2,1)}), bf16[4096,1024]{1,0:T(8,128)(2,1)}) %all-gather.3.cloned.1.call-update) | async-done | bytes 8388624 | tf_op jit(solution)/shard_map/all_gather | solution.py:153
  89.0 11.5 %copy.29 = bf16[4096,1024]{0,1:T(8,128)(2,1)} copy(bf16[4096,1024]{1,0:T(8,128)(2,1)} %all-gather.3.cloned.1.call-done) | data formatting | bytes 16777216
  102.2 9.6 %while.34 = (s32[]{:T(128)}, f32[4,8,128]{2,1,0:T(8,128)S(1)}, f32[4,8,128]{2,1,0:T(8,128)S(1)}, f32[128,4,8,128]{3,0,2,1:T(8,128)}, s32[]{:T(128)}, /*index=5*/...) while((s32[]{:T(128)}, f32[4,8,128]{2,1,0:T(8,128)S(1)}, ...), condition=%wide.region_7.11_spmd.clone, body=%wide.region_2.10_spmd.clone.sunk | while | flops 1098199680 | bytes 50865816 | solution.py:26
  102.2 9.3 %conditional.6 = ((f32[4,8,128]{2,1,0:T(8,128)S(1)}, f32[4,8,128]{2,1,0:T(8,128)S(1)}, f32[128,4,8,128]{3,0,2,1:T(8,128)})) conditional(s32[]{:T(128)} %convert_element_type.118, (f32[4,8,128]{2,1,0:T(8,128)S(1)}, f32[4,8,128]{2,1,0:T(8,128)S(1)}, f32[128,4,8,128]{3,0,2,1:T(8,128)}) %tuple.116, (bf16[128]{0:T(256)(128)(2,1)S(1)}, s32[]{:T(128)}, ...), branch_computations={%region_3.0_spmd, %region_4.9_spmd} | conditional | flops 1098199680 | bytes 50865052 | solution.py:142
  107.1 3.1 bitcast_add_fusion
  111.7 3.0 copy.31
  114.7 3.4 multiply_reduce_fusion
  119.7 4.2 broadcast_in_dim.91
  123.9 24.7 %while.35 = (s32[]{:T(128)}, f32[128,4,8,128]{3,0,2,1:T(8,128)}, f32[4096,512]{0,1:T(8,128)}, s32[]{:T(128)}, bf16[128]{0:T(256)(128)(2,1)S(1)}, /*index=5*/bf16...) while((s32[]{:T(128)}, f32[128,4,8,128]{3,0,2,1:T(8,128)}, ...), condition=%wide.region_12.16_spmd.clone, body=%wide.region_9.15_spmd.clone.sunk | while | flops 2170094080 | bytes 42722960 | solution.py:26
  123.9 24.4 %conditional.7 = ((f32[128,4,8,128]{3,0,2,1:T(8,128)}, f32[4096,512]{0,1:T(8,128)})) conditional(s32[]{:T(128)} %convert_element_type.119, (f32[128,4,8,128]{3,0,2,1:T(8,128)}, f32[4096,512]{0,1:T(8,128)}) %tuple.119, (bf16[128]{0:T(256)(128)(2,1)S(1)}, s32[]{:T(128)}, bf16[4096]{0:T(1024)(128)(2,1)S(1)}, s32[]{:T(128)}, ...), branch_computations={%region_10.13_spmd, %region_11.14_spmd} | conditional | flops 2170094080 | bytes 42722172 | solution.py:194
  123.9 2.1 fusion.57
  126.1 4.6 fusion.59
  130.9 9.6 %bitcast_add_fusion.1 = f32[128,4,8,128]{3,0,2,1:T(8,128)} fusion(f32[128,4,8,128]{3,0,2,1:T(8,128)} %get-tuple-element.596, bf16[512,4,128,1]{0,2,3,1:T(8,128)(2,1)} %bitcast.128, f32[4,512,128,8]{2,1,3,0:T(8,128)} %fusion.59, f32[4,8,128]{2,1,0:T(8,128)S(1)} %get-tuple-element.605, f32[4,8,128]{2,1,0:T(8,128)S(1)} %get-tuple-element.603, ...), kind=kOutput, calls=%fused_computation.44 | convolution fusion | flops 1087373312 | bytes 14778368 | tf_op jit(solution)/shard_map/while/body/eval_jaxpr/cond/branch_1_fun/kgrt,tkd->rkgd/dot_general | solution.py:179
  140.6 5.3 fusion.25
  145.9 2.4 constant_dynamic-update-slice_fusion
  154.3 319.4 %reduce-scatter.2.cloned.1.call-done = f32[128,512]{0,1:T(8,128)} async-done(((f32[4096,512]{0,1:T(8,128)}), f32[128,512]{0,1:T(8,128)}) %reduce-scatter.2.cloned.1.call-update) | async-done | bytes 262160 | tf_op jit(solution)/shard_map/reduce_scatter | solution.py:210
  476.3 4.1 all-to-all-start.3
  480.5 2.0 convolution_multiply_fusion.3
  482.4 2.3 all-to-all-done.3
  485.4 2.7 convolution_bitcast_fusion
  490.7 156.2 %all-reduce.3.cloned.1.call-done = (f32[8192,128]{0,1:T(8,128)}, f32[64,4096]{1,0:T(8,128)}, f32[64,512]{1,0:T(8,128)}) async-done(((f32[8192,128]{0,1:T(8,128)}, f32[64,4096]{1,0:T(8,128)}, f32[64,512]{1,0:T(8,128)}), (f32[8192,128]{0,1:T(8,128)}, f32[64,4096]{1,0:T(8,128)}, f32[64,512]{1,0:T(8,128)})) %all-reduce.3.cloned.1.call-update) | async-done | bytes 5373968 | tf_op jit(solution)/shard_map/psum | solution.py:240
  646.9 5.7 copy.39
  (137 shorter events, 33.4 us)
Async XLA Ops:
  7.2 2.1 copy-start
  7.2 11.5 %copy-start.10 = (s32[1,4,4]{2,1,0:T(4,128)S(1)}, s32[1,4,4]{2,1,0:T(4,128)}, u32[]{:S(2)}) copy-start(s32[1,4,4]{2,1,0:T(4,128)} %param.30) | copy-start | bytes 196
  7.2 11.6 %copy-start.6 = (bf16[1,128,1024]{2,1,0:T(8,128)(2,1)S(1)}, bf16[1,128,1024]{2,1,0:T(8,128)(2,1)}, u32[]{:S(2)}) copy-start(bf16[1,128,1024]{2,1,0:T(8,128)(2,1)} %param.25) | copy-start | bytes 786436
  7.2 25.4 %copy-start.7 = (bf16[64,512]{1,0:T(8,128)(2,1)S(1)}, bf16[64,512]{1,0:T(8,128)(2,1)}, u32[]{:S(2)}) copy-start(bf16[64,512]{1,0:T(8,128)(2,1)} %param.28) | copy-start | bytes 196612
  8.6 0.6 copy-start.12
  12.9 10.2 %all-to-all-start.1 = ((bf16[4,32,128]{2,1,0:T(8,128)(2,1)}), bf16[4,32,128]{2,1,0:T(8,128)(2,1)S(1)}, u32[]{:S(2)}, u32[]{:S(2)}) async-start(bf16[4,32,128]{2,1,0:T(8,128)(2,1)} %broadcast_select_fusion.7), calls=%async_computation.1 | async-start | bytes 65536 | tf_op jit(solution)/shard_map/all_to_all | solution.py:80
  18.7 14.9 %copy-start.14 = (s32[4]{0:T(128)}, s32[4]{0:T(128)S(1)}, u32[]{:S(2)}) copy-start(s32[4]{0:T(128)S(1)} %select_reduce_fusion.1) | copy-start | bytes 52
  23.0 8.9 %all-to-all-start = ((bf16[4,32,1024]{2,1,0:T(8,128)(2,1)}), bf16[4,32,1024]{2,1,0:T(8,128)(2,1)S(1)}, u32[]{:S(2)}, u32[]{:S(2)}) async-start(bf16[4,32,1024]{2,1,0:T(8,128)(2,1)} %broadcast_select_fusion.3), calls=%async_computation | async-start | bytes 524288 | tf_op jit(solution)/shard_map/all_to_all | solution.py:77
  26.4 62.6 %all-gather.3.cloned.1.call-start = ((), (), s32[]{:S(2)}) async-start(), calls=%async_computation.5 | async-start | bytes 8650752 | tf_op jit(solution)/shard_map/all_gather | solution.py:153
  33.6 9.6 %copy-start.16 = (s32[1,128]{1,0:T(1,128)S(1)}, s32[1,128]{1,0:T(1,128)}, u32[]{:S(2)}) copy-start(s32[1,128]{1,0:T(1,128)} %param.29) | copy-start | bytes 1540
  36.6 31.5 %all-to-all-start.2 = ((bf16[4,32,4096]{2,1,0:T(8,128)(2,1)}), bf16[4,32,4096]{2,1,0:T(8,128)(2,1)}, u32[]{:S(2)}, u32[]{:S(2)}) async-start(bf16[4,32,4096]{2,1,0:T(8,128)(2,1)} %broadcast_select_fusion.1), calls=%async_computation.2 | async-start | bytes 2097152 | tf_op jit(solution)/shard_map/all_to_all | solution.py:74
  40.9 432.8 %reduce-scatter.2.cloned.1.call-start = ((), (), s32[]{:S(2)}) async-start(), calls=%async_computation.6 | async-start | bytes 8650752 | tf_op jit(solution)/shard_map/reduce_scatter | solution.py:210
  105.2 1.8 copy-start.2
  110.1 1.3 copy-start.3
  126.1 4.6 copy-start.1
  148.6 0.7 copy-start.15
  148.6 0.8 copy-start.13
  149.3 324.4 %copy-start.8 = (bf16[64,512]{1,0:T(8,128)(2,1)S(1)}, bf16[64,512]{1,0:T(8,128)(2,1)}, u32[]{:S(2)}) copy-start(bf16[64,512]{1,0:T(8,128)(2,1)} %param.28) | copy-start | bytes 196612
  149.3 336.0 %copy-start.11 = (pred[4]{0:T(512)(128)(4,1)S(1)}, pred[4]{0:T(512)(128)(4,1)}, u32[]{:S(2)}) copy-start(pred[4]{0:T(512)(128)(4,1)} %get-tuple-element.798) | copy-start | bytes 16
  476.3 8.4 %all-to-all-start.3 = ((bf16[4,32,128]{2,1,0:T(8,128)(2,1)}), bf16[4,32,128]{2,1,0:T(8,128)(2,1)S(1)}, u32[]{:S(2)}, u32[]{:S(2)}) async-start(bf16[4,32,128]{2,1,0:T(8,128)(2,1)} %broadcast_select_fusion.5), calls=%async_computation.4 | async-start | bytes 65536 | tf_op jit(solution)/shard_map/all_to_all | solution.py:235
  480.5 166.5 %all-reduce.3.cloned.1.call-start = ((), (), s32[]{:S(2)}) async-start(), calls=%async_computation.7 | async-start | bytes 10747904 | tf_op jit(solution)/shard_map/psum | solution.py:240
  488.2 1.2 copy-start.4
  646.9 5.7 copy-start.5
  646.9 6.6 %copy-start.9 = (f32[64,512]{1,0:T(8,128)S(1)}, f32[64,512]{1,0:T(8,128)}, u32[]{:S(2)}) copy-start(f32[64,512]{1,0:T(8,128)} %get-tuple-element.1045) | copy-start | bytes 393220
Sparse Core Ops, SparseCore 0:
  33.7 55.2 all-gather.2
  148.8 324.8 reduce-scatter.1
  488.3 158.5 all-reduce.2
where the time goes:
time: 663 us; the launch traced here: 661 us
  waiting for transfers between devices  502 us (76%)
  local copies, waits for them, and re-layouts  49.9 us (8%)
  matrix products  36.8 us (6%)
  blocking collectives  24.9 us (4%)
  starting transfers between devices  17.7 us (3%)
  other arithmetic  14.3 us (2%)
  between operations  14.1 us (2%)
    reduce_scatter x1, waiting for transfers between devices, on_device(): dv_own = lax.psum_scatter(dv_full, 'ctx', scatter_dimension=0, tiled=True)  319 us
    psum x1, waiting for transfers between devices, on_device(): lax.psum((grad_a, query_up_gradient, value_up_gradient), ('dp', 'ctx'))  156 us
    all_gather x1, blocking collectives, on_device(): lax.all_gather(seg_own, 'ctx', axis=0, tiled=True)  24.9 us
    unnamed x35, local copies, waits for them, and re-layouts  24.2 us
    all_gather x1, waiting for transfers between devices, on_device(): lax.all_gather(key_value, 'ctx', axis=0, tiled=True)  16.7 us
  transfers between devices with their start and end apart: 7, of which 6 were waited for; matrix products, arithmetic and copies ran while one was open for 3% of the time, Pallas kernels for 0%

commit v1 on v0

v1 whole, which is shorter than its diff:
```python
import functools
import math

import jax
import jax.numpy as jnp
from jax import lax
from jax.experimental import pallas as pl
from jax.experimental.pallas import tpu as pltpu
from jax.sharding import Mesh
from jax.sharding import PartitionSpec as P

HEAD = 128
BLOCK = 128
QUARTER = 32
KEY_CHUNK = 512
PAD = KEY_CHUNK - BLOCK
HEADS_STEP = 4
SCALE = 0.5
MASKED = -1e30
INVERSE = 1.0 / math.sqrt(HEAD)
LOG2E = 1.4426950408889634
BF = jnp.bfloat16
F32 = jnp.float32
NT = (((1,), (1,)), ((), ()))
TN = (((0,), (0,)), ((), ()))
VMEM = pltpu.VMEM
CHIP = ("dp", "y", "x")
LANE = ("x", "core")


def whole():
    return pl.BlockSpec(memory_space=pltpu.VMEM)


def scalars():
    return pl.BlockSpec(memory_space=pltpu.SMEM)


def params(mib):
    return pltpu.CompilerParams(vmem_limit_bytes=mib << 20)


def front_kernel(order_ref, x_ref, a_ref, kv_ref, out_ref, low_ref):
    low_ref[...] = jnp.dot(x_ref[...], a_ref[...], preferred_element_type=F32).astype(BF)
    for r in range(4):
        rows = pl.ds(pl.multiple_of(order_ref[r] * QUARTER, QUARTER), QUARTER)
        low = low_ref[rows, :]
        for y in range(4):
            out_ref[r * 4 + y, :, 0:128] = kv_ref[rows, y * 128 : y * 128 + 128]
            out_ref[r * 4 + y, :, 128:256] = kv_ref[rows, 512 + y * 128 : 640 + y * 128]
            out_ref[r * 4 + y, :, 256:384] = low


def front(order, x, a, kv):
    return pl.pallas_call(
        front_kernel,
        out_shape=jax.ShapeDtypeStruct((16, QUARTER, 384), BF),
        in_specs=[scalars(), whole(), whole(), whole()],
        out_specs=whole(),
        scratch_shapes=[VMEM((BLOCK, 128), BF)],
        compiler_params=params(32),
        cost_estimate=pl.CostEstimate(flops=2 * 128 * 8192 * 128, bytes_accessed=5 << 20, transcendentals=0),
    )(order, x, a, kv)


def query_chunks_kernel(order_ref, q_ref, out_ref):
    for y in range(4):
        out_ref[0, y] = q_ref[:, y * 1024 : (y + 1) * 1024]


def query_chunks(order, q):
    return pl.pallas_call(
        query_chunks_kernel,
        out_shape=jax.ShapeDtypeStruct((4, 4, QUARTER, 1024), BF),
        grid_spec=pltpu.PrefetchScalarGridSpec(
            num_scalar_prefetch=1,
            grid=(4,),
            in_specs=[pl.BlockSpec((QUARTER, 4096), lambda r, order: (order[r], 0))],
            out_specs=pl.BlockSpec((1, 4, QUARTER, 1024), lambda r, order: (r, 0, 0, 0)),
        ),
        cost_estimate=pl.CostEstimate(flops=0, bytes_accessed=2 << 20, transcendentals=0),
    )(order, q)


def pack_kernel(order_ref, c0, c1, c2, c3, resp_ref, wv_ref, out_ref):
    rows = jnp.concatenate([c0[0], c1[0], c2[0], c3[0]], axis=0)
    low_v = rows[:, 320:384]
    value = rows[:, 128:256].astype(F32) + SCALE * jnp.dot(low_v, wv_ref[...], preferred_element_type=F32)
    lane = lax.broadcasted_iota(jnp.int32, (BLOCK, 64), 1)
    resp = resp_ref[0].astype(F32)
    extra = jnp.where(lane == 0, 1.0, jnp.where(lane == 1, resp, 0.0))
    out_ref[0, :, 0:128] = rows[:, 0:128]
    out_ref[0, :, 128:256] = value.astype(BF)
    out_ref[0, :, 256:384] = jnp.concatenate([low_v.astype(F32), extra], axis=1).astype(BF)


def pack(order, got, resp, wv):
    def chunk(k):
        return pl.BlockSpec((1, QUARTER, 384), lambda i, order: (order[i * 4 + k], 0, 0))

    return pl.pallas_call(
        pack_kernel,
        out_shape=jax.ShapeDtypeStruct((4, BLOCK, 384), BF),
        grid_spec=pltpu.PrefetchScalarGridSpec(
            num_scalar_prefetch=1,
            grid=(4,),
            in_specs=[chunk(k) for k in range(4)]
            + [
                pl.BlockSpec((1, BLOCK, 1), lambda i, order: (i, 0, 0)),
                pl.BlockSpec((64, 128), lambda i, order: (0, 0)),
            ],
            out_specs=pl.BlockSpec((1, BLOCK, 384), lambda i, order: (i, 0, 0)),
        ),
        cost_estimate=pl.CostEstimate(flops=1 << 23, bytes_accessed=1 << 20, transcendentals=0),
    )(order, got, got, got, got, resp, wv)


def attention_kernel(
    order_ref, steps_ref, lane_ref,
    q0, q1, q2, q3, l0, l1, l2, l3, do_ref, start_ref, kv_ref, wv_ref, wq_ref,
    out_ref, lg_ref, send_ref,
    kv_s, s_s, w_s, t_s, m_s, acc_s, dq_s, qup_s, vup_s, sem,
):
    i, hg = pl.program_id(0), pl.program_id(1)
    rows_all = HEADS_STEP * BLOCK

    @pl.when((i == 0) & (hg == 0))
    def _():
        copies = []
        for c in range(32):
            copies.append(
                pltpu.make_async_copy(
                    kv_ref.at[c % 8, c // 8], kv_s.at[pl.ds(PAD + c * BLOCK, BLOCK), :], sem.at[c]
                )
            )
        for copy in copies:
            copy.start()
        kv_s[0:PAD, :] = jnp.zeros((PAD, 384), BF)
        t_s[...] = jnp.zeros_like(t_s)
        qup_s[...] = jnp.zeros_like(qup_s)
        vup_s[...] = jnp.zeros_like(vup_s)
        for copy in copies:
            copy.wait()

    @pl.when(hg == 0)
    def _():
        lg_ref[...] = jnp.zeros_like(lg_ref)

    block = i * 8 + lane_ref[0]
    high = (block + 1) * BLOCK
    steps = steps_ref[i]

    low = jnp.concatenate([l0[0], l1[0], l2[0], l3[0]], axis=0)
    wq = wq_ref[...]
    q_in = jnp.concatenate([q0[0], q1[0], q2[0], q3[0]], axis=0).astype(F32)
    query = (q_in + SCALE * jnp.dot(low[:, 0:64], wq, preferred_element_type=F32)).astype(BF)
    query = jnp.concatenate([query[:, h * HEAD : (h + 1) * HEAD] for h in range(HEADS_STEP)], axis=0)
    dout = do_ref[0]
    dout = jnp.concatenate([dout[:, h * HEAD : (h + 1) * HEAD] for h in range(HEADS_STEP)], axis=0)
    start = jnp.concatenate([start_ref[0]] * HEADS_STEP, axis=0)
    row = block * BLOCK + lax.broadcasted_iota(jnp.int32, (BLOCK, 1), 0)
    row = jnp.concatenate([row] * HEADS_STEP, axis=0)

    def place(t):
        return pl.multiple_of(PAD + high - KEY_CHUNK * (t + 1), BLOCK)

    m_s[...] = jnp.full_like(m_s, MASKED)

    def scores(t, _):
        at = place(t)
        s = lax.dot_general(query, kv_s[pl.ds(at, KEY_CHUNK), 0:128], NT, preferred_element_type=F32)
        key = at - PAD + lax.broadcasted_iota(jnp.int32, (1, KEY_CHUNK), 1)
        s = jnp.where((key >= start) & (key <= row), s, MASKED)
        s_s[t] = s
        top = m_s[...]
        for c in range(KEY_CHUNK // 128):
            top = jnp.maximum(top, s[:, c * 128 : (c + 1) * 128])
        m_s[...] = top
        return 0

    lax.fori_loop(0, steps, scores, 0)
    top = jnp.max(m_s[...], axis=1, keepdims=True)
    acc_s[...] = jnp.zeros_like(acc_s)

    def forward(t, _):
        w = jnp.exp2((s_s[t] - top) * (INVERSE * LOG2E)).astype(BF)
        w_s[t] = w
        acc_s[...] += jnp.dot(w, kv_s[pl.ds(place(t), KEY_CHUNK), 128:384], preferred_element_type=F32)
        return 0

    lax.fori_loop(0, steps, forward, 0)
    over = 1.0 / acc_s[:, 192:193]
    out = (acc_s[:, 0:128] * over).astype(BF)
    for h in range(HEADS_STEP):
        out_ref[0, :, h * HEAD : (h + 1) * HEAD] = out[h * BLOCK : (h + 1) * BLOCK, :]
    wide = dout.astype(F32)
    delta = jnp.sum(wide * out.astype(F32), axis=1, keepdims=True) * over
    scaled = (wide * over).astype(BF)
    g = lax.dot_general(wv_ref[...], scaled, NT, preferred_element_type=F32).astype(BF)
    weighted_low = (acc_s[:, 128:256] * over).astype(BF)
    vup_s[...] += lax.dot_general(weighted_low, dout, TN, preferred_element_type=F32)
    dq_s[...] = jnp.zeros_like(dq_s)

    def backward(t, _):
        at = place(t)
        w = w_s[t]
        dp = lax.dot_general(scaled, kv_s[pl.ds(at, KEY_CHUNK), 128:256], NT, preferred_element_type=F32)
        ds = (w.astype(F32) * (dp - delta)).astype(BF)
        dq_s[...] += jnp.dot(ds, kv_s[pl.ds(at, KEY_CHUNK), 0:128], preferred_element_type=F32)
        t_s[:, pl.ds(at, KEY_CHUNK)] += jnp.dot(g, w, preferred_element_type=F32)
        return 0

    lax.fori_loop(0, steps, backward, 0)
    dq = (dq_s[...] * INVERSE).astype(BF)
    low_t = jnp.transpose(low.astype(F32))[0:64, :].astype(BF)
    lg = lg_ref[...]
    for h in range(HEADS_STEP):
        dq_h = dq[h * BLOCK : (h + 1) * BLOCK, :]
        lg = lg + lax.dot_general(
            wq[:, h * HEAD : (h + 1) * HEAD], dq_h, NT, preferred_element_type=F32
        )
        qup_s[hg * HEADS_STEP + h] += jnp.dot(low_t, dq_h, preferred_element_type=F32)
    lg_ref[...] = lg

    @pl.when((i == 3) & (hg == 8 // HEADS_STEP - 1))
    def _():
        for c in range(32):
            part = t_s[:, PAD + c * BLOCK : PAD + (c + 1) * BLOCK] * SCALE
            send_ref[c % 8, :, (c // 8) * BLOCK : (c // 8 + 1) * BLOCK] = part.astype(BF)
        vup = (vup_s[0:64, :] * SCALE).astype(BF)
        for c in range(8):
            send_ref[c, :, 512:640] = (qup_s[c] * SCALE).astype(BF)
            send_ref[c, :, 640:768] = vup


def attention(order, steps, lane, q, got, dout, start, kv, wv, wq):
    width = HEADS_STEP * HEAD
    rows = HEADS_STEP * BLOCK
    chunks = 4096 // KEY_CHUNK

    def q_part(k):
        return pl.BlockSpec((1, QUARTER, width), lambda i, h, order, *_: (order[i * 4 + k], 0, h))

    def low_part(k):
        return pl.BlockSpec((1, QUARTER, 128), lambda i, h, order, *_: (order[i * 4 + k], 0, 2))

    return pl.pallas_call(
        attention_kernel,
        out_shape=(
            jax.ShapeDtypeStruct((4, BLOCK, 1024), BF),
            jax.ShapeDtypeStruct((64, 512), F32),
            jax.ShapeDtypeStruct((8, 64, 768), BF),
        ),
        grid_spec=pltpu.PrefetchScalarGridSpec(
            num_scalar_prefetch=3,
            grid=(4, 8 // HEADS_STEP),
            in_specs=[q_part(k) for k in range(4)]
            + [low_part(k) for k in range(4)]
            + [
                pl.BlockSpec((1, BLOCK, width), lambda i, h, *_: (i, 0, h)),
                pl.BlockSpec((1, BLOCK, 1), lambda i, h, *_: (i, 0, 0)),
                pl.BlockSpec(memory_space=pl.ANY),
                pl.BlockSpec((64, 128), lambda i, h, *_: (0, 0)),
                pl.BlockSpec((64, width), lambda i, h, *_: (0, h)),
            ],
            out_specs=(
                pl.BlockSpec((1, BLOCK, width), lambda i, h, *_: (i, 0, h)),
                pl.BlockSpec((64, BLOCK), lambda i, h, *_: (0, i)),
                pl.BlockSpec((8, 64, 768), lambda i, h, *_: (0, 0, 0)),
            ),
            scratch_shapes=[
                VMEM((PAD + 4096, 384), BF),
                VMEM((chunks, rows, KEY_CHUNK), F32),
                VMEM((chunks, rows, KEY_CHUNK), BF),
                VMEM((64, PAD + 4096), F32),
                VMEM((rows, 128), F32),
                VMEM((rows, 256), F32),
                VMEM((rows, 128), F32),
                VMEM((8, 64, 128), F32),
                VMEM((128, 128), F32),
                pltpu.SemaphoreType.DMA((32,)),
            ],
        ),
        compiler_params=params(48),
        cost_estimate=pl.CostEstimate(flops=20 << 30, bytes_accessed=8 << 20, transcendentals=8 << 20),
    )(order, steps, lane, q, q, q, q, got, got, got, got, dout, start, kv, wv, wq)


def middle_kernel(back_ref, mine_ref, got_ref, lg_ref, out_ref, low_ref):
    total = got_ref[0].astype(F32)
    for c in range(1, 8):
        total = total + got_ref[c].astype(F32)
    low_ref[...] = jnp.transpose(jnp.concatenate([lg_ref[...] * SCALE, total[:, 0:512]], axis=0))
    for g in range(4):
        for y in range(4):
            rows = pl.ds(pl.multiple_of(y * BLOCK + back_ref[g * 4 + y] * QUARTER, QUARTER), QUARTER)
            out_ref[g * 4 + y, 0:32, :] = low_ref[rows, :].astype(BF)
            keep = jnp.where(mine_ref[0] == y, 1.0, 0.0)
            out_ref[g * 4 + y, 32:48, :] = (total[g * 16 : g * 16 + 16, 512:640] * keep).astype(BF)
            out_ref[g * 4 + y, 48:64, :] = (total[g * 16 : g * 16 + 16, 640:768] * keep).astype(BF)


def middle(back, mine, got, lg):
    return pl.pallas_call(
        middle_kernel,
        out_shape=jax.ShapeDtypeStruct((16, 64, 128), BF),
        in_specs=[scalars(), scalars(), whole(), whole()],
        out_specs=whole(),
        scratch_shapes=[VMEM((512, 128), F32)],
        cost_estimate=pl.CostEstimate(flops=1 << 20, bytes_accessed=1 << 20, transcendentals=0),
    )(back, mine, got, lg)


def low_back_kernel(outgoing_ref, got_ref, low_ref, up_ref, sum_ref):
    up = jnp.zeros((32, 128), F32)
    for r in range(4):
        total = got_ref[r * 4].astype(F32)
        for y in range(1, 4):
            total = total + got_ref[r * 4 + y].astype(F32)
        sum_ref[r] = total[0:32, :]
        up = up + total[32:64, :]
    for k in range(4):
        low_ref[k * QUARTER : (k + 1) * QUARTER, :] = sum_ref[outgoing_ref[k]].astype(BF)
    up_ref[...] = up


def low_back_of(outgoing, got):
    return pl.pallas_call(
        low_back_kernel,
        out_shape=(jax.ShapeDtypeStruct((BLOCK, 128), BF), jax.ShapeDtypeStruct((32, 128), F32)),
        in_specs=[scalars(), whole()],
        out_specs=(whole(), whole()),
        scratch_shapes=[VMEM((4, QUARTER, 128), F32)],
        cost_estimate=pl.CostEstimate(flops=1 << 18, bytes_accessed=1 << 19, transcendentals=0),
    )(outgoing, got)


def on_device(
    generated_input,
    frozen_query,
    frozen_key_value,
    adapter_down_weight,
    query_up_weight,
    value_up_weight,
    response_numbers,
    target_replica,
    output_gradient,
):
    me = lax.axis_index("dp")
    my_y = lax.axis_index("y")
    my_core = lax.axis_index("core")
    my_lane = lax.axis_index("x") * 2 + my_core
    places = jnp.arange(4, dtype=jnp.int32)
    route = target_replica[0]
    outgoing = lax.dynamic_index_in_dim(route, me, 0, keepdims=False)
    send_order = jnp.sum(places[None, :] * (outgoing[None, :] == places[:, None]), axis=1).astype(jnp.int32)
    swap = [(0, 1), (1, 0)]

    rows = generated_input[0]
    own_half = lax.dynamic_slice_in_dim(rows, my_core * 4096, 4096, 1)
    other_half = lax.ppermute(
        lax.dynamic_slice_in_dim(rows, (1 - my_core) * 4096, 4096, 1), "core", swap
    )

    notes = jnp.concatenate([response_numbers[0], route.reshape(16), jnp.zeros((112,), jnp.int32)])
    notes = lax.all_to_all(jnp.broadcast_to(notes.reshape(1, 2, 128), (4, 2, 128)), "y", 0, 0, tiled=True)
    resp = notes[:, 0, :]
    routes = notes[:, 1, 0:16].reshape(4, 4, 4)
    mine = (routes == me).astype(jnp.int32)
    order = (jnp.sum(mine * places[None, :, None], axis=1) * 4 + places[:, None]).reshape(16)
    back = jnp.transpose(jnp.sum(mine * places[None, None, :], axis=2)).reshape(16)

    got = lax.all_to_all(
        front(send_order, rows, adapter_down_weight, frozen_key_value[0]), ("dp", "y"), 0, 0, tiled=True
    )
    wv = lax.dynamic_slice_in_dim(value_up_weight, my_y * 128, 128, 1)
    wq = lax.dynamic_slice_in_dim(query_up_weight, my_y * 1024, 1024, 1)
    packed = pack(order, got, resp[:, :, None], wv)
    kv = lax.all_gather(packed, LANE, axis=0, tiled=False)
    q = lax.all_to_all(
        query_chunks(send_order, frozen_query[0]).reshape(16, QUARTER, 1024), ("dp", "y"), 0, 0, tiled=True
    )
    dout = lax.all_to_all(
        jnp.transpose(output_gradient[0].reshape(BLOCK, 4, 1024), (1, 0, 2)), "y", 0, 0, tiled=True
    )

    all_resp = kv[:, :, :, 321].astype(jnp.int32)
    below = jnp.sum(all_resp.reshape(1, -1) < places[:, None], axis=1).astype(jnp.int32)
    start = jnp.sum((resp[:, :, None] == places) * below, axis=2).astype(jnp.int32)
    high = ((places * 8 + my_lane) + 1) * BLOCK
    steps = (high - start[:, 0] + KEY_CHUNK - 1) // KEY_CHUNK

    out, lg, send = attention(
        order, steps, my_lane.reshape(1), q, got, dout, start[:, :, None], kv, wv, wq
    )
    sums = lax.all_to_all(send, LANE, 0, 0, tiled=True)
    chunks = lax.all_to_all(middle(back, my_y.reshape(1), sums, lg), ("dp", "y"), 0, 0, tiled=True)
    low_back, up = low_back_of(outgoing, chunks)
    low_other = lax.ppermute(low_back, "core", swap)
    grad = lax.dot_general(
        jnp.concatenate([own_half, other_half], axis=0),
        jnp.concatenate([low_back, low_other], axis=0),
        TN,
        preferred_element_type=F32,
    ).astype(BF)
    parts = lax.all_to_all(grad.reshape(64, 64, 128), CHIP, 0, 0, tiled=True)
    grad_rows = jnp.sum(parts.astype(F32), axis=0)
    vup_rows = lax.dynamic_slice_in_dim(up[16:32], my_lane * 2, 2, 0)
    shard = jnp.concatenate([grad_rows, up[0:16], vup_rows, jnp.zeros((6, 128), F32)], axis=0).astype(BF)
    own = lax.all_to_all(jnp.broadcast_to(shard[None], (64, 88, 128)), CHIP, 0, 0, tiled=True)
    other = lax.ppermute(own, "core", swap)
    first = jnp.where(my_core == 0, own, other)
    second = jnp.where(my_core == 0, other, own)
    both = jnp.stack([first, second], axis=1)
    grad_a = jnp.transpose(both[:, :, 0:64], (1, 0, 2, 3)).reshape(8192, 128).astype(F32)
    both = both.reshape(4, 4, 8, 88, 128)
    query_up_gradient = jnp.transpose(both[:, :, :, 64:80], (0, 3, 1, 2, 4)).reshape(64, 4096).astype(F32)
    value_up_gradient = jnp.transpose(both[:, :, :, 80:82], (0, 2, 3, 1, 4)).reshape(64, 512).astype(F32)

    out = lax.all_to_all(out, "y", 0, 0, tiled=True)
    attn_out = jnp.transpose(out, (1, 0, 2)).reshape(1, BLOCK, 4096)
    return (attn_out, grad_a, query_up_gradient, value_up_gradient)


def solution(mesh):
    grid = Mesh(mesh.devices.reshape(4, 4, 4, 2), ("dp", "y", "x", "core"))
    ctx = ("y", "x", "core")
    return jax.shard_map(
        on_device,
        mesh=grid,
        in_specs=(
            P("dp", ctx, None),
            P("dp", ctx, None),
            P("dp", ctx, None),
            P(),
            P(),
            P(),
            P("dp", ctx),
            P(ctx, None, None),
            P("dp", ctx, None),
        ),
        out_specs=(P("dp", ctx, None), P(), P(), P()),
        check_vma=False,
    )
```

time: 663 us -> 264 us (0.40)
  waiting for transfers between devices: 502 us -> 66 us
  Pallas kernels: 0 us -> 50.4 us
  starting transfers between devices: 17.7 us -> 55 us
  matrix products: 36.8 us -> 2.97 us
  local copies, waits for them, and re-layouts: 49.9 us -> 22.3 us
  blocking collectives: 24.9 us -> 42.2 us
    reduce_scatter x1 -> x0, waiting for transfers between devices: 319 us -> none  [on_device(): dv_own = lax.psum_scatter(dv_full, 'ctx', scatter_dimension=0, tiled=True)]
    psum x1 -> x0, waiting for transfers between devices: 156 us -> none  [on_device(): lax.psum((grad_a, query_up_gradient, value_up_gradient), ('dp', 'ctx'))]
    all_to_all x4 -> x7, waiting for transfers between devices: 10 us -> 64.9 us  [the longest x1 18.1 us: on_device(): parts = lax.all_to_all(grad.reshape(64, 64, 128), CHIP, 0, 0, tiled=True)]
    pallas_call x0 -> x6, Pallas kernels: none -> 50.4 us  [the longest x1 36.4 us: attention(): pl.pallas_call(attention_kernel, out_shape=(jax.ShapeDtypeStruct((4, BLOC...]
    all_to_all x0 -> x2, blocking collectives: none -> 42.2 us  [the longest x1 25.9 us: on_device(): lax.all_to_all(jnp.broadcast_to(shard[None], (64, 88, 128)), CHIP, 0, 0,...]
    dot_general x13 -> x1, matrix products: 36.8 us -> 2.97 us  [on_device(): lax.dot_general(jnp.concatenate([own_half, other_half], axis=0), jnp.conc...]
    all_to_all x4 -> x7, starting transfers between devices: 17.7 us -> 46 us  [the longest x1 16.1 us: on_device(): sums = lax.all_to_all(send, LANE, 0, 0, tiled=True)]
    all_gather x1 -> x0, blocking collectives: 24.9 us -> none  [on_device(): lax.all_gather(seg_own, 'ctx', axis=0, tiled=True)]
  transfers between devices with their start and end apart: 7 -> 11, of which waited for: 6 -> 7; matrix products, arithmetic and copies ran while one was open for 3% -> 6% of each run, Pallas kernels for 0% -> 18%
where the time goes in v1:
time: 264 us; the launch traced here: 261 us
  waiting for transfers between devices  66 us (25%)
  starting transfers between devices  55 us (21%)
  Pallas kernels  50.4 us (19%)
  blocking collectives  42.2 us (16%)
  local copies, waits for them, and re-layouts  22.3 us (8%)
  between operations  14.3 us (5%)
  other arithmetic  7.93 us (3%)
  matrix products  2.97 us (1%)
    pallas_call x1, Pallas kernels, attention(): pl.pallas_call(attention_kernel, out_shape=(jax.ShapeDtypeStruct((4, BLOC...  36.4 us
    all_to_all x1, blocking collectives, on_device(): lax.all_to_all(jnp.broadcast_to(shard[None], (64, 88, 128)), CHIP, 0, 0,...  25.9 us
    all_to_all x1, waiting for transfers between devices, on_device(): parts = lax.all_to_all(grad.reshape(64, 64, 128), CHIP, 0, 0, tiled=True)  18.1 us
    all_to_all x1, blocking collectives, on_device(): lax.all_to_all(middle(back, my_y.reshape(1), sums, lg), ('dp', 'y'), 0, 0...  16.3 us
    all_to_all x1, starting transfers between devices, on_device(): sums = lax.all_to_all(send, LANE, 0, 0, tiled=True)  16.1 us
    all_to_all x1, waiting for transfers between devices, on_device(): out = lax.all_to_all(out, 'y', 0, 0, tiled=True)  15.2 us
    all_to_all x1, waiting for transfers between devices, on_device(): sums = lax.all_to_all(send, LANE, 0, 0, tiled=True)  11.6 us
    unnamed x35, local copies, waits for them, and re-layouts  10.1 us
  transfers between devices with their start and end apart: 11, of which 7 were waited for; matrix products, arithmetic and copies ran while one was open for 6% of the time, Pallas kernels for 18%

profile of v1, /device:TPU:1, one launch (start us, length us, event | category | flops | bytes accessed | tf_op | source)
XLA Modules:
  0.0 261.1 jit_solution(11908845153598856994)
XLA Ops:
  9.3 5.0 %all-to-all-start = ((s32[4,2,128]{2,1,0:T(2,128)}), s32[4,2,128]{2,1,0:T(2,128)S(1)}, u32[]{:S(2)}, u32[]{:S(2)}) async-start(s32[4,2,128]{2,1,0:T(2,128)} %broadcast_in_dim.14), calls=%async_computation | async-start | bytes 8192 | tf_op jit(solution)/shard_map/all_to_all | solution.py:366
  16.5 1.6 copy-done.3
  18.1 1.6 copy-done.5
  20.6 2.0 shard_map.120
  22.6 8.0 %all-to-all-start.1 = ((bf16[16,32,384]{2,1,0:T(8,128)(2,1)}), bf16[16,32,384]{2,1,0:T(8,128)(2,1)S(1)}, u32[]{:S(2)}, u32[]{:S(2)}) async-start(bf16[16,32,384]{2,1,0:T(8,128)(2,1)} %shard_map.120), calls=%async_computation.1 | async-start | bytes 786432 | tf_op jit(solution)/shard_map/all_to_all | solution.py:373
  32.5 6.6 %all-to-all-done.1.c0.c1.c2.c3.l0.l1.l2.l3 = bf16[16,32,384]{2,1,0:T(8,128)(2,1)S(1)} async-done(((bf16[16,32,384]{2,1,0:T(8,128)(2,1)}), bf16[16,32,384]{2,1,0:T(8,128)(2,1)S(1)}, u32[]{:S(2)}, u32[]{:S(2)}) %all-to-all-start.1) | async-done | bytes 393248 | tf_op jit(solution)/shard_map/all_to_all | solution.py:373
  39.8 4.2 %shard_map.121 = bf16[4,128,384]{2,1,0:T(8,128)(2,1)} custom-call(s32[16]{0:T(128)} %add.52.order_ref, bf16[16,32,384]{2,1,0:T(8,128)(2,1)} %copy-done.1, bf16[16,32,384]{2,1,0:T(8,128)(2,1)} %copy-done.1, bf16[16,32,384]{2,1,0:T(8,128)(2,1)} %copy-done.1, bf16[16,32,384]{2,1,0:T(8,128)(2,1)} %copy-done.1, s32[4,128,1]{2,1,0:T(8,128)} %copy.50.resp_ref, ...), custom_call_target="tpu_custom_call" | custom-call | flops 8388608 | bytes 1048576 | tf_op jit(solution)/shard_map/pallas_call | solution.py:101
  46.0 4.3 %all-to-all-start.3 = ((bf16[4,128,1024]{2,1,0:T(8,128)(2,1)}), bf16[4,128,1024]{2,1,0:T(8,128)(2,1)}, u32[]{:S(2)}, u32[]{:S(2)}) async-start(bf16[4,128,1024]{2,1,0:T(8,128)(2,1)} %bitcast.12), calls=%async_computation.3 | async-start | bytes 2097152 | tf_op jit(solution)/shard_map/all_to_all | solution.py:383
  50.3 4.2 %shard_map.122 = bf16[4,4,32,1024]{3,2,1,0:T(8,128)(2,1)} custom-call(s32[4]{0:T(128)} %copy-done.9, bf16[128,4096]{1,0:T(8,128)(2,1)} %bitcast.54), custom_call_target="tpu_custom_call" | custom-call | bytes 2097152 | tf_op jit(solution)/shard_map/pallas_call | solution.py:72
  54.5 8.1 %all-to-all-done.3.do_ref = bf16[4,128,1024]{2,1,0:T(8,128)(2,1)} async-done(((bf16[4,128,1024]{2,1,0:T(8,128)(2,1)}), bf16[4,128,1024]{2,1,0:T(8,128)(2,1)}, u32[]{:S(2)}, u32[]{:S(2)}) %all-to-all-start.3) | async-done | bytes 1048608 | tf_op jit(solution)/shard_map/all_to_all | solution.py:383
  62.5 4.3 %all-to-all-start.2 = ((bf16[16,32,1024]{2,1,0:T(8,128)(2,1)}), bf16[16,32,1024]{2,1,0:T(8,128)(2,1)}, u32[]{:S(2)}, u32[]{:S(2)}) async-start(bf16[16,32,1024]{2,1,0:T(8,128)(2,1)} %bitcast.48), calls=%async_computation.2 | async-start | bytes 2097152 | tf_op jit(solution)/shard_map/all_to_all | solution.py:380
  66.9 1.5 dynamic-slice_bitcast_fusion.1
  68.4 3.8 %collective-permute-start = (bf16[128,4096]{1,0:T(8,128)(2,1)}, bf16[128,4096]{1,0:T(8,128)(2,1)}, u32[]{:S(2)}, u32[]{:S(2)}) collective-permute-start(bf16[128,4096]{1,0:T(8,128)(2,1)} %get-tuple-element.39), channel_id=1, source_target_pairs={{0,1},{1,0},{2,3},{3,2},{4,5},{5,4},{6,7},{7,6},{8,9},{9,8},{10,11... | collective-permute-start | bytes 3145736 | tf_op jit(solution)/shard_map/ppermute | solution.py:361
  72.3 2.1 convert_reduce_fusion
  75.0 5.4 %all-to-all-done.2.q0.q1.q2.q3 = bf16[16,32,1024]{2,1,0:T(8,128)(2,1)} async-done(((bf16[16,32,1024]{2,1,0:T(8,128)(2,1)}), bf16[16,32,1024]{2,1,0:T(8,128)(2,1)}, u32[]{:S(2)}, u32[]{:S(2)}) %all-to-all-start.2) | async-done | bytes 1048608 | tf_op jit(solution)/shard_map/all_to_all | solution.py:380
  80.4 36.4 %shard_map.123 = (bf16[4,128,1024]{2,1,0:T(8,128)(2,1)}, f32[64,512]{1,0:T(8,128)S(1)}, bf16[8,64,768]{2,1,0:T(8,128)(2,1)}) custom-call(s32[16]{0:T(128)S(1)} %copy-done.10, s32[4]{0:T(128)S(1)} %and_select_fusion.steps_ref, s32[1]{0:T(128)} %bitcast.8.lane_ref, bf16[16,32,1024]{2,1,0:T(8,128)(2,1)} %all-to-all-done.2.q0.q1.q2.q3, ...), custom_call_target="tpu_custom_call" | custom-call | flops 21474836480 | bytes 8388608 | tf_op jit(solution)/shard_map/pallas_call | solution.py:247
  117.5 16.1 %all-to-all-start.5 = ((bf16[8,64,768]{2,1,0:T(8,128)(2,1)}), bf16[8,64,768]{2,1,0:T(8,128)(2,1)S(1)}, u32[]{:S(2)}, u32[]{:S(2)}) async-start(bf16[8,64,768]{2,1,0:T(8,128)(2,1)} %get-tuple-element.10), calls=%async_computation.5 | async-start | bytes 1572864 | tf_op jit(solution)/shard_map/all_to_all | solution.py:396
  134.3 11.6 %all-to-all-done.5.got_ref = bf16[8,64,768]{2,1,0:T(8,128)(2,1)S(1)} async-done(((bf16[8,64,768]{2,1,0:T(8,128)(2,1)}), bf16[8,64,768]{2,1,0:T(8,128)(2,1)S(1)}, u32[]{:S(2)}, u32[]{:S(2)}) %all-to-all-start.5) | async-done | bytes 786464 | tf_op jit(solution)/shard_map/all_to_all | solution.py:396
  146.8 2.0 shard_map.124
  148.8 16.3 %all_to_all.45.got_ref = bf16[16,64,128]{2,1,0:T(8,128)(2,1)} all-to-all(bf16[16,64,128]{2,1,0:T(8,128)(2,1)} %shard_map.124), channel_id=1, replica_groups=mesh['dp'=4,'y'=4,'x'=4,'core'=2] {'dp','y'}, dimensions={0} | all-to-all | bytes 524288 | tf_op jit(solution)/shard_map/all_to_all | solution.py:397
  165.1 1.6 shard_map.125
  166.7 2.3 collective-permute-start.1
  170.0 3.0 %convolution_convert_fusion = bf16[4096,128]{1,0:T(8,128)(2,1)} fusion(bf16[128,4096]{1,0:T(8,128)(2,1)} %collective-permute-done, bf16[128,4096]{1,0:T(8,128)(2,1)S(1)} %copy-done.12, bf16[128,128]{1,0:T(8,128)(2,1)S(1)} %collective-permute-done.1, bf16[128,128]{1,0:T(8,128)(2,1)} %get-tuple-element.12), kind=kOutput, calls=%fused_computation | convolution fusion | flops 273285120 | bytes 3211264 | tf_op jit(solution)/shard_map/dot_general | solution.py:400
  173.0 4.8 %all-to-all-start.7 = ((bf16[64,64,128]{2,1,0:T(8,128)(2,1)}), bf16[64,64,128]{2,1,0:T(8,128)(2,1)S(1)}, u32[]{:S(2)}, u32[]{:S(2)}) async-start(bf16[64,64,128]{2,1,0:T(8,128)(2,1)} %bitcast.20), calls=%async_computation.7 | async-start | bytes 2097152 | tf_op jit(solution)/shard_map/all_to_all | solution.py:406
  177.9 18.1 %all-to-all-done.7 = bf16[64,64,128]{2,1,0:T(8,128)(2,1)S(1)} async-done(((bf16[64,64,128]{2,1,0:T(8,128)(2,1)}), bf16[64,64,128]{2,1,0:T(8,128)(2,1)S(1)}, u32[]{:S(2)}, u32[]{:S(2)}) %all-to-all-start.7) | async-done | bytes 1048608 | tf_op jit(solution)/shard_map/all_to_all | solution.py:406
  196.4 25.9 %all_to_all.46 = bf16[64,88,128]{2,1,0:T(8,128)(2,1)S(1)} all-to-all(bf16[64,88,128]{2,1,0:T(8,128)(2,1)S(1)} %broadcast_in_dim.17), channel_id=1, replica_groups=mesh['dp'=4,'y'=4,'x'=4,'core'=2] {'dp','y','x'}, dimensions={0} | all-to-all | bytes 2883584 | tf_op jit(solution)/shard_map/all_to_all | solution.py:410
  222.4 2.9 %collective-permute-start.2 = (bf16[64,88,128]{2,1,0:T(8,128)(2,1)S(1)}, bf16[64,88,128]{2,1,0:T(8,128)(2,1)}, u32[]{:S(2)}, u32[]{:S(2)}) collective-permute-start(bf16[64,88,128]{2,1,0:T(8,128)(2,1)S(1)} %all_to_all.46), channel_id=1, source_target_pairs={{0,1},{1,0},{2,3},{3,2},{4,5},{5,4},{6,7},{7,6},{8,9},{9,8},{10,11... | collective-permute-start | bytes 4325384 | tf_op jit(solution)/shard_map/ppermute | solution.py:411
  225.2 3.5 %all-to-all-start.4 = ((bf16[4,128,1024]{2,1,0:T(8,128)(2,1)}), bf16[4,128,1024]{2,1,0:T(8,128)(2,1)S(1)}, u32[]{:S(2)}, u32[]{:S(2)}) async-start(bf16[4,128,1024]{2,1,0:T(8,128)(2,1)} %get-tuple-element.9), calls=%async_computation.4 | async-start | bytes 2097152 | tf_op jit(solution)/shard_map/all_to_all | solution.py:420
  228.8 15.2 %all-to-all-done.4 = bf16[4,128,1024]{2,1,0:T(8,128)(2,1)S(1)} async-done(((bf16[4,128,1024]{2,1,0:T(8,128)(2,1)}), bf16[4,128,1024]{2,1,0:T(8,128)(2,1)S(1)}, u32[]{:S(2)}, u32[]{:S(2)}) %all-to-all-start.4) | async-done | bytes 1048608 | tf_op jit(solution)/shard_map/all_to_all | solution.py:420
  245.3 2.3 copy.59
  247.6 1.6 select_bitcast_fusion
  249.8 2.3 fusion.1
  (77 shorter events, 18.4 us)
Async XLA Ops:
  7.2 65.1 %copy-start = (bf16[64,4096]{1,0:T(8,128)(2,1)S(1)}, bf16[64,4096]{1,0:T(8,128)(2,1)}, u32[]{:S(2)}) copy-start(bf16[64,4096]{1,0:T(8,128)(2,1)} %param.13) | copy-start | bytes 1572868
  9.3 13.3 %all-to-all-start = ((s32[4,2,128]{2,1,0:T(2,128)}), s32[4,2,128]{2,1,0:T(2,128)S(1)}, u32[]{:S(2)}, u32[]{:S(2)}) async-start(s32[4,2,128]{2,1,0:T(2,128)} %broadcast_in_dim.14), calls=%async_computation | async-start | bytes 8192 | tf_op jit(solution)/shard_map/all_to_all | solution.py:366
  15.0 7.6 %copy-start.15 = (s32[4]{0:T(128)}, s32[4]{0:T(128)S(1)}, u32[]{:S(2)}) copy-start(s32[4]{0:T(128)S(1)} %fusion.9.outgoing_ref) | copy-start | bytes 52
  15.2 7.5 %copy-start.9 = (s32[4]{0:T(128)}, s32[4]{0:T(128)S(1)}, u32[]{:S(2)}) copy-start(s32[4]{0:T(128)S(1)} %select_reduce_fusion.3.order_ref) | copy-start | bytes 52
  16.5 1.6 copy-start.3
  18.1 1.6 copy-start.5
  19.7 0.9 copy-start.6
  22.6 21.4 %copy-start.13 = (bf16[1,128,4096]{2,1,0:T(8,128)(2,1)S(1)}, bf16[1,128,4096]{2,1,0:T(8,128)(2,1)}, u32[]{:S(2)}) copy-start(bf16[1,128,4096]{2,1,0:T(8,128)(2,1)} %param.17) | copy-start | bytes 3145732
  22.6 16.4 %all-to-all-start.1 = ((bf16[16,32,384]{2,1,0:T(8,128)(2,1)}), bf16[16,32,384]{2,1,0:T(8,128)(2,1)S(1)}, u32[]{:S(2)}, u32[]{:S(2)}) async-start(bf16[16,32,384]{2,1,0:T(8,128)(2,1)} %shard_map.120), calls=%async_computation.1 | async-start | bytes 786432 | tf_op jit(solution)/shard_map/all_to_all | solution.py:373
  30.6 41.7 %all-gather.3.cloned.1.call-start = ((), (), s32[]{:S(2)}) async-start(), calls=%async_computation.9 | async-start | bytes 3538944 | tf_op jit(solution)/shard_map/all_gather | solution.py:379
  39.0 0.8 copy-start.1
  46.0 16.5 %all-to-all-start.3 = ((bf16[4,128,1024]{2,1,0:T(8,128)(2,1)}), bf16[4,128,1024]{2,1,0:T(8,128)(2,1)}, u32[]{:S(2)}, u32[]{:S(2)}) async-start(bf16[4,128,1024]{2,1,0:T(8,128)(2,1)} %bitcast.12), calls=%async_computation.3 | async-start | bytes 2097152 | tf_op jit(solution)/shard_map/all_to_all | solution.py:383
  50.3 16.6 %copy-start.4 = (bf16[1,128,8192]{2,1,0:T(8,128)(2,1)S(1)}, bf16[1,128,8192]{2,1,0:T(8,128)(2,1)}, u32[]{:S(2)}) copy-start(bf16[1,128,8192]{2,1,0:T(8,128)(2,1)} %param.9) | copy-start | bytes 6291460
  62.5 17.9 %all-to-all-start.2 = ((bf16[16,32,1024]{2,1,0:T(8,128)(2,1)}), bf16[16,32,1024]{2,1,0:T(8,128)(2,1)}, u32[]{:S(2)}, u32[]{:S(2)}) async-start(bf16[16,32,1024]{2,1,0:T(8,128)(2,1)} %bitcast.48), calls=%async_computation.2 | async-start | bytes 2097152 | tf_op jit(solution)/shard_map/all_to_all | solution.py:380
  66.9 13.6 %copy-start.2 = (bf16[16,32,384]{2,1,0:T(8,128)(2,1)S(1)}, bf16[16,32,384]{2,1,0:T(8,128)(2,1)}, u32[]{:S(2)}) copy-start(bf16[16,32,384]{2,1,0:T(8,128)(2,1)} %copy-done.1) | copy-start | bytes 1179652
  66.9 13.5 %copy-start.8 = (bf16[64,128]{1,0:T(8,128)(2,1)S(1)}, bf16[64,128]{1,0:T(8,128)(2,1)}, u32[]{:S(2)}) copy-start(bf16[64,128]{1,0:T(8,128)(2,1)} %constant_dynamic-slice_fusion.2.wv_ref) | copy-start | bytes 49156
  66.9 13.5 %copy-start.10 = (s32[16]{0:T(128)S(1)}, s32[16]{0:T(128)}, u32[]{:S(2)}) copy-start(s32[16]{0:T(128)} %add.52.order_ref) | copy-start | bytes 196
  68.4 100.5 %collective-permute-start = (bf16[128,4096]{1,0:T(8,128)(2,1)}, bf16[128,4096]{1,0:T(8,128)(2,1)}, u32[]{:S(2)}, u32[]{:S(2)}) collective-permute-start(bf16[128,4096]{1,0:T(8,128)(2,1)} %get-tuple-element.39), channel_id=1, source_target_pairs={{0,1},{1,0},{2,3},{3,2},{4,5},{5,4},{6,7},{7,6},{8,9},{9,8},{10,11... | collective-permute-start | bytes 3145736 | tf_op jit(solution)/shard_map/ppermute | solution.py:361
  116.8 0.7 copy-start.7
  117.5 52.6 %copy-start.12 = (bf16[128,4096]{1,0:T(8,128)(2,1)S(1)}, bf16[128,4096]{1,0:T(8,128)(2,1)}, u32[]{:S(2)}) copy-start(bf16[128,4096]{1,0:T(8,128)(2,1)} %get-tuple-element.38) | copy-start | bytes 3145732
  117.5 28.4 %all-to-all-start.5 = ((bf16[8,64,768]{2,1,0:T(8,128)(2,1)}), bf16[8,64,768]{2,1,0:T(8,128)(2,1)S(1)}, u32[]{:S(2)}, u32[]{:S(2)}) async-start(bf16[8,64,768]{2,1,0:T(8,128)(2,1)} %get-tuple-element.10), calls=%async_computation.5 | async-start | bytes 1572864 | tf_op jit(solution)/shard_map/all_to_all | solution.py:396
  145.9 0.9 copy-start.11
  166.7 3.3 %collective-permute-start.1 = (bf16[128,128]{1,0:T(8,128)(2,1)}, bf16[128,128]{1,0:T(8,128)(2,1)S(1)}, u32[]{:S(2)}, u32[]{:S(2)}) collective-permute-start(bf16[128,128]{1,0:T(8,128)(2,1)} %get-tuple-element.12), channel_id=1, source_target_pairs={{0,1},{1,0},{2,3},{3,2},{4,5},{5,4},{6,7},{7,6},{8,9},{9,8},{10,11... | collective-permute-start | bytes 98312 | tf_op jit(solution)/shard_map/ppermute | solution.py:399
  173.0 4.9 %copy-start.14 = (f32[32,128]{1,0:T(8,128)S(1)}, f32[32,128]{1,0:T(8,128)}, u32[]{:S(2)}) copy-start(f32[32,128]{1,0:T(8,128)} %get-tuple-element.13) | copy-start | bytes 49156
  173.0 23.0 %all-to-all-start.7 = ((bf16[64,64,128]{2,1,0:T(8,128)(2,1)}), bf16[64,64,128]{2,1,0:T(8,128)(2,1)S(1)}, u32[]{:S(2)}, u32[]{:S(2)}) async-start(bf16[64,64,128]{2,1,0:T(8,128)(2,1)} %bitcast.20), calls=%async_computation.7 | async-start | bytes 2097152 | tf_op jit(solution)/shard_map/all_to_all | solution.py:406
  222.4 25.2 %collective-permute-start.2 = (bf16[64,88,128]{2,1,0:T(8,128)(2,1)S(1)}, bf16[64,88,128]{2,1,0:T(8,128)(2,1)}, u32[]{:S(2)}, u32[]{:S(2)}) collective-permute-start(bf16[64,88,128]{2,1,0:T(8,128)(2,1)S(1)} %all_to_all.46), channel_id=1, source_target_pairs={{0,1},{1,0},{2,3},{3,2},{4,5},{5,4},{6,7},{7,6},{8,9},{9,8},{10,11... | collective-permute-start | bytes 4325384 | tf_op jit(solution)/shard_map/ppermute | solution.py:411
  225.2 18.8 %all-to-all-start.4 = ((bf16[4,128,1024]{2,1,0:T(8,128)(2,1)}), bf16[4,128,1024]{2,1,0:T(8,128)(2,1)S(1)}, u32[]{:S(2)}, u32[]{:S(2)}) async-start(bf16[4,128,1024]{2,1,0:T(8,128)(2,1)} %get-tuple-element.9), calls=%async_computation.4 | async-start | bytes 2097152 | tf_op jit(solution)/shard_map/all_to_all | solution.py:420
Sparse Core Ops, SparseCore 0:
  44.1 27.5 all-gather.2

commit v2 on v1

v2 whole, which is shorter than its diff:
```python
import functools
import math

import jax
import jax.numpy as jnp
from jax import lax
from jax.experimental import pallas as pl
from jax.experimental.pallas import tpu as pltpu
from jax.sharding import Mesh
from jax.sharding import PartitionSpec as P

HEAD = 128
BLOCK = 128
QUARTER = 32
KEY_CHUNK = 512
PAD = KEY_CHUNK - BLOCK
ROWS_STEP = 8 * BLOCK
SCALE = 0.5
MASKED = -1e30
INVERSE = 1.0 / math.sqrt(HEAD)
LOG2E = 1.4426950408889634
BF = jnp.bfloat16
F32 = jnp.float32
NT = (((1,), (1,)), ((), ()))
TN = (((0,), (0,)), ((), ()))
VMEM = pltpu.VMEM
CHIP = ("dp", "y", "x")
ROWS = ("dp", "y")
ALL = ("dp", "y", "x", "core")
SHARD = 88


def turn(d):
    return [(y, (y + d) % 4) for y in range(4)]


def whole():
    return pl.BlockSpec(memory_space=pltpu.VMEM)


def scalars():
    return pl.BlockSpec(memory_space=pltpu.SMEM)


def params(mib):
    return pltpu.CompilerParams(vmem_limit_bytes=mib << 20)


def front_kernel(order_ref, x_ref, a_ref, kv_ref, out_ref, acc_ref, low_ref):
    step = pl.program_id(0)

    @pl.when(step == 0)
    def _():
        acc_ref[...] = jnp.zeros_like(acc_ref)

    acc_ref[...] += jnp.dot(x_ref[...], a_ref[...], preferred_element_type=F32)

    @pl.when(step == pl.num_programs(0) - 1)
    def _():
        low_ref[...] = acc_ref[...].astype(BF)
        for r in range(4):
            rows = pl.ds(pl.multiple_of(order_ref[r] * QUARTER, QUARTER), QUARTER)
            low = low_ref[rows, :]
            for y in range(4):
                out_ref[r * 4 + y, :, 0:128] = kv_ref[rows, y * 128 : y * 128 + 128]
                out_ref[r * 4 + y, :, 128:256] = kv_ref[rows, 512 + y * 128 : 640 + y * 128]
                out_ref[r * 4 + y, :, 256:384] = low


def front(order, x, a, kv):
    steps = 8
    part = 8192 // steps
    return pl.pallas_call(
        front_kernel,
        out_shape=jax.ShapeDtypeStruct((16, QUARTER, 384), BF),
        grid_spec=pltpu.PrefetchScalarGridSpec(
            num_scalar_prefetch=1,
            grid=(steps,),
            in_specs=[
                pl.BlockSpec((BLOCK, part), lambda i, order: (0, i)),
                pl.BlockSpec((part, 128), lambda i, order: (i, 0)),
                pl.BlockSpec((BLOCK, 1024), lambda i, order: (0, 0)),
            ],
            out_specs=pl.BlockSpec((16, QUARTER, 384), lambda i, order: (0, 0, 0)),
            scratch_shapes=[VMEM((BLOCK, 128), F32), VMEM((BLOCK, 128), BF)],
        ),
        compiler_params=params(58),
        cost_estimate=pl.CostEstimate(flops=2 * 128 * 8192 * 128, bytes_accessed=5 << 20, transcendentals=0),
    )(order, x, a, kv)


def query_chunks_kernel(order_ref, q_ref, out_ref, sem):
    copies = []
    for r in range(4):
        rows = pl.ds(pl.multiple_of(order_ref[r] * QUARTER, QUARTER), QUARTER)
        for y in range(4):
            copies.append(
                pltpu.make_async_copy(
                    q_ref.at[rows, pl.ds(y * 1024, 1024)], out_ref.at[r * 4 + y], sem.at[r * 4 + y]
                )
            )
    for copy in copies:
        copy.start()
    for copy in copies:
        copy.wait()


def query_chunks(order, q):
    return pl.pallas_call(
        query_chunks_kernel,
        out_shape=jax.ShapeDtypeStruct((16, QUARTER, 1024), BF),
        in_specs=[scalars(), pl.BlockSpec(memory_space=pl.ANY)],
        out_specs=pl.BlockSpec(memory_space=pl.ANY),
        scratch_shapes=[pltpu.SemaphoreType.DMA((16,))],
        compiler_params=params(48),
        cost_estimate=pl.CostEstimate(flops=0, bytes_accessed=2 << 20, transcendentals=0),
    )(order, q)


def pack_kernel(scalar_ref, got_ref, notes_ref, wv_ref, out_ref):
    lane = lax.broadcasted_iota(jnp.int32, (QUARTER, 64), 1)
    for i in range(4):
        y = scalar_ref[28 + i]
        below = [
            jnp.sum(jnp.where(notes_ref[i, 0:1, :] < v, 1.0, 0.0), axis=1, keepdims=True) for v in range(1, 4)
        ]
        for k in range(4):
            at = scalar_ref[i * 4 + k]
            rows = got_ref[at]
            low_v = rows[:, 320:384]
            value = rows[:, 128:256].astype(F32) + SCALE * jnp.dot(
                low_v, wv_ref[...], preferred_element_type=F32
            )
            source = (at // 4).astype(F32)
            extra = jnp.where(lane == 0, 1.0, jnp.where(lane == 1, source, 0.0))
            for v in range(1, 4):
                extra = jnp.where(lane == 1 + v, below[v - 1], extra)
            span = slice(k * QUARTER, (k + 1) * QUARTER)
            out_ref[y, span, 0:128] = rows[:, 0:128]
            out_ref[y, span, 128:256] = value.astype(BF)
            out_ref[y, span, 256:384] = jnp.concatenate([low_v.astype(F32), extra], axis=1).astype(BF)


def pack(scalar, got, notes, wv):
    return pl.pallas_call(
        pack_kernel,
        out_shape=jax.ShapeDtypeStruct((4, BLOCK, 384), BF),
        in_specs=[scalars(), whole(), whole(), whole()],
        out_specs=whole(),
        cost_estimate=pl.CostEstimate(flops=1 << 23, bytes_accessed=1 << 20, transcendentals=0),
    )(scalar, got, notes, wv)


def attention_kernel(
    scalar_ref, q_ref, got_ref, d0, d1, d2, d3, notes_ref, kv_ref, wv_ref, wq_ref,
    out_ref, send_ref, up_ref,
    kv_s, s_s, w_s, t_s, m_s, acc_s, dq_s, dout_s, lg_s, qup_s, vup_s, below_s, sem,
):
    copies = []
    for c in range(32):
        copies.append(
            pltpu.make_async_copy(
                kv_ref.at[c % 8, c // 8], kv_s.at[pl.ds(PAD + c * BLOCK, BLOCK), :], sem.at[c]
            )
        )
    for copy in copies:
        copy.start()
    kv_s[0:PAD, :] = jnp.zeros((PAD, 384), BF)
    t_s[...] = jnp.zeros_like(t_s)
    qup_s[...] = jnp.zeros_like(qup_s)
    vup_s[...] = jnp.zeros_like(vup_s)
    for i, d in enumerate((d0, d1, d2, d3)):
        for h in range(8):
            dout_s[i, h * BLOCK : (h + 1) * BLOCK, :] = d[:, h * HEAD : (h + 1) * HEAD]
    for copy in copies:
        copy.wait()
    counts = kv_s[PAD : PAD + 16, 256:384].astype(F32)
    for c in range(1, 32):
        counts = counts + kv_s[PAD + c * BLOCK : PAD + c * BLOCK + 16, 256:384].astype(F32)
    lane = lax.broadcasted_iota(jnp.int32, (1, 128), 1)
    below_s[0] = 0
    for v in range(1, 4):
        below_s[v] = jnp.sum(jnp.where(lane == 65 + v, counts[0:1, :], 0.0)).astype(jnp.int32)
    diagonal = lax.broadcasted_iota(jnp.int32, (BLOCK, BLOCK), 0) == lax.broadcasted_iota(
        jnp.int32, (BLOCK, BLOCK), 1
    )

    def turn_of(i, _):
        block = scalar_ref[16 + i]
        high = (block + 1) * BLOCK
        steps = (high - below_s[scalar_ref[20 + i]] + KEY_CHUNK - 1) // KEY_CHUNK
        clean = jnp.clip((high - below_s[scalar_ref[24 + i]]) // KEY_CHUNK, 1, steps)
        resp = notes_ref[i, 0:1, :]
        start = jnp.zeros((1, BLOCK), jnp.int32)
        for v in range(1, 4):
            start = jnp.where(resp == v, below_s[v], start)
        start = jnp.sum(jnp.where(diagonal, start.astype(F32), 0.0), axis=1, keepdims=True).astype(jnp.int32)
        start = jnp.concatenate([start] * 8, axis=0)
        row = block * BLOCK + lax.broadcasted_iota(jnp.int32, (BLOCK, 1), 0)
        row = jnp.concatenate([row] * 8, axis=0)

        chunks = [scalar_ref[i * 4 + k] for k in range(4)]
        low = jnp.concatenate([got_ref[c, :, 256:384] for c in chunks], axis=0)
        q_in = jnp.concatenate([q_ref[c] for c in chunks], axis=0).astype(F32)
        query = (
            q_in + SCALE * jnp.dot(low[:, 0:64], wq_ref[...], preferred_element_type=F32)
        ).astype(BF)
        query = jnp.concatenate([query[:, h * HEAD : (h + 1) * HEAD] for h in range(8)], axis=0)
        dout = dout_s[i]

        def place(t):
            return pl.multiple_of(PAD + high - KEY_CHUNK * (t + 1), BLOCK)

        m_s[...] = jnp.full_like(m_s, MASKED)

        def scores(t, masked):
            at = place(t)
            s = lax.dot_general(query, kv_s[pl.ds(at, KEY_CHUNK), 0:128], NT, preferred_element_type=F32)
            if masked:
                key = at - PAD + lax.broadcasted_iota(jnp.int32, (1, KEY_CHUNK), 1)
                s = jnp.where((key >= start) & (key <= row), s, MASKED)
            s_s[t] = s
            top = m_s[...]
            for c in range(KEY_CHUNK // 128):
                top = jnp.maximum(top, s[:, c * 128 : (c + 1) * 128])
            m_s[...] = top

        def clean_scores(t, _):
            scores(t, False)
            return 0

        def masked_scores(t, _):
            scores(t, True)
            return 0

        scores(0, True)
        lax.fori_loop(1, clean, clean_scores, 0)
        lax.fori_loop(clean, steps, masked_scores, 0)
        top = jnp.max(m_s[...], axis=1, keepdims=True)
        acc_s[...] = jnp.zeros_like(acc_s)

        def forward(t, _):
            w = jnp.exp2((s_s[t] - top) * (INVERSE * LOG2E)).astype(BF)
            w_s[t] = w
            acc_s[...] += jnp.dot(w, kv_s[pl.ds(place(t), KEY_CHUNK), 128:384], preferred_element_type=F32)
            return 0

        lax.fori_loop(0, steps, forward, 0)
        over = 1.0 / acc_s[:, 192:193]
        out = (acc_s[:, 0:128] * over).astype(BF)
        for h in range(8):
            out_ref[i, :, h * HEAD : (h + 1) * HEAD] = out[h * BLOCK : (h + 1) * BLOCK, :]
        wide = dout.astype(F32)
        delta = jnp.sum(wide * out.astype(F32), axis=1, keepdims=True) * over
        scaled = (wide * over).astype(BF)
        g = lax.dot_general(wv_ref[...], scaled, NT, preferred_element_type=F32).astype(BF)
        weighted_low = (acc_s[:, 128:256] * over).astype(BF)
        vup_s[...] += lax.dot_general(weighted_low, dout, TN, preferred_element_type=F32)
        dq_s[...] = jnp.zeros_like(dq_s)

        def backward(t, _):
            at = place(t)
            w = w_s[t]
            dp = lax.dot_general(scaled, kv_s[pl.ds(at, KEY_CHUNK), 128:256], NT, preferred_element_type=F32)
            ds = (w.astype(F32) * (dp - delta)).astype(BF)
            dq_s[...] += jnp.dot(ds, kv_s[pl.ds(at, KEY_CHUNK), 0:128], preferred_element_type=F32)
            t_s[:, pl.ds(at, KEY_CHUNK)] += jnp.dot(g, w, preferred_element_type=F32)
            return 0

        lax.fori_loop(0, steps, backward, 0)
        dq = (dq_s[...] * INVERSE).astype(BF)
        low_t = jnp.transpose(low.astype(F32))[0:64, :].astype(BF)
        lg = jnp.zeros((64, BLOCK), F32)
        for h in range(8):
            dq_h = dq[h * BLOCK : (h + 1) * BLOCK, :]
            lg = lg + lax.dot_general(
                wq_ref[:, h * HEAD : (h + 1) * HEAD], dq_h, NT, preferred_element_type=F32
            )
            qup_s[h] += jnp.dot(low_t, dq_h, preferred_element_type=F32)
        lg_s[i] = lg
        return 0

    lax.fori_loop(0, 4, turn_of, 0)

    for c in range(32):
        at = (scalar_ref[28] - c // 8 + 4) % 4
        own = jnp.where(scalar_ref[16 + at] == c, 1.0, 0.0)
        both = jnp.concatenate([lg_s[at] * own, t_s[:, PAD + c * BLOCK : PAD + (c + 1) * BLOCK]], axis=0)
        both = jnp.transpose(both) * SCALE
        source = kv_s[PAD + c * BLOCK : PAD + (c + 1) * BLOCK, 256:384].astype(F32)[:, 65:66]
        for g in range(4):
            chosen = jnp.where(source == g, both, 0.0)
            send_ref[g * 32 + c] = (
                chosen[0:32, :] + chosen[32:64, :] + chosen[64:96, :] + chosen[96:128, :]
            ).astype(BF)
    for c in range(2):
        for h in range(4):
            up_ref[c, h * 64 : (h + 1) * 64, :] = (qup_s[c * 4 + h] * SCALE).astype(BF)
        up_ref[c, 256:288, :] = (vup_s[c * 32 : (c + 1) * 32, :] * SCALE).astype(BF)


def attention(scalar, q, got, dout, notes, kv, wv, wq):
    chunks = 4096 // KEY_CHUNK
    return pl.pallas_call(
        attention_kernel,
        out_shape=(
            jax.ShapeDtypeStruct((4, BLOCK, 1024), BF),
            jax.ShapeDtypeStruct((128, QUARTER, 128), BF),
            jax.ShapeDtypeStruct((2, 288, 128), BF),
        ),
        in_specs=[scalars()]
        + [whole()] * 7
        + [pl.BlockSpec(memory_space=pl.ANY), whole(), whole()],
        out_specs=(whole(), whole(), whole()),
        scratch_shapes=[
            VMEM((PAD + 4096, 384), BF),
            VMEM((chunks, ROWS_STEP, KEY_CHUNK), F32),
            VMEM((chunks, ROWS_STEP, KEY_CHUNK), BF),
            VMEM((64, PAD + 4096), F32),
            VMEM((ROWS_STEP, 128), F32),
            VMEM((ROWS_STEP, 256), F32),
            VMEM((ROWS_STEP, 128), F32),
            VMEM((4, ROWS_STEP, 128), BF),
            VMEM((4, 64, BLOCK), F32),
            VMEM((8, 64, 128), F32),
            VMEM((128, 128), F32),
            pltpu.SMEM((4,), jnp.int32),
            pltpu.SemaphoreType.DMA((32,)),
        ],
        compiler_params=params(56),
        cost_estimate=pl.CostEstimate(flops=20 << 30, bytes_accessed=8 << 20, transcendentals=8 << 20),
    )(scalar, q, got, *dout, notes, kv, wv, wq)


def low_back_kernel(outgoing_ref, got_ref, low_ref, sum_ref):
    for r in range(4):
        total = got_ref[r * 32].astype(F32)
        for c in range(1, 32):
            total = total + got_ref[r * 32 + c].astype(F32)
        sum_ref[r] = total
    for k in range(4):
        low_ref[k * QUARTER : (k + 1) * QUARTER, :] = sum_ref[outgoing_ref[k]].astype(BF)


def low_back_of(outgoing, got):
    return pl.pallas_call(
        low_back_kernel,
        out_shape=jax.ShapeDtypeStruct((BLOCK, 128), BF),
        in_specs=[scalars(), whole()],
        out_specs=whole(),
        scratch_shapes=[VMEM((4, QUARTER, 128), F32)],
        cost_estimate=pl.CostEstimate(flops=1 << 19, bytes_accessed=1 << 20, transcendentals=0),
    )(outgoing, got)


def grad_kernel(place_ref, x_ref, other_ref, low_ref, low_other_ref, up_ref, up_other_ref, out_ref):
    j = pl.program_id(0)
    rows = jnp.concatenate([x_ref[...], other_ref[...]], axis=0)
    low = jnp.concatenate([low_ref[...], low_other_ref[...]], axis=0)
    grad = lax.dot_general(rows, low, TN, preferred_element_type=F32).astype(BF)
    for d in range(16):
        out_ref[d, 0:64, :] = grad[d * 64 : (d + 1) * 64, :]
    head = pl.ds(pl.multiple_of(j * 64, 64), 64)
    up = up_ref[0, head, :].astype(F32) + up_other_ref[head, :].astype(F32)
    tail = up_ref[0, 256:288, :].astype(F32) + up_other_ref[256:288, :].astype(F32)
    for y in range(4):
        keep = jnp.where(place_ref[1] == y, 1.0, 0.0)
        for x in range(4):
            out_ref[y * 4 + x, 64:80, :] = (up[x * 16 : (x + 1) * 16, :] * keep).astype(BF)
            low_rows = jnp.zeros((2, 128), F32)
            for dp in range(4):
                at = (dp * 4 + x) * 2
                low_rows = low_rows + tail[at : at + 2, :] * jnp.where(j == dp, keep, 0.0)
            out_ref[y * 4 + x, 80:SHARD, :] = jnp.concatenate(
                [low_rows, jnp.zeros((SHARD - 82, 128), F32)], axis=0
            ).astype(BF)


def grad_chunks(place, x, other, low, low_other, up, up_other):
    return pl.pallas_call(
        grad_kernel,
        out_shape=jax.ShapeDtypeStruct((64, SHARD, 128), BF),
        grid_spec=pltpu.PrefetchScalarGridSpec(
            num_scalar_prefetch=1,
            grid=(4,),
            in_specs=[
                pl.BlockSpec((BLOCK, 1024), lambda j, place: (0, place[0] * 4 + j)),
                pl.BlockSpec((BLOCK, 1024), lambda j, place: (0, j)),
                pl.BlockSpec((BLOCK, 128), lambda j, place: (0, 0)),
                pl.BlockSpec((BLOCK, 128), lambda j, place: (0, 0)),
                pl.BlockSpec((1, 288, 128), lambda j, place: (place[0], 0, 0)),
                pl.BlockSpec((288, 128), lambda j, place: (0, 0)),
            ],
            out_specs=pl.BlockSpec((16, SHARD, 128), lambda j, place: (j, 0, 0)),
        ),
        cost_estimate=pl.CostEstimate(flops=2 * 256 * 4096 * 128, bytes_accessed=4 << 20, transcendentals=0),
    )(place, x, other, low, low_other, up, up_other)


def gather_kernel(place_ref, own_ref, other_ref, down_ref, query_ref, value_ref):
    zero = place_ref[0] == 0
    for chip in range(64):
        dp, y, x = chip // 16, chip // 4 % 4, chip % 4
        own, other = own_ref[chip].astype(F32), other_ref[chip].astype(F32)
        for core in range(2):
            part = jnp.where(zero, own, other) if core == 0 else jnp.where(zero, other, own)
            down_ref[core * 4096 + chip * 64 : core * 4096 + (chip + 1) * 64, :] = part[0:64, :]
            column = (y * 8 + core * 4 + dp) * 128
            query_ref[x * 16 : (x + 1) * 16, column : column + 128] = part[64:80, :]
            row = core * 32 + (dp * 4 + x) * 2
            value_ref[row : row + 2, y * 128 : (y + 1) * 128] = part[80:82, :]


def gather_outputs(place, own, other):
    return pl.pallas_call(
        gather_kernel,
        out_shape=(
            jax.ShapeDtypeStruct((8192, 128), F32),
            jax.ShapeDtypeStruct((64, 4096), F32),
            jax.ShapeDtypeStruct((64, 512), F32),
        ),
        in_specs=[scalars(), whole(), whole()],
        out_specs=(whole(), whole(), whole()),
        compiler_params=params(32),
        cost_estimate=pl.CostEstimate(flops=1 << 20, bytes_accessed=8 << 20, transcendentals=0),
    )(place, own, other)


def join_kernel(place_ref, p0, p1, p2, p3, out_ref):
    for i, piece in enumerate((p0, p1, p2, p3)):
        column = (place_ref[1] + i) % 4 * 1024
        out_ref[0, :, pl.ds(pl.multiple_of(column, 1024), 1024)] = piece[...]


def join_heads(place, pieces):
    return pl.pallas_call(
        join_kernel,
        out_shape=jax.ShapeDtypeStruct((1, BLOCK, 4096), BF),
        in_specs=[scalars()] + [whole()] * 4,
        out_specs=whole(),
        cost_estimate=pl.CostEstimate(flops=0, bytes_accessed=2 << 20, transcendentals=0),
    )(place, *pieces)


def on_device(
    generated_input,
    frozen_query,
    frozen_key_value,
    adapter_down_weight,
    query_up_weight,
    value_up_weight,
    response_numbers,
    target_replica,
    output_gradient,
):
    me = lax.axis_index("dp")
    my_y = lax.axis_index("y")
    my_core = lax.axis_index("core")
    my_lane = lax.axis_index("x") * 2 + my_core
    places = jnp.arange(4, dtype=jnp.int32)
    route = target_replica[0]
    outgoing = lax.dynamic_index_in_dim(route, me, 0, keepdims=False)
    send_order = jnp.sum(places[None, :] * (outgoing[None, :] == places[:, None]), axis=1).astype(jnp.int32)
    place = jnp.stack([my_core, my_y]).astype(jnp.int32)
    swap = [(0, 1), (1, 0)]

    rows = generated_input[0]
    sent = front(send_order, rows, adapter_down_weight, frozen_key_value[0])

    row = (my_y - places + 4) % 4
    notes = jnp.concatenate([response_numbers[0], route.reshape(16), jnp.zeros((112,), jnp.int32)])
    notes, sent = lax.optimization_barrier((notes.reshape(2, 128), sent))
    notes = jnp.stack([notes] + [lax.ppermute(notes, "y", turn(d)) for d in range(1, 4)])
    resp = notes[:, 0, :]
    routes = notes[:, 1, 0:16].reshape(4, 4, 4)
    mine = (routes == me).astype(jnp.int32)
    order = (jnp.sum(mine * places[None, :, None], axis=1) * 4 + row[:, None]).reshape(16)
    block = row * 8 + my_lane
    scalar = jnp.concatenate([order, block, resp[:, 0], resp[:, 127], row]).astype(jnp.int32)

    got = lax.all_to_all(sent, ROWS, 0, 0, tiled=True)
    gradient = output_gradient[0]
    dout = []
    for d in range(4):
        part = lax.dynamic_slice_in_dim(gradient, (my_y + d) % 4 * 1024, 1024, 1)
        dout.append(lax.ppermute(part, "y", turn(d)) if d else part)
    wv = lax.dynamic_slice_in_dim(value_up_weight, my_y * 128, 128, 1)
    wq = lax.dynamic_slice_in_dim(query_up_weight, my_y * 1024, 1024, 1)
    packed = pack(scalar, got, notes, wv)
    kv = lax.all_gather(packed, ("x", "core"), axis=0, tiled=False)
    q = lax.all_to_all(
        query_chunks(send_order, frozen_query[0]), ROWS, 0, 0, tiled=True
    )
    other_half = lax.ppermute(
        lax.dynamic_slice_in_dim(rows, (1 - my_core) * 4096, 4096, 1), "core", swap
    )

    out, send, up = attention(scalar, q, got, dout, notes, kv, wv, wq)
    pieces = [out[0]] + [lax.ppermute(out[i], "y", turn(-i)) for i in range(1, 4)]
    up_other = lax.ppermute(
        lax.dynamic_index_in_dim(up, 1 - my_core, 0, keepdims=False), "core", swap
    )
    low_back = low_back_of(outgoing, lax.all_to_all(send, ALL, 0, 0, tiled=True))
    low_back, pieces = lax.optimization_barrier((low_back, pieces))
    low_other = lax.ppermute(low_back, "core", swap)
    chunks = grad_chunks(place, rows, other_half, low_back, low_other, up, up_other)
    parts = lax.all_to_all(chunks, CHIP, 0, 0, tiled=True)
    shard = jnp.sum(parts.astype(F32), axis=0).astype(BF)
    own = lax.all_to_all(jnp.broadcast_to(shard[None], parts.shape), CHIP, 0, 0, tiled=True)
    other = lax.ppermute(own, "core", swap)
    grad_a, query_up_gradient, value_up_gradient = gather_outputs(place, own, other)

    attn_out = join_heads(place, pieces)
    return (attn_out, grad_a, query_up_gradient, value_up_gradient)


def solution(mesh):
    grid = Mesh(mesh.devices.reshape(4, 4, 4, 2), ("dp", "y", "x", "core"))
    ctx = ("y", "x", "core")
    return jax.shard_map(
        on_device,
        mesh=grid,
        in_specs=(
            P("dp", ctx, None),
            P("dp", ctx, None),
            P("dp", ctx, None),
            P(),
            P(),
            P(),
            P("dp", ctx),
            P(ctx, None, None),
            P("dp", ctx, None),
        ),
        out_specs=(P("dp", ctx, None), P(), P(), P()),
        check_vma=False,
    )
```

time: 264 us -> 230 us (0.87)
  waiting for transfers between devices: 66 us -> 38.9 us
  blocking collectives: 42.2 us -> 57.8 us
  local copies, waits for them, and re-layouts: 22.3 us -> 10.3 us
  other arithmetic: 7.93 us -> 2.37 us
  Pallas kernels: 50.4 us -> 54.2 us
  starting transfers between devices: 55 us -> 51.3 us
  matrix products: 2.97 us -> 0 us
    all_to_all x7 -> x3, waiting for transfers between devices: 64.9 us -> 16 us  [the longest x1 10.3 us: on_device(): lax.all_to_all(send, ALL, 0, 0, tiled=True)]
    ppermute x0 -> x10, waiting for transfers between devices: none -> 21.8 us  [the longest x3 17.4 us: on_device(): dout.append(lax.ppermute(part, 'y', turn(d)) if d else part)]
    all_to_all x2, blocking collectives: 42.2 us -> 57.8 us  [the longest x1 30.7 us: on_device(): parts = lax.all_to_all(chunks, CHIP, 0, 0, tiled=True)]
    ppermute x0 -> x10, starting transfers between devices: none -> 14.5 us  [the longest x3 4.68 us: on_device(): lax.ppermute(notes, 'y', turn(d))]
    all_to_all x7 -> x3, starting transfers between devices: 46 us -> 32.5 us  [the longest x1 21.9 us: on_device(): lax.all_to_all(send, ALL, 0, 0, tiled=True)]
    unnamed x35 -> x42, local copies, waits for them, and re-layouts: 10.1 us -> 2.98 us
    pallas_call x3 -> x5, Pallas kernels: 7.83 us -> 14 us  [the longest x1 5.05 us: grad_chunks(): pl.pallas_call(grad_kernel, out_shape=jax.ShapeDtypeStruct((64, SHARD, 12...]
    pallas_call x1, Pallas kernels: 36.4 us -> 31 us  [attention(): pl.pallas_call(attention_kernel, out_shape=(jax.ShapeDtypeStruct((4, BLOC...]
  transfers between devices with their start and end apart: 11 -> 17, of which waited for: 7 -> 8; matrix products, arithmetic and copies ran while one was open for 6% -> 3% of each run, Pallas kernels for 18% -> 3%
where the time goes in v2:
time: 230 us; the launch traced here: 229 us
  blocking collectives  57.8 us (25%)
  Pallas kernels  54.2 us (24%)
  starting transfers between devices  51.3 us (22%)
  waiting for transfers between devices  38.9 us (17%)
  between operations  14.4 us (6%)
  local copies, waits for them, and re-layouts  10.3 us (4%)
  other arithmetic  2.37 us (1%)
    pallas_call x1, Pallas kernels, attention(): pl.pallas_call(attention_kernel, out_shape=(jax.ShapeDtypeStruct((4, BLOC...  31 us
    all_to_all x1, blocking collectives, on_device(): parts = lax.all_to_all(chunks, CHIP, 0, 0, tiled=True)  30.7 us
    all_to_all x1, blocking collectives, on_device(): lax.all_to_all(jnp.broadcast_to(shard[None], parts.shape), CHIP, 0, 0, ti...  27.1 us
    all_to_all x1, starting transfers between devices, on_device(): lax.all_to_all(send, ALL, 0, 0, tiled=True)  21.9 us
    ppermute x3, waiting for transfers between devices, on_device(): dout.append(lax.ppermute(part, 'y', turn(d)) if d else part)  17.4 us
    all_to_all x1, waiting for transfers between devices, on_device(): lax.all_to_all(send, ALL, 0, 0, tiled=True)  10.3 us
    pallas_call x1, Pallas kernels, front(): pl.pallas_call(front_kernel, out_shape=jax.ShapeDtypeStruct((16, QUARTER,...  7.03 us
    all_to_all x1, starting transfers between devices, on_device(): got = lax.all_to_all(sent, ROWS, 0, 0, tiled=True)  6.84 us
  transfers between devices with their start and end apart: 17, of which 8 were waited for; matrix products, arithmetic and copies ran while one was open for 3% of the time, Pallas kernels for 3%

profile of v2, /device:TPU:1, one launch (start us, length us, event | category | flops | bytes accessed | tf_op | source)
XLA Modules:
  0.0 229.1 jit_solution(3628083601729332177)
XLA Ops:
  7.2 0.8 reshape_squeeze.4
  10.1 7.0 %shard_map.120 = bf16[16,32,384]{2,1,0:T(8,128)(2,1)} custom-call(s32[4]{0:T(128)} %select_reduce_fusion.1.order_ref, bf16[128,8192]{1,0:T(8,128)(2,1)} %bitcast.37, bf16[8192,128]{1,0:T(8,128)(2,1)} %a_ref.1, bf16[128,1024]{1,0:T(8,128)(2,1)} %bitcast.39), custom_call_target="tpu_custom_call" | custom-call | flops 268435456 | bytes 5242880 | tf_op jit(solution)/shard_map/pallas_call | solution.py:73
  17.1 3.6 %collective-permute-start.2 = (s32[2,128]{1,0:T(2,128)S(1)}, s32[2,128]{1,0:T(2,128)S(1)}, u32[]{:S(2)}, u32[]{:S(2)}) collective-permute-start(s32[2,128]{1,0:T(2,128)S(1)} %add_bitcast_fusion), channel_id=1, source_target_pairs={{0,24},{8,0},{16,8},{24,16},{1,25},{9,1},{17,9},{25,17},{2,26},{10... | collective-permute-start | bytes 3080 | tf_op jit(solution)/shard_map/ppermute | solution.py:473
  21.8 6.8 %all-to-all-start.1 = ((bf16[16,32,384]{2,1,0:T(8,128)(2,1)}), bf16[16,32,384]{2,1,0:T(8,128)(2,1)S(1)}, u32[]{:S(2)}, u32[]{:S(2)}) async-start(bf16[16,32,384]{2,1,0:T(8,128)(2,1)} %shard_map.120), calls=%async_computation.1 | async-start | bytes 786432 | tf_op jit(solution)/shard_map/all_to_all | solution.py:481
  28.7 1.3 constant_dynamic-slice_fusion.1.wv_ref
  31.2 5.7 %all-to-all-done.1.got_ref = bf16[16,32,384]{2,1,0:T(8,128)(2,1)S(1)} async-done(((bf16[16,32,384]{2,1,0:T(8,128)(2,1)}), bf16[16,32,384]{2,1,0:T(8,128)(2,1)S(1)}, u32[]{:S(2)}, u32[]{:S(2)}) %all-to-all-start.1) | async-done | bytes 393248 | tf_op jit(solution)/shard_map/all_to_all | solution.py:481
  37.6 2.2 shard_map.122
  39.9 1.6 shard_map.121
  41.5 3.7 %all-to-all-start = ((bf16[16,32,1024]{2,1,0:T(8,128)(2,1)}), bf16[16,32,1024]{2,1,0:T(8,128)(2,1)S(1)}, u32[]{:S(2)}, u32[]{:S(2)}) async-start(bf16[16,32,1024]{2,1,0:T(8,128)(2,1)} %shard_map.121), calls=%async_computation | async-start | bytes 2097152 | tf_op jit(solution)/shard_map/all_to_all | solution.py:491
  45.3 0.8 dynamic-slice_bitcast_fusion.1
  46.0 2.4 %collective-permute-start.5 = (bf16[128,1024]{1,0:T(8,128)(2,1)S(1)}, bf16[128,1024]{1,0:T(8,128)(2,1)S(1)}, u32[]{:S(2)}, u32[]{:S(2)}) collective-permute-start(bf16[128,1024]{1,0:T(8,128)(2,1)S(1)} %get-tuple-element.36), channel_id=1, source_target_pairs={{0,24},{8,0},{16,8},{24,16},{1,25},{9,1},{17,9},{25,17},{2,26},{10... | collective-permute-start | bytes 786440 | tf_op jit(solution)/shard_map/ppermute | solution.py:486
  48.5 1.7 collective-permute-start.4
  50.9 10.9 %collective-permute-done.5.d3 = bf16[128,1024]{1,0:T(8,128)(2,1)S(1)} collective-permute-done((bf16[128,1024]{1,0:T(8,128)(2,1)S(1)}, bf16[128,1024]{1,0:T(8,128)(2,1)S(1)}, u32[]{:S(2)}, u32[]{:S(2)}) %collective-permute-start.5) | collective-permute-done | bytes 262176 | tf_op jit(solution)/shard_map/ppermute | solution.py:486
  61.8 4.5 %collective-permute-done.3.d1 = bf16[128,1024]{1,0:T(8,128)(2,1)S(1)} collective-permute-done((bf16[128,1024]{1,0:T(8,128)(2,1)S(1)}, bf16[128,1024]{1,0:T(8,128)(2,1)S(1)}, u32[]{:S(2)}, u32[]{:S(2)}) %collective-permute-start.3) | collective-permute-done | bytes 262176 | tf_op jit(solution)/shard_map/ppermute | solution.py:486
  66.3 2.0 collective-permute-done.4.d2
  69.3 31.0 %shard_map.123 = (bf16[4,128,1024]{2,1,0:T(8,128)(2,1)}, bf16[128,32,128]{2,1,0:T(8,128)(2,1)}, bf16[2,288,128]{2,1,0:T(8,128)(2,1)}) custom-call(s32[32]{0:T(128)} %concatenate.7.scalar_ref, bf16[16,32,1024]{2,1,0:T(8,128)(2,1)} %copy-done.8, bf16[16,32,384]{2,1,0:T(8,128)(2,1)} %copy-done.5, bf16[128,1024]{1,0:T(8,128)(2,1)} %get-tuple-element.38.d0, ...), custom_call_target="tpu_custom_call" | custom-call | flops 21474836480 | bytes 8388608 | tf_op jit(solution)/shard_map/pallas_call | solution.py:304
  100.3 21.9 %all-to-all-start.2 = ((bf16[128,32,128]{2,1,0:T(8,128)(2,1)}), bf16[128,32,128]{2,1,0:T(8,128)(2,1)}, u32[]{:S(2)}, u32[]{:S(2)}) async-start(bf16[128,32,128]{2,1,0:T(8,128)(2,1)} %get-tuple-element.19), calls=%async_computation.2 | async-start | bytes 2097152 | tf_op jit(solution)/shard_map/all_to_all | solution.py:503
  122.3 1.1 dynamic-slice_bitcast_fusion
  123.4 1.1 collective-permute-start.9
  124.5 0.8 slice_bitcast_fusion
  126.1 2.4 %collective-permute-start.7 = (bf16[128,1024]{1,0:T(8,128)(2,1)S(1)}, bf16[128,1024]{1,0:T(8,128)(2,1)S(1)}, u32[]{:S(2)}, u32[]{:S(2)}) collective-permute-start(bf16[128,1024]{1,0:T(8,128)(2,1)S(1)} %get-tuple-element.33), channel_id=1, source_target_pairs={{0,16},{8,24},{16,0},{24,8},{1,17},{9,25},{17,1},{25,9},{2,18},{10... | collective-permute-start | bytes 786440 | tf_op jit(solution)/shard_map/ppermute | solution.py:499
  128.5 1.1 collective-permute-start.6
  129.7 1.3 collective-permute-start.11
  131.0 10.3 %all-to-all-done.2.got_ref = bf16[128,32,128]{2,1,0:T(8,128)(2,1)} async-done(((bf16[128,32,128]{2,1,0:T(8,128)(2,1)}), bf16[128,32,128]{2,1,0:T(8,128)(2,1)}, u32[]{:S(2)}, u32[]{:S(2)}) %all-to-all-start.2) | async-done | bytes 1048608 | tf_op jit(solution)/shard_map/all_to_all | solution.py:503
  141.3 2.0 shard_map.124.low_ref
  143.3 4.4 %collective-permute-done.7.p2 = bf16[128,1024]{1,0:T(8,128)(2,1)S(1)} collective-permute-done((bf16[128,1024]{1,0:T(8,128)(2,1)S(1)}, bf16[128,1024]{1,0:T(8,128)(2,1)S(1)}, u32[]{:S(2)}, u32[]{:S(2)}) %collective-permute-start.7) | collective-permute-done | bytes 262176 | tf_op jit(solution)/shard_map/ppermute | solution.py:499
  150.6 5.0 %shard_map.126 = bf16[64,88,128]{2,1,0:T(8,128)(2,1)} custom-call(s32[2]{0:T(128)} %pad_add_fusion.1.place_ref, bf16[128,8192]{1,0:T(8,128)(2,1)} %bitcast.38, bf16[128,4096]{1,0:T(8,128)(2,1)} %copy-done.6, bf16[128,128]{1,0:T(8,128)(2,1)} %shard_map.124.low_ref, bf16[128,128]{1,0:T(8,128)(2,1)} %copy-done.16, ...), custom_call_target="tpu_custom_call" | custom-call | flops 268435456 | bytes 4194304 | tf_op jit(solution)/shard_map/pallas_call | solution.py:380
  155.7 30.7 %all_to_all.25 = bf16[64,88,128]{2,1,0:T(8,128)(2,1)S(1)} all-to-all(bf16[64,88,128]{2,1,0:T(8,128)(2,1)} %shard_map.126), channel_id=1, replica_groups=mesh['dp'=4,'y'=4,'x'=4,'core'=2] {'dp','y','x'}, dimensions={0} | all-to-all | bytes 2883584 | tf_op jit(solution)/shard_map/all_to_all | solution.py:507
  186.8 27.1 %all_to_all.26.own_ref = bf16[64,88,128]{2,1,0:T(8,128)(2,1)S(1)} all-to-all(bf16[64,88,128]{2,1,0:T(8,128)(2,1)S(1)} %broadcast_in_dim.5), channel_id=1, replica_groups=mesh['dp'=4,'y'=4,'x'=4,'core'=2] {'dp','y','x'}, dimensions={0} | all-to-all | bytes 2883584 | tf_op jit(solution)/shard_map/all_to_all | solution.py:509
  213.9 2.5 %collective-permute-start.12 = (bf16[64,88,128]{2,1,0:T(8,128)(2,1)S(1)}, bf16[64,88,128]{2,1,0:T(8,128)(2,1)S(1)}, u32[]{:S(2)}, u32[]{:S(2)}) collective-permute-start(bf16[64,88,128]{2,1,0:T(8,128)(2,1)S(1)} %all_to_all.26.own_ref), channel_id=1, source_target_pairs={{0,1},{1,0},{2,3},{3,2},{4,5},{5,4},{6,7},{7,6},{8,9},{9,8},{10,11... | collective-permute-start | bytes 4325384 | tf_op jit(solution)/shard_map/ppermute | solution.py:510
  216.4 2.2 shard_map.125
  219.2 3.1 %shard_map.127 = (f32[8192,128]{1,0:T(8,128)}, f32[64,4096]{1,0:T(8,128)}, f32[64,512]{1,0:T(8,128)}) custom-call(s32[2]{0:T(128)S(1)} %copy-done.2, bf16[64,88,128]{2,1,0:T(8,128)(2,1)S(1)} %all_to_all.26.own_ref, bf16[64,88,128]{2,1,0:T(8,128)(2,1)S(1)} %collective-permute-done.12.other_ref), custom_call_target="tpu_custom_call" | custom-call | flops 1048576 | bytes 8388608 | tf_op jit(solution)/shard_map/pallas_call | solution.py:415
  (79 shorter events, 11.5 us)
Async XLA Ops:
  7.2 43.0 %copy-start = (bf16[64,4096]{1,0:T(8,128)(2,1)S(1)}, bf16[64,4096]{1,0:T(8,128)(2,1)}, u32[]{:S(2)}) copy-start(bf16[64,4096]{1,0:T(8,128)(2,1)} %param.13) | copy-start | bytes 1572868
  8.7 8.4 %copy-start.17 = (s32[4]{0:T(128)}, s32[4]{0:T(128)S(1)}, u32[]{:S(2)}) copy-start(s32[4]{0:T(128)S(1)} %fusion.1.outgoing_ref) | copy-start | bytes 52
  17.1 22.8 %copy-start.1 = (bf16[1,128,4096]{2,1,0:T(8,128)(2,1)S(1)}, bf16[1,128,4096]{2,1,0:T(8,128)(2,1)}, u32[]{:S(2)}) copy-start(bf16[1,128,4096]{2,1,0:T(8,128)(2,1)} %param.10) | copy-start | bytes 3145732
  17.1 22.8 %copy-start.3 = (s32[4]{0:T(128)S(1)}, s32[4]{0:T(128)}, u32[]{:S(2)}) copy-start(s32[4]{0:T(128)} %select_reduce_fusion.1.order_ref) | copy-start | bytes 52
  17.1 12.9 %collective-permute-start.2 = (s32[2,128]{1,0:T(2,128)S(1)}, s32[2,128]{1,0:T(2,128)S(1)}, u32[]{:S(2)}, u32[]{:S(2)}) collective-permute-start(s32[2,128]{1,0:T(2,128)S(1)} %add_bitcast_fusion), channel_id=1, source_target_pairs={{0,24},{8,0},{16,8},{24,16},{1,25},{9,1},{17,9},{25,17},{2,26},{10... | collective-permute-start | bytes 3080 | tf_op jit(solution)/shard_map/ppermute | solution.py:473
  20.7 9.3 %collective-permute-start.1 = (s32[2,128]{1,0:T(2,128)S(1)}, s32[2,128]{1,0:T(2,128)S(1)}, u32[]{:S(2)}, u32[]{:S(2)}) collective-permute-start(s32[2,128]{1,0:T(2,128)S(1)} %add_bitcast_fusion), channel_id=1, source_target_pairs={{0,16},{8,24},{16,0},{24,8},{1,17},{9,25},{17,1},{25,9},{2,18},{10... | collective-permute-start | bytes 3080 | tf_op jit(solution)/shard_map/ppermute | solution.py:473
  21.1 9.0 %collective-permute-start = (s32[2,128]{1,0:T(2,128)S(1)}, s32[2,128]{1,0:T(2,128)S(1)}, u32[]{:S(2)}, u32[]{:S(2)}) collective-permute-start(s32[2,128]{1,0:T(2,128)S(1)} %add_bitcast_fusion), channel_id=1, source_target_pairs={{0,8},{8,16},{16,24},{24,0},{1,9},{9,17},{17,25},{25,1},{2,10},{10... | collective-permute-start | bytes 3080 | tf_op jit(solution)/shard_map/ppermute | solution.py:473
  21.8 15.1 %all-to-all-start.1 = ((bf16[16,32,384]{2,1,0:T(8,128)(2,1)}), bf16[16,32,384]{2,1,0:T(8,128)(2,1)S(1)}, u32[]{:S(2)}, u32[]{:S(2)}) async-start(bf16[16,32,384]{2,1,0:T(8,128)(2,1)} %shard_map.120), calls=%async_computation.1 | async-start | bytes 786432 | tf_op jit(solution)/shard_map/all_to_all | solution.py:481
  28.6 39.7 %all-gather.3.cloned.1.call-start = ((), (), s32[]{:S(2)}) async-start(), calls=%async_computation.5 | async-start | bytes 3538944 | tf_op jit(solution)/shard_map/all_gather | solution.py:490
  30.1 6.8 %copy-start.15 = (s32[4,2,128]{2,1,0:T(2,128)}, s32[4,2,128]{2,1,0:T(2,128)S(1)}, u32[]{:S(2)}) copy-start(s32[4,2,128]{2,1,0:T(2,128)S(1)} %pad_add_fusion.notes_ref) | copy-start | bytes 12292
  39.9 5.4 %copy-start.7 = (bf16[1,128,4096]{2,1,0:T(8,128)(2,1)S(1)}, bf16[1,128,4096]{2,1,0:T(8,128)(2,1)}, u32[]{:S(2)}) copy-start(bf16[1,128,4096]{2,1,0:T(8,128)(2,1)} %param.17) | copy-start | bytes 3145732
  41.5 26.8 %all-to-all-start = ((bf16[16,32,1024]{2,1,0:T(8,128)(2,1)}), bf16[16,32,1024]{2,1,0:T(8,128)(2,1)S(1)}, u32[]{:S(2)}, u32[]{:S(2)}) async-start(bf16[16,32,1024]{2,1,0:T(8,128)(2,1)} %shard_map.121), calls=%async_computation | async-start | bytes 2097152 | tf_op jit(solution)/shard_map/all_to_all | solution.py:491
  46.0 15.7 %collective-permute-start.5 = (bf16[128,1024]{1,0:T(8,128)(2,1)S(1)}, bf16[128,1024]{1,0:T(8,128)(2,1)S(1)}, u32[]{:S(2)}, u32[]{:S(2)}) collective-permute-start(bf16[128,1024]{1,0:T(8,128)(2,1)S(1)} %get-tuple-element.36), channel_id=1, source_target_pairs={{0,24},{8,0},{16,8},{24,16},{1,25},{9,1},{17,9},{25,17},{2,26},{10... | collective-permute-start | bytes 786440 | tf_op jit(solution)/shard_map/ppermute | solution.py:486
  48.5 17.8 %collective-permute-start.3 = (bf16[128,1024]{1,0:T(8,128)(2,1)S(1)}, bf16[128,1024]{1,0:T(8,128)(2,1)S(1)}, u32[]{:S(2)}, u32[]{:S(2)}) collective-permute-start(bf16[128,1024]{1,0:T(8,128)(2,1)S(1)} %get-tuple-element.37), channel_id=1, source_target_pairs={{0,8},{8,16},{16,24},{24,0},{1,9},{9,17},{17,25},{25,1},{2,10},{10... | collective-permute-start | bytes 786440 | tf_op jit(solution)/shard_map/ppermute | solution.py:486
  48.5 19.8 %collective-permute-start.4 = (bf16[128,1024]{1,0:T(8,128)(2,1)S(1)}, bf16[128,1024]{1,0:T(8,128)(2,1)S(1)}, u32[]{:S(2)}, u32[]{:S(2)}) collective-permute-start(bf16[128,1024]{1,0:T(8,128)(2,1)S(1)} %get-tuple-element.39), channel_id=1, source_target_pairs={{0,16},{8,24},{16,0},{24,8},{1,17},{9,25},{17,1},{25,9},{2,18},{10... | collective-permute-start | bytes 786440 | tf_op jit(solution)/shard_map/ppermute | solution.py:486
  61.8 6.5 %copy-start.18 = (bf16[128,1024]{1,0:T(8,128)(2,1)}, bf16[128,1024]{1,0:T(8,128)(2,1)S(1)}, u32[]{:S(2)}) copy-start(bf16[128,1024]{1,0:T(8,128)(2,1)S(1)} %collective-permute-done.5.d3) | copy-start | bytes 786436
  66.3 2.1 copy-start.19
  100.3 22.0 %copy-start.4 = (bf16[1,128,8192]{2,1,0:T(8,128)(2,1)S(1)}, bf16[1,128,8192]{2,1,0:T(8,128)(2,1)}, u32[]{:S(2)}) copy-start(bf16[1,128,8192]{2,1,0:T(8,128)(2,1)} %param.9) | copy-start | bytes 6291460
  100.3 40.9 %all-to-all-start.2 = ((bf16[128,32,128]{2,1,0:T(8,128)(2,1)}), bf16[128,32,128]{2,1,0:T(8,128)(2,1)}, u32[]{:S(2)}, u32[]{:S(2)}) async-start(bf16[128,32,128]{2,1,0:T(8,128)(2,1)} %get-tuple-element.19), calls=%async_computation.2 | async-start | bytes 2097152 | tf_op jit(solution)/shard_map/all_to_all | solution.py:503
  122.3 2.2 copy-start.9
  122.3 7.4 %copy-start.10 = (bf16[2,288,128]{2,1,0:T(8,128)(2,1)S(1)}, bf16[2,288,128]{2,1,0:T(8,128)(2,1)}, u32[]{:S(2)}) copy-start(bf16[2,288,128]{2,1,0:T(8,128)(2,1)} %get-tuple-element.26.up_ref) | copy-start | bytes 442372
  123.4 25.7 %collective-permute-start.9 = (bf16[128,4096]{1,0:T(8,128)(2,1)}, bf16[128,4096]{1,0:T(8,128)(2,1)S(1)}, u32[]{:S(2)}, u32[]{:S(2)}) collective-permute-start(bf16[128,4096]{1,0:T(8,128)(2,1)} %dynamic-slice_bitcast_fusion), channel_id=1, source_target_pairs={{0,1},{1,0},{2,3},{3,2},{4,5},{5,4},{6,7},{7,6},{8,9},{9,8},{10,11... | collective-permute-start | bytes 3145736 | tf_op jit(solution)/shard_map/ppermute | solution.py:494
  125.3 18.0 %collective-permute-start.8 = (bf16[128,1024]{1,0:T(8,128)(2,1)S(1)}, bf16[128,1024]{1,0:T(8,128)(2,1)S(1)}, u32[]{:S(2)}, u32[]{:S(2)}) collective-permute-start(bf16[128,1024]{1,0:T(8,128)(2,1)S(1)} %get-tuple-element.32), channel_id=1, source_target_pairs={{0,8},{8,16},{16,24},{24,0},{1,9},{9,17},{17,25},{25,1},{2,10},{10... | collective-permute-start | bytes 786440 | tf_op jit(solution)/shard_map/ppermute | solution.py:499
  126.1 21.6 %collective-permute-start.7 = (bf16[128,1024]{1,0:T(8,128)(2,1)S(1)}, bf16[128,1024]{1,0:T(8,128)(2,1)S(1)}, u32[]{:S(2)}, u32[]{:S(2)}) collective-permute-start(bf16[128,1024]{1,0:T(8,128)(2,1)S(1)} %get-tuple-element.33), channel_id=1, source_target_pairs={{0,16},{8,24},{16,0},{24,8},{1,17},{9,25},{17,1},{25,9},{2,18},{10... | collective-permute-start | bytes 786440 | tf_op jit(solution)/shard_map/ppermute | solution.py:499
  128.5 19.1 %collective-permute-start.6 = (bf16[128,1024]{1,0:T(8,128)(2,1)S(1)}, bf16[128,1024]{1,0:T(8,128)(2,1)S(1)}, u32[]{:S(2)}, u32[]{:S(2)}) collective-permute-start(bf16[128,1024]{1,0:T(8,128)(2,1)S(1)} %get-tuple-element.34), channel_id=1, source_target_pairs={{0,24},{8,0},{16,8},{24,16},{1,25},{9,1},{17,9},{25,17},{2,26},{10... | collective-permute-start | bytes 786440 | tf_op jit(solution)/shard_map/ppermute | solution.py:499
  129.7 19.4 %collective-permute-start.11 = (bf16[288,128]{1,0:T(8,128)(2,1)S(1)}, bf16[288,128]{1,0:T(8,128)(2,1)S(1)}, u32[]{:S(2)}, u32[]{:S(2)}) collective-permute-start(bf16[288,128]{1,0:T(8,128)(2,1)S(1)} %dynamic-slice_bitcast_fusion.5), channel_id=1, source_target_pairs={{0,1},{1,0},{2,3},{3,2},{4,5},{5,4},{6,7},{7,6},{8,9},{9,8},{10,11... | collective-permute-start | bytes 221192 | tf_op jit(solution)/shard_map/ppermute | solution.py:500
  143.3 6.2 %copy-start.11 = (bf16[128,1024]{1,0:T(8,128)(2,1)}, bf16[128,1024]{1,0:T(8,128)(2,1)S(1)}, u32[]{:S(2)}) copy-start(bf16[128,1024]{1,0:T(8,128)(2,1)S(1)} %collective-permute-done.8.p3) | copy-start | bytes 786436
  147.7 1.8 copy-start.12
  147.7 39.1 %copy-start.13 = (bf16[128,1024]{1,0:T(8,128)(2,1)}, bf16[128,1024]{1,0:T(8,128)(2,1)S(1)}, u32[]{:S(2)}) copy-start(bf16[128,1024]{1,0:T(8,128)(2,1)S(1)} %collective-permute-done.6.p1) | copy-start | bytes 786436
  147.7 1.8 collective-permute-start.10
  186.8 32.4 %copy-start.2 = (s32[2]{0:T(128)S(1)}, s32[2]{0:T(128)}, u32[]{:S(2)}) copy-start(s32[2]{0:T(128)} %pad_add_fusion.1.place_ref) | copy-start | bytes 28
  213.9 5.3 %collective-permute-start.12 = (bf16[64,88,128]{2,1,0:T(8,128)(2,1)S(1)}, bf16[64,88,128]{2,1,0:T(8,128)(2,1)S(1)}, u32[]{:S(2)}, u32[]{:S(2)}) collective-permute-start(bf16[64,88,128]{2,1,0:T(8,128)(2,1)S(1)} %all_to_all.26.own_ref), channel_id=1, source_target_pairs={{0,1},{1,0},{2,3},{3,2},{4,5},{5,4},{6,7},{7,6},{8,9},{9,8},{10,11... | collective-permute-start | bytes 4325384 | tf_op jit(solution)/shard_map/ppermute | solution.py:510
  (6 other events, 5.0 us)
Sparse Core Ops, SparseCore 0:
  40.0 27.8 all-gather.2

commit v3 on v2

v3 whole, which is shorter than its diff:
```python
import functools
import math

import jax
import jax.numpy as jnp
from jax import lax
from jax.experimental import pallas as pl
from jax.experimental.pallas import tpu as pltpu
from jax.sharding import Mesh
from jax.sharding import PartitionSpec as P

HEAD = 128
BLOCK = 128
QUARTER = 32
KEY_CHUNK = 512
HALF = KEY_CHUNK // 2
PAD = KEY_CHUNK - BLOCK
ROWS_STEP = 8 * BLOCK
SCALE = 0.5
MASKED = -1e30
INVERSE = 1.0 / math.sqrt(HEAD)
LOG2E = 1.4426950408889634
BF = jnp.bfloat16
F32 = jnp.float32
NT = (((1,), (1,)), ((), ()))
TN = (((0,), (0,)), ((), ()))
VMEM = pltpu.VMEM
CHIP = ("dp", "y", "x")
ROWS = ("dp", "y")
SHARD = 88


def turn(d):
    return [(y, (y + d) % 4) for y in range(4)]


def whole():
    return pl.BlockSpec(memory_space=pltpu.VMEM)


def scalars():
    return pl.BlockSpec(memory_space=pltpu.SMEM)


def params(mib):
    return pltpu.CompilerParams(vmem_limit_bytes=mib << 20)


def quarter_rows(route_ref, r):
    me = lax.axis_index("dp")
    quarter = sum(jnp.where(route_ref[0, me, k] == r, k, 0) for k in range(1, 4))
    return pl.ds(pl.multiple_of(quarter * QUARTER, QUARTER), QUARTER)


def front_kernel(route_ref, x_ref, a_ref, kv_ref, resp_ref, out_ref, note_ref, acc_ref, low_ref):
    step = pl.program_id(0)

    @pl.when(step == 0)
    def _():
        acc_ref[...] = jnp.zeros_like(acc_ref)

    acc_ref[...] += jnp.dot(x_ref[...], a_ref[...], preferred_element_type=F32)

    @pl.when(step == pl.num_programs(0) - 1)
    def _():
        lane = lax.broadcasted_iota(jnp.int32, (1, 128), 1)
        note = jnp.zeros((1, 128), jnp.int32)
        for g in range(4):
            for k in range(4):
                note = jnp.where(lane == g * 4 + k, route_ref[0, g, k], note)
        note_ref[0:1, :] = resp_ref[...]
        note_ref[1:2, :] = note
        low_ref[...] = acc_ref[...].astype(BF)
        for r in range(4):
            rows = quarter_rows(route_ref, r)
            low = low_ref[rows, :]
            for y in range(4):
                out_ref[r * 4 + y, :, 0:128] = kv_ref[rows, y * 128 : y * 128 + 128]
                out_ref[r * 4 + y, :, 128:256] = kv_ref[rows, 512 + y * 128 : 640 + y * 128]
                out_ref[r * 4 + y, :, 256:384] = low


def front(route, x, a, kv, resp):
    steps = 2
    part = 8192 // steps
    return pl.pallas_call(
        front_kernel,
        out_shape=(
            jax.ShapeDtypeStruct((16, QUARTER, 384), BF),
            jax.ShapeDtypeStruct((2, 128), jnp.int32),
        ),
        grid=(steps,),
        in_specs=[
            scalars(),
            pl.BlockSpec((BLOCK, part), lambda i: (0, i)),
            pl.BlockSpec((part, 128), lambda i: (i, 0)),
            pl.BlockSpec((BLOCK, 1024), lambda i: (0, 0)),
            pl.BlockSpec((1, BLOCK), lambda i: (0, 0)),
        ],
        out_specs=(
            pl.BlockSpec((16, QUARTER, 384), lambda i: (0, 0, 0)),
            pl.BlockSpec((2, 128), lambda i: (0, 0)),
        ),
        scratch_shapes=[VMEM((BLOCK, 128), F32), VMEM((BLOCK, 128), BF)],
        compiler_params=params(58),
        cost_estimate=pl.CostEstimate(flops=2 * 128 * 8192 * 128, bytes_accessed=5 << 20, transcendentals=0),
    )(route, x, a, kv, resp)


def query_chunks_kernel(route_ref, q_ref, out_ref, sem):
    copies = []
    for r in range(4):
        rows = quarter_rows(route_ref, r)
        for y in range(4):
            copies.append(
                pltpu.make_async_copy(
                    q_ref.at[rows, pl.ds(y * 1024, 1024)], out_ref.at[r * 4 + y], sem.at[r * 4 + y]
                )
            )
    for copy in copies:
        copy.start()
    for copy in copies:
        copy.wait()


def query_chunks(route, q):
    return pl.pallas_call(
        query_chunks_kernel,
        out_shape=jax.ShapeDtypeStruct((16, QUARTER, 1024), BF),
        in_specs=[scalars(), pl.BlockSpec(memory_space=pl.ANY)],
        out_specs=pl.BlockSpec(memory_space=pl.ANY),
        scratch_shapes=[pltpu.SemaphoreType.DMA((16,))],
        compiler_params=params(48),
        cost_estimate=pl.CostEstimate(flops=0, bytes_accessed=2 << 20, transcendentals=0),
    )(route, q)


def pack_kernel(scalar_ref, got_ref, notes_ref, wv_ref, out_ref):
    lane = lax.broadcasted_iota(jnp.int32, (1, 64), 1)
    for i in range(4):
        y = scalar_ref[28 + i]
        extra = jnp.where(lane == 0, 1.0, 0.0)
        for k in range(4):
            source = (scalar_ref[i * 4 + k] // 4).astype(F32)
            extra = jnp.where(lane == 1 + k, source, extra)
        for v in range(1, 4):
            below = jnp.sum(jnp.where(notes_ref[i, 0:1, :] < v, 1.0, 0.0), axis=1, keepdims=True)
            extra = jnp.where(lane == 4 + v, below, extra)
        rows = jnp.concatenate([got_ref[scalar_ref[i * 4 + k]] for k in range(4)], axis=0)
        low_v = rows[:, 320:384]
        value = rows[:, 128:256].astype(F32) + SCALE * jnp.dot(
            low_v, wv_ref[...], preferred_element_type=F32
        )
        extra = jnp.broadcast_to(extra, (BLOCK, 64))
        out_ref[y, :, 0:128] = rows[:, 0:128]
        out_ref[y, :, 128:256] = value.astype(BF)
        out_ref[y, :, 256:384] = jnp.concatenate([low_v.astype(F32), extra], axis=1).astype(BF)


def pack(scalar, got, notes, wv):
    return pl.pallas_call(
        pack_kernel,
        out_shape=jax.ShapeDtypeStruct((4, BLOCK, 384), BF),
        in_specs=[scalars(), whole(), whole(), whole()],
        out_specs=whole(),
        cost_estimate=pl.CostEstimate(flops=1 << 23, bytes_accessed=1 << 20, transcendentals=0),
    )(scalar, got, notes, wv)


def attention_kernel(
    scalar_ref, q_ref, got_ref, d0, d1, d2, d3, notes_ref, kv_ref, wv_ref, wq_ref,
    out_ref, send_ref, send_other_ref, up_ref, up_other_ref,
    kv_s, s_s, w_s, t_s, m_s, acc_s, dq_s, dout_s, lg_s, qup_s, vup_s, send_s, up_s, below_s, sem,
):
    copies = []
    for c in range(32):
        copies.append(
            pltpu.make_async_copy(
                kv_ref.at[c % 8, c // 8], kv_s.at[pl.ds(PAD + c * BLOCK, BLOCK), :], sem.at[c]
            )
        )
    for copy in copies:
        copy.start()
    kv_s[0:PAD, :] = jnp.zeros((PAD, 384), BF)
    t_s[...] = jnp.zeros_like(t_s)
    qup_s[...] = jnp.zeros_like(qup_s)
    vup_s[...] = jnp.zeros_like(vup_s)
    for i, d in enumerate((d0, d1, d2, d3)):
        for h in range(8):
            dout_s[i, h * BLOCK : (h + 1) * BLOCK, :] = d[:, h * HEAD : (h + 1) * HEAD]
    for copy in copies:
        copy.wait()
    counts = kv_s[PAD : PAD + 16, 256:384].astype(F32)
    for c in range(1, 32):
        counts = counts + kv_s[PAD + c * BLOCK : PAD + c * BLOCK + 16, 256:384].astype(F32)
    lane = lax.broadcasted_iota(jnp.int32, (1, 128), 1)
    below_s[0] = 0
    for v in range(1, 4):
        below_s[v] = jnp.sum(jnp.where(lane == 68 + v, counts[0:1, :], 0.0)).astype(jnp.int32)
    diagonal = lax.broadcasted_iota(jnp.int32, (BLOCK, BLOCK), 0) == lax.broadcasted_iota(
        jnp.int32, (BLOCK, BLOCK), 1
    )

    def turn_of(i, _):
        block = scalar_ref[16 + i]
        high = (block + 1) * BLOCK
        width = high - below_s[scalar_ref[20 + i]]
        steps = (width + HALF - 1) // KEY_CHUNK
        half = width > steps * KEY_CHUNK
        clean = jnp.maximum(jnp.minimum((high - below_s[scalar_ref[24 + i]]) // KEY_CHUNK, steps), 1)
        resp = notes_ref[i, 0:1, :]
        start = jnp.zeros((1, BLOCK), jnp.int32)
        for v in range(1, 4):
            start = jnp.where(resp == v, below_s[v], start)
        start = jnp.sum(jnp.where(diagonal, start.astype(F32), 0.0), axis=1, keepdims=True).astype(jnp.int32)
        start = jnp.concatenate([start] * 8, axis=0)
        row = block * BLOCK + lax.broadcasted_iota(jnp.int32, (BLOCK, 1), 0)
        row = jnp.concatenate([row] * 8, axis=0)

        chunks = [scalar_ref[i * 4 + k] for k in range(4)]
        low = jnp.concatenate([got_ref[c, :, 256:384] for c in chunks], axis=0)
        q_in = jnp.concatenate([q_ref[c] for c in chunks], axis=0).astype(F32)
        query = (
            q_in + SCALE * jnp.dot(low[:, 0:64], wq_ref[...], preferred_element_type=F32)
        ).astype(BF)
        query = jnp.concatenate([query[:, h * HEAD : (h + 1) * HEAD] for h in range(8)], axis=0)
        dout = dout_s[i]

        def place(t, size):
            return pl.multiple_of(PAD + high - KEY_CHUNK * t - size, BLOCK)

        m_s[...] = jnp.full_like(m_s, MASKED)

        def scores(t, size, masked):
            at = place(t, size)
            s = lax.dot_general(query, kv_s[pl.ds(at, size), 0:128], NT, preferred_element_type=F32)
            if masked:
                key = at - PAD + lax.broadcasted_iota(jnp.int32, (1, size), 1)
                s = jnp.where((key >= start) & (key <= row), s, MASKED)
            s_s[t, :, 0:size] = s
            top = m_s[...]
            for c in range(size // 128):
                top = jnp.maximum(top, s[:, c * 128 : (c + 1) * 128])
            m_s[...] = top

        def clean_scores(t, _):
            scores(t, KEY_CHUNK, False)
            return 0

        def masked_scores(t, _):
            scores(t, KEY_CHUNK, True)
            return 0

        lax.fori_loop(0, jnp.minimum(steps, 1), masked_scores, 0)
        lax.fori_loop(1, clean, clean_scores, 0)
        lax.fori_loop(clean, steps, masked_scores, 0)

        @pl.when(half)
        def _():
            scores(steps, HALF, True)

        top = jnp.max(m_s[...], axis=1, keepdims=True)
        acc_s[...] = jnp.zeros_like(acc_s)

        def forward(t, size):
            w = jnp.exp2((s_s[t, :, 0:size] - top) * (INVERSE * LOG2E)).astype(BF)
            w_s[t, :, 0:size] = w
            acc_s[...] += jnp.dot(w, kv_s[pl.ds(place(t, size), size), 128:384], preferred_element_type=F32)

        def forward_step(t, _):
            forward(t, KEY_CHUNK)
            return 0

        lax.fori_loop(0, steps, forward_step, 0)

        @pl.when(half)
        def _():
            forward(steps, HALF)

        over = 1.0 / acc_s[:, 192:193]
        out = (acc_s[:, 0:128] * over).astype(BF)
        for h in range(8):
            out_ref[i, :, h * HEAD : (h + 1) * HEAD] = out[h * BLOCK : (h + 1) * BLOCK, :]
        wide = dout.astype(F32)
        delta = jnp.sum(wide * out.astype(F32), axis=1, keepdims=True) * over
        scaled = (wide * over).astype(BF)
        g = lax.dot_general(wv_ref[...], scaled, NT, preferred_element_type=F32).astype(BF)
        weighted_low = (acc_s[:, 128:256] * over).astype(BF)
        vup_s[...] += lax.dot_general(weighted_low, dout, TN, preferred_element_type=F32)
        dq_s[...] = jnp.zeros_like(dq_s)

        def backward(t, size):
            at = place(t, size)
            w = w_s[t, :, 0:size]
            dp = lax.dot_general(scaled, kv_s[pl.ds(at, size), 128:256], NT, preferred_element_type=F32)
            ds = (w.astype(F32) * (dp - delta)).astype(BF)
            dq_s[...] += jnp.dot(ds, kv_s[pl.ds(at, size), 0:128], preferred_element_type=F32)
            t_s[:, pl.ds(at, size)] += jnp.dot(g, w, preferred_element_type=F32)

        def backward_step(t, _):
            backward(t, KEY_CHUNK)
            return 0

        lax.fori_loop(0, steps, backward_step, 0)

        @pl.when(half)
        def _():
            backward(steps, HALF)

        dq = (dq_s[...] * INVERSE).astype(BF)
        low_t = jnp.transpose(low.astype(F32))[0:64, :].astype(BF)
        lg = jnp.zeros((64, BLOCK), F32)
        for h in range(8):
            dq_h = dq[h * BLOCK : (h + 1) * BLOCK, :]
            lg = lg + lax.dot_general(
                wq_ref[:, h * HEAD : (h + 1) * HEAD], dq_h, NT, preferred_element_type=F32
            )
            qup_s[h] += jnp.dot(low_t, dq_h, preferred_element_type=F32)
        lg_s[i] = lg
        return 0

    lax.fori_loop(0, 4, turn_of, 0)

    token_row = lax.broadcasted_iota(jnp.int32, (1, BLOCK), 1)
    token = lax.broadcasted_iota(jnp.int32, (BLOCK, BLOCK), 1)
    slot = lax.broadcasted_iota(jnp.int32, (BLOCK, BLOCK), 0)
    within = token % QUARTER == slot % QUARTER
    wanted = (slot // QUARTER).astype(F32)
    for c in range(32):
        at = (scalar_ref[28] - c // 8 + 4) % 4
        own = jnp.where(scalar_ref[16 + at] == c, 1.0, 0.0)
        both = jnp.concatenate([lg_s[at] * own, t_s[:, PAD + c * BLOCK : PAD + (c + 1) * BLOCK]], axis=0)
        both = (both * SCALE).astype(BF)
        note = kv_s[PAD + c * BLOCK : PAD + c * BLOCK + 16, 256:384].astype(F32)[0:1, :]
        source = note[:, 65:66]
        for k in range(1, 4):
            source = jnp.where(token_row // QUARTER == k, note[:, 65 + k : 66 + k], source)
        pick = jnp.where(within & (source == wanted), 1.0, 0.0).astype(BF)
        sent = lax.dot_general(pick, both, NT, preferred_element_type=F32).astype(BF)
        for g in range(4):
            send_s[c % 2, g * 16 + c // 2] = sent[g * QUARTER : (g + 1) * QUARTER, :]
    for c in range(2):
        for h in range(4):
            up_s[c, h * 64 : (h + 1) * 64, :] = (qup_s[c * 4 + h] * SCALE).astype(BF)
        up_s[c, 256:288, :] = (vup_s[c * 32 : (c + 1) * 32, :] * SCALE).astype(BF)
    core = lax.axis_index("core")
    send_ref[...] = send_s[core]
    send_other_ref[...] = send_s[1 - core]
    up_ref[...] = up_s[core]
    up_other_ref[...] = up_s[1 - core]


def attention(scalar, q, got, dout, notes, kv, wv, wq):
    chunks = 4096 // KEY_CHUNK
    return pl.pallas_call(
        attention_kernel,
        out_shape=(
            jax.ShapeDtypeStruct((4, BLOCK, 1024), BF),
            jax.ShapeDtypeStruct((64, QUARTER, 128), BF),
            jax.ShapeDtypeStruct((64, QUARTER, 128), BF),
            jax.ShapeDtypeStruct((288, 128), BF),
            jax.ShapeDtypeStruct((288, 128), BF),
        ),
        in_specs=[scalars()]
        + [whole()] * 7
        + [pl.BlockSpec(memory_space=pl.ANY), whole(), whole()],
        out_specs=(whole(),) * 5,
        scratch_shapes=[
            VMEM((PAD + 4096, 384), BF),
            VMEM((chunks, ROWS_STEP, KEY_CHUNK), F32),
            VMEM((chunks, ROWS_STEP, KEY_CHUNK), BF),
            VMEM((64, PAD + 4096), F32),
            VMEM((ROWS_STEP, 128), F32),
            VMEM((ROWS_STEP, 256), F32),
            VMEM((ROWS_STEP, 128), F32),
            VMEM((4, ROWS_STEP, 128), BF),
            VMEM((4, 64, BLOCK), F32),
            VMEM((8, 64, 128), F32),
            VMEM((128, 128), F32),
            VMEM((2, 64, QUARTER, 128), BF),
            VMEM((2, 288, 128), BF),
            pltpu.SMEM((4,), jnp.int32),
            pltpu.SemaphoreType.DMA((32,)),
        ],
        compiler_params=params(56),
        cost_estimate=pl.CostEstimate(flops=20 << 30, bytes_accessed=8 << 20, transcendentals=8 << 20),
    )(scalar, q, got, *dout, notes, kv, wv, wq)


def low_back_kernel(route_ref, got_ref, low_ref, sum_ref):
    me = lax.axis_index("dp")
    for r in range(4):
        total = got_ref[r * 16].astype(F32)
        for c in range(1, 16):
            total = total + got_ref[r * 16 + c].astype(F32)
        sum_ref[r] = total
    for k in range(4):
        low_ref[k * QUARTER : (k + 1) * QUARTER, :] = sum_ref[route_ref[0, me, k]].astype(BF)


def low_back_of(route, got):
    return pl.pallas_call(
        low_back_kernel,
        out_shape=jax.ShapeDtypeStruct((BLOCK, 128), BF),
        in_specs=[scalars(), whole()],
        out_specs=whole(),
        scratch_shapes=[VMEM((4, QUARTER, 128), F32)],
        cost_estimate=pl.CostEstimate(flops=1 << 19, bytes_accessed=1 << 20, transcendentals=0),
    )(route, got)


def grad_kernel(x_ref, other_ref, low_ref, low_other_ref, up_ref, up_other_ref, out_ref, own_s, sem):
    half = pl.ds(pl.multiple_of(lax.axis_index("core") * 4096, 4096), 4096)
    copy = pltpu.make_async_copy(x_ref.at[:, half], own_s, sem)
    copy.start()
    my_y = lax.axis_index("y")
    low = jnp.concatenate([low_ref[...], low_other_ref[...]], axis=0)
    up = up_ref[...].astype(F32) + up_other_ref[...].astype(F32)
    for d in range(64):
        dp, y, x = d // 16, d // 4 % 4, d % 4
        keep = jnp.where(my_y == y, 1.0, 0.0)
        first = 256 + (dp * 4 + x) * 2
        tail = jnp.concatenate([up[first : first + 2, :] * keep, jnp.zeros((SHARD - 82, 128), F32)], axis=0)
        out_ref[d, 64:80, :] = (up[dp * 64 + x * 16 : dp * 64 + (x + 1) * 16, :] * keep).astype(BF)
        out_ref[d, 80:SHARD, :] = tail.astype(BF)
    copy.wait()
    for j in range(4):
        span = slice(j * 1024, (j + 1) * 1024)
        rows = jnp.concatenate([own_s[:, span], other_ref[:, span]], axis=0)
        grad = lax.dot_general(rows, low, TN, preferred_element_type=F32).astype(BF)
        for d in range(16):
            out_ref[j * 16 + d, 0:64, :] = grad[d * 64 : (d + 1) * 64, :]


def grad_chunks(x, other, low, low_other, up, up_other):
    return pl.pallas_call(
        grad_kernel,
        out_shape=jax.ShapeDtypeStruct((64, SHARD, 128), BF),
        in_specs=[pl.BlockSpec(memory_space=pl.ANY)] + [whole()] * 5,
        out_specs=whole(),
        scratch_shapes=[VMEM((BLOCK, 4096), BF), pltpu.SemaphoreType.DMA],
        compiler_params=params(48),
        cost_estimate=pl.CostEstimate(flops=2 * 256 * 4096 * 128, bytes_accessed=4 << 20, transcendentals=0),
    )(x, other, low, low_other, up, up_other)


def gather_kernel(own_ref, other_ref, down_ref, query_ref, value_ref):
    zero = lax.axis_index("core") == 0
    for chip in range(64):
        dp, y, x = chip // 16, chip // 4 % 4, chip % 4
        own, other = own_ref[chip].astype(F32), other_ref[chip].astype(F32)
        for core in range(2):
            part = jnp.where(zero, own, other) if core == 0 else jnp.where(zero, other, own)
            down_ref[core * 4096 + chip * 64 : core * 4096 + (chip + 1) * 64, :] = part[0:64, :]
            column = (y * 8 + core * 4 + dp) * 128
            query_ref[x * 16 : (x + 1) * 16, column : column + 128] = part[64:80, :]
            row = core * 32 + (dp * 4 + x) * 2
            value_ref[row : row + 2, y * 128 : (y + 1) * 128] = part[80:82, :]


def gather_outputs(own, other):
    return pl.pallas_call(
        gather_kernel,
        out_shape=(
            jax.ShapeDtypeStruct((8192, 128), F32),
            jax.ShapeDtypeStruct((64, 4096), F32),
            jax.ShapeDtypeStruct((64, 512), F32),
        ),
        in_specs=[whole(), whole()],
        out_specs=(whole(), whole(), whole()),
        compiler_params=params(32),
        cost_estimate=pl.CostEstimate(flops=1 << 20, bytes_accessed=8 << 20, transcendentals=0),
    )(own, other)


def join_kernel(p0, p1, p2, p3, out_ref):
    for i, piece in enumerate((p0, p1, p2, p3)):
        column = (lax.axis_index("y") + i) % 4 * 1024
        out_ref[0, :, pl.ds(pl.multiple_of(column, 1024), 1024)] = piece[...]


def join_heads(pieces):
    return pl.pallas_call(
        join_kernel,
        out_shape=jax.ShapeDtypeStruct((1, BLOCK, 4096), BF),
        in_specs=[whole()] * 4,
        out_specs=whole(),
        cost_estimate=pl.CostEstimate(flops=0, bytes_accessed=2 << 20, transcendentals=0),
    )(*pieces)


def on_device(
    generated_input,
    frozen_query,
    frozen_key_value,
    adapter_down_weight,
    query_up_weight,
    value_up_weight,
    response_numbers,
    target_replica,
    output_gradient,
):
    me = lax.axis_index("dp")
    my_y = lax.axis_index("y")
    my_core = lax.axis_index("core")
    my_lane = lax.axis_index("x") * 2 + my_core
    places = jnp.arange(4, dtype=jnp.int32)
    swap = [(0, 1), (1, 0)]

    rows = generated_input[0]
    sent, notes = front(target_replica, rows, adapter_down_weight, frozen_key_value[0], response_numbers)

    row = (my_y - places + 4) % 4
    notes = jnp.stack([notes] + [lax.ppermute(notes, "y", turn(d)) for d in range(1, 4)])
    resp = notes[:, 0, :]
    routes = notes[:, 1, 0:16].reshape(4, 4, 4)
    mine = (routes == me).astype(jnp.int32)
    order = (jnp.sum(mine * places[None, :, None], axis=1) * 4 + row[:, None]).reshape(16)
    block = row * 8 + my_lane
    scalar = jnp.concatenate([order, block, resp[:, 0], resp[:, 127], row]).astype(jnp.int32)

    got = lax.all_to_all(sent, ROWS, 0, 0, tiled=True)
    gradient = output_gradient[0]
    dout = []
    for d in range(4):
        part = lax.dynamic_slice_in_dim(gradient, (my_y + d) % 4 * 1024, 1024, 1)
        dout.append(lax.ppermute(part, "y", turn(d)) if d else part)
    wv = lax.dynamic_slice_in_dim(value_up_weight, my_y * 128, 128, 1)
    wq = lax.dynamic_slice_in_dim(query_up_weight, my_y * 1024, 1024, 1)
    packed = pack(scalar, got, notes, wv)
    kv = lax.all_gather(packed, ("x", "core"), axis=0, tiled=False)
    q = lax.all_to_all(
        query_chunks(target_replica, frozen_query[0]), ROWS, 0, 0, tiled=True
    )
    other_half = lax.ppermute(
        lax.dynamic_slice_in_dim(rows, (1 - my_core) * 4096, 4096, 1), "core", swap
    )

    out, send, send_other, up, up_other = attention(scalar, q, got, dout, notes, kv, wv, wq)
    pieces = [out[0]] + [lax.ppermute(out[i], "y", turn(-i)) for i in range(1, 4)]
    up_other = lax.ppermute(up_other, "core", swap)
    send_other = lax.ppermute(send_other, "core", swap)
    send = (send.astype(F32) + send_other.astype(F32)).astype(BF)
    low_back = low_back_of(target_replica, lax.all_to_all(send, CHIP, 0, 0, tiled=True))
    low_other = lax.ppermute(low_back, "core", swap)
    chunks = grad_chunks(rows, other_half, low_back, low_other, up, up_other)
    parts = lax.all_to_all(chunks, CHIP, 0, 0, tiled=True)
    shard = jnp.sum(parts.astype(F32), axis=0).astype(BF)
    shard, pieces[2] = lax.optimization_barrier((shard, pieces[2]))
    own = lax.all_to_all(jnp.broadcast_to(shard[None], parts.shape), CHIP, 0, 0, tiled=True)
    own, pieces[1], pieces[3] = lax.optimization_barrier((own, pieces[1], pieces[3]))
    other = lax.ppermute(own, "core", swap)
    attn_out = join_heads(pieces)
    grad_a, query_up_gradient, value_up_gradient = gather_outputs(own, other)

    return (attn_out, grad_a, query_up_gradient, value_up_gradient)


def solution(mesh):
    grid = Mesh(mesh.devices.reshape(4, 4, 4, 2), ("dp", "y", "x", "core"))
    ctx = ("y", "x", "core")
    return jax.shard_map(
        on_device,
        mesh=grid,
        in_specs=(
            P("dp", ctx, None),
            P("dp", ctx, None),
            P("dp", ctx, None),
            P(),
            P(),
            P(),
            P("dp", ctx),
            P(ctx, None, None),
            P("dp", ctx, None),
        ),
        out_specs=(P("dp", ctx, None), P(), P(), P()),
        check_vma=False,
    )
```

time: 230 us -> 215 us (0.935)
  blocking collectives: 57.8 us -> 0 us
  waiting for transfers between devices: 38.9 us -> 77.2 us
  starting transfers between devices: 51.3 us -> 65.6 us
  Pallas kernels: 54.2 us -> 43.5 us
  local copies, waits for them, and re-layouts: 10.3 us -> 12.9 us
    all_to_all x2 -> x0, blocking collectives: 57.8 us -> none  [the longest x1 30.7 us: on_device(): parts = lax.all_to_all(chunks, CHIP, 0, 0, tiled=True)]
    all_to_all x2 -> x4, waiting for transfers between devices: 10.3 us -> 30.7 us  [the longest x1 19.2 us: on_device(): parts = lax.all_to_all(chunks, CHIP, 0, 0, tiled=True)]
    ppermute x3, waiting for transfers between devices: 4.39 us -> 21.8 us  [on_device(): lax.ppermute(out[i], 'y', turn(-i))]
    all_to_all x2 -> x4, starting transfers between devices: 25.6 us -> 36.5 us  [the longest x1 19 us: on_device(): lax.all_to_all(send, CHIP, 0, 0, tiled=True)]
    ppermute x1 -> x2, starting transfers between devices: 1.28 us -> 5.08 us  [the longest x1 4.16 us: on_device(): send_other = lax.ppermute(send_other, 'core', swap)]
    pallas_call x1, Pallas kernels: 31 us -> 27.4 us  [attention(): pl.pallas_call(attention_kernel, out_shape=(jax.ShapeDtypeStruct((4, BLOC...]
    pallas_call x1, Pallas kernels: 7.03 us -> 3.61 us  [front(): pl.pallas_call(front_kernel, out_shape=(jax.ShapeDtypeStruct((16, QUARTER...]
    unnamed x42, local copies, waits for them, and re-layouts: 2.98 us -> 5.87 us
  transfers between devices with their start and end apart: 17 -> 20, of which waited for: 8 -> 11; matrix products, arithmetic and copies ran while one was open for 3% -> 4% of each run, Pallas kernels for 3% -> 3%
where the time goes in v3:
time: 215 us
  waiting for transfers between devices  77.2 us (36%)
  starting transfers between devices  65.6 us (31%)
  Pallas kernels  43.5 us (20%)
  between operations  14.3 us (7%)
  local copies, waits for them, and re-layouts  12.9 us (6%)
    pallas_call x1, Pallas kernels, attention(): pl.pallas_call(attention_kernel, out_shape=(jax.ShapeDtypeStruct((4, BLOC...  27.4 us
    ppermute x3, waiting for transfers between devices, on_device(): lax.ppermute(out[i], 'y', turn(-i))  21.8 us
    all_to_all x1, waiting for transfers between devices, on_device(): parts = lax.all_to_all(chunks, CHIP, 0, 0, tiled=True)  19.2 us
    all_to_all x1, starting transfers between devices, on_device(): lax.all_to_all(send, CHIP, 0, 0, tiled=True)  19 us
    ppermute x3, waiting for transfers between devices, on_device(): dout.append(lax.ppermute(part, 'y', turn(d)) if d else part)  17.4 us
    all_to_all x1, waiting for transfers between devices, on_device(): lax.all_to_all(send, CHIP, 0, 0, tiled=True)  11.5 us
    all_to_all x1, starting transfers between devices, on_device(): lax.all_to_all(jnp.broadcast_to(shard[None], parts.shape), CHIP, 0, 0, ti...  8.96 us
    all_to_all x1, starting transfers between devices, on_device(): got = lax.all_to_all(sent, ROWS, 0, 0, tiled=True)  6.84 us
  transfers between devices with their start and end apart: 20, of which 11 were waited for; matrix products, arithmetic and copies ran while one was open for 4% of the time, Pallas kernels for 3%

profile of v3, /device:TPU:1, one launch (start us, length us, event | category | flops | bytes accessed | tf_op | source)
XLA Modules:
  0.0 215.5 jit_solution(4569696676139294679)
XLA Ops:
  7.2 3.6 %shard_map.120 = (bf16[16,32,384]{2,1,0:T(8,128)(2,1)}, s32[2,128]{1,0:T(2,128)}) custom-call(s32[1,4,4]{2,1,0:T(4,128)} %route_ref.5, bf16[128,8192]{1,0:T(8,128)(2,1)} %bitcast.27, bf16[8192,128]{1,0:T(8,128)(2,1)} %a_ref.1, bf16[128,1024]{1,0:T(8,128)(2,1)} %bitcast.30, s32[1,128]{1,0:T(1,128)} %resp_ref.1), custom_call_target="tpu_custom_call" | custom-call | flops 268435456 | bytes 5242880 | tf_op jit(solution)/shard_map/pallas_call | solution.py:86
  10.8 3.6 %collective-permute-start.2 = (s32[2,128]{1,0:T(2,128)}, s32[2,128]{1,0:T(2,128)S(1)}, u32[]{:S(2)}, u32[]{:S(2)}) collective-permute-start(s32[2,128]{1,0:T(2,128)} %get-tuple-element.19), channel_id=1, source_target_pairs={{0,24},{8,0},{16,8},{24,16},{1,25},{9,1},{17,9},{25,17},{2,26},{10... | collective-permute-start | bytes 3080 | tf_op jit(solution)/shard_map/ppermute | solution.py:514
  15.5 6.8 %all-to-all-start.1 = ((bf16[16,32,384]{2,1,0:T(8,128)(2,1)}), bf16[16,32,384]{2,1,0:T(8,128)(2,1)S(1)}, u32[]{:S(2)}, u32[]{:S(2)}) async-start(bf16[16,32,384]{2,1,0:T(8,128)(2,1)} %get-tuple-element.20), calls=%async_computation.1 | async-start | bytes 786432 | tf_op jit(solution)/shard_map/all_to_all | solution.py:522
  22.4 1.3 constant_dynamic-slice_fusion.1.wv_ref
  25.5 5.0 %all-to-all-done.1.got_ref = bf16[16,32,384]{2,1,0:T(8,128)(2,1)S(1)} async-done(((bf16[16,32,384]{2,1,0:T(8,128)(2,1)}), bf16[16,32,384]{2,1,0:T(8,128)(2,1)S(1)}, u32[]{:S(2)}, u32[]{:S(2)}) %all-to-all-start.1) | async-done | bytes 393248 | tf_op jit(solution)/shard_map/all_to_all | solution.py:522
  31.3 2.1 shard_map.122
  33.5 1.7 shard_map.121
  35.2 3.7 %all-to-all-start = ((bf16[16,32,1024]{2,1,0:T(8,128)(2,1)}), bf16[16,32,1024]{2,1,0:T(8,128)(2,1)S(1)}, u32[]{:S(2)}, u32[]{:S(2)}) async-start(bf16[16,32,1024]{2,1,0:T(8,128)(2,1)} %shard_map.121), calls=%async_computation | async-start | bytes 2097152 | tf_op jit(solution)/shard_map/all_to_all | solution.py:532
  39.7 2.4 %collective-permute-start.5 = (bf16[128,1024]{1,0:T(8,128)(2,1)S(1)}, bf16[128,1024]{1,0:T(8,128)(2,1)S(1)}, u32[]{:S(2)}, u32[]{:S(2)}) collective-permute-start(bf16[128,1024]{1,0:T(8,128)(2,1)S(1)} %get-tuple-element.40), channel_id=1, source_target_pairs={{0,24},{8,0},{16,8},{24,16},{1,25},{9,1},{17,9},{25,17},{2,26},{10... | collective-permute-start | bytes 786440 | tf_op jit(solution)/shard_map/ppermute | solution.py:527
  42.1 1.7 collective-permute-start.4
  44.6 10.9 %collective-permute-done.5.d3 = bf16[128,1024]{1,0:T(8,128)(2,1)S(1)} collective-permute-done((bf16[128,1024]{1,0:T(8,128)(2,1)S(1)}, bf16[128,1024]{1,0:T(8,128)(2,1)S(1)}, u32[]{:S(2)}, u32[]{:S(2)}) %collective-permute-start.5) | collective-permute-done | bytes 262176 | tf_op jit(solution)/shard_map/ppermute | solution.py:527
  55.4 4.5 %collective-permute-done.3.d1 = bf16[128,1024]{1,0:T(8,128)(2,1)S(1)} collective-permute-done((bf16[128,1024]{1,0:T(8,128)(2,1)S(1)}, bf16[128,1024]{1,0:T(8,128)(2,1)S(1)}, u32[]{:S(2)}, u32[]{:S(2)}) %collective-permute-start.3) | collective-permute-done | bytes 262176 | tf_op jit(solution)/shard_map/ppermute | solution.py:527
  59.9 2.0 collective-permute-done.4.d2
  63.0 27.4 %shard_map.123 = (bf16[4,128,1024]{2,1,0:T(8,128)(2,1)}, bf16[64,32,128]{2,1,0:T(8,128)(2,1)}, bf16[64,32,128]{2,1,0:T(8,128)(2,1)}, bf16[288,128]{1,0:T(8,128)(2,1)}, bf16[288,128]{1,0:T(8,128)(2,1)}) custom-call(s32[32]{0:T(128)} %concatenate.3.scalar_ref, bf16[16,32,1024]{2,1,0:T(8,128)(2,1)} %copy-done.10, bf16[16,32,384]{2,1,0:T(8,128)(2,1)} %copy-done.8, ...), custom_call_target="tpu_custom_call" | custom-call | flops 21474836480 | bytes 8388608 | tf_op jit(solution)/shard_map/pallas_call | solution.py:355
  90.4 4.2 %collective-permute-start.7 = (bf16[64,32,128]{2,1,0:T(8,128)(2,1)}, bf16[64,32,128]{2,1,0:T(8,128)(2,1)S(1)}, u32[]{:S(2)}, u32[]{:S(2)}) collective-permute-start(bf16[64,32,128]{2,1,0:T(8,128)(2,1)} %get-tuple-element.23), channel_id=1, source_target_pairs={{0,1},{1,0},{2,3},{3,2},{4,5},{5,4},{6,7},{7,6},{8,9},{9,8},{10,11... | collective-permute-start | bytes 1572872 | tf_op jit(solution)/shard_map/ppermute | solution.py:542
  97.3 19.0 %all-to-all-start.2 = ((bf16[64,32,128]{2,1,0:T(8,128)(2,1)}), bf16[64,32,128]{2,1,0:T(8,128)(2,1)S(1)}, u32[]{:S(2)}, u32[]{:S(2)}) async-start(bf16[64,32,128]{2,1,0:T(8,128)(2,1)} %add_convert_fusion), calls=%async_computation.2 | async-start | bytes 1048576 | tf_op jit(solution)/shard_map/all_to_all | solution.py:544
  117.3 11.5 %all-to-all-done.2.got_ref = bf16[64,32,128]{2,1,0:T(8,128)(2,1)S(1)} async-done(((bf16[64,32,128]{2,1,0:T(8,128)(2,1)}), bf16[64,32,128]{2,1,0:T(8,128)(2,1)S(1)}, u32[]{:S(2)}, u32[]{:S(2)}) %all-to-all-start.2) | async-done | bytes 524320 | tf_op jit(solution)/shard_map/all_to_all | solution.py:544
  129.5 1.7 shard_map.124.low_ref
  131.3 1.9 collective-permute-start.8
  135.0 2.2 %shard_map.125 = bf16[64,88,128]{2,1,0:T(8,128)(2,1)S(1)} custom-call(bf16[128,8192]{1,0:T(8,128)(2,1)S(1)} %bitcast.28, bf16[128,4096]{1,0:T(8,128)(2,1)} %collective-permute-done.6.other_ref, bf16[128,128]{1,0:T(8,128)(2,1)S(1)} %copy-done.4, bf16[128,128]{1,0:T(8,128)(2,1)S(1)} %collective-permute-done.8.low_other_ref, bf16[288,128]{1,0:T(8,128)(2,1)S(1)} %copy-done.5, ...), custom_call_target="tpu_custom_call" | custom-call | flops 268435456 | bytes 4194304 | tf_op jit(solution)/shard_map/pallas_call | solution.py:436
  137.2 1.1 copy-done.2
  138.3 4.8 %all-to-all-start.3 = ((bf16[64,88,128]{2,1,0:T(8,128)(2,1)}), bf16[64,88,128]{2,1,0:T(8,128)(2,1)S(1)}, u32[]{:S(2)}, u32[]{:S(2)}) async-start(bf16[64,88,128]{2,1,0:T(8,128)(2,1)} %copy-done.2), calls=%async_computation.3 | async-start | bytes 2883584 | tf_op jit(solution)/shard_map/all_to_all | solution.py:547
  144.0 2.5 %collective-permute-start.10 = (bf16[128,1024]{1,0:T(8,128)(2,1)}, bf16[128,1024]{1,0:T(8,128)(2,1)S(1)}, u32[]{:S(2)}, u32[]{:S(2)}) collective-permute-start(bf16[128,1024]{1,0:T(8,128)(2,1)} %get-tuple-element.38), channel_id=1, source_target_pairs={{0,16},{8,24},{16,0},{24,8},{1,17},{9,25},{17,1},{25,9},{2,18},{10... | collective-permute-start | bytes 786440 | tf_op jit(solution)/shard_map/ppermute | solution.py:540
  146.5 19.2 %all-to-all-done.3 = bf16[64,88,128]{2,1,0:T(8,128)(2,1)S(1)} async-done(((bf16[64,88,128]{2,1,0:T(8,128)(2,1)}), bf16[64,88,128]{2,1,0:T(8,128)(2,1)S(1)}, u32[]{:S(2)}, u32[]{:S(2)}) %all-to-all-start.3) | async-done | bytes 1441824 | tf_op jit(solution)/shard_map/all_to_all | solution.py:547
  166.8 1.3 broadcast_in_dim.2
  168.1 9.0 %all-to-all-start.4 = ((bf16[64,88,128]{2,1,0:T(8,128)(2,1)}), bf16[64,88,128]{2,1,0:T(8,128)(2,1)S(1)}, u32[]{:S(2)}, u32[]{:S(2)}) async-start(bf16[64,88,128]{2,1,0:T(8,128)(2,1)} %broadcast_in_dim.2), calls=%async_computation.4 | async-start | bytes 2883584 | tf_op jit(solution)/shard_map/all_to_all | solution.py:550
  177.0 1.1 collective-permute-start.12
  178.1 1.7 collective-permute-start.11
  179.8 20.8 %collective-permute-done.12.p3 = bf16[128,1024]{1,0:T(8,128)(2,1)S(1)} collective-permute-done((bf16[128,1024]{1,0:T(8,128)(2,1)S(1)}, bf16[128,1024]{1,0:T(8,128)(2,1)S(1)}, u32[]{:S(2)}, u32[]{:S(2)}) %collective-permute-start.12) | collective-permute-done | bytes 262176 | tf_op jit(solution)/shard_map/ppermute | solution.py:540
  202.0 1.2 collective-permute-start.13
  203.2 2.2 %shard_map.126 = bf16[1,128,4096]{2,1,0:T(8,128)(2,1)} custom-call(bf16[128,1024]{1,0:T(8,128)(2,1)} %get-tuple-element.39.p0, bf16[128,1024]{1,0:T(8,128)(2,1)} %copy-done.15, bf16[128,1024]{1,0:T(8,128)(2,1)} %copy-done.13, bf16[128,1024]{1,0:T(8,128)(2,1)} %copy-done.14), custom_call_target="tpu_custom_call" | custom-call | bytes 2097152 | tf_op jit(solution)/shard_map/pallas_call | solution.py:483
  206.1 2.5 %shard_map.127 = (f32[8192,128]{1,0:T(8,128)}, f32[64,4096]{1,0:T(8,128)}, f32[64,512]{1,0:T(8,128)}) custom-call(bf16[64,88,128]{2,1,0:T(8,128)(2,1)S(1)} %all-to-all-done.4.own_ref, bf16[64,88,128]{2,1,0:T(8,128)(2,1)S(1)} %collective-permute-done.13.other_ref), custom_call_target="tpu_custom_call" | custom-call | flops 1048576 | bytes 8388608 | tf_op jit(solution)/shard_map/pallas_call | solution.py:462
  (77 shorter events, 16.5 us)
Async XLA Ops:
  7.2 36.7 %copy-start = (bf16[64,4096]{1,0:T(8,128)(2,1)S(1)}, bf16[64,4096]{1,0:T(8,128)(2,1)}, u32[]{:S(2)}) copy-start(bf16[64,4096]{1,0:T(8,128)(2,1)} %param.13) | copy-start | bytes 1572868
  10.8 22.7 %copy-start.3 = (bf16[1,128,4096]{2,1,0:T(8,128)(2,1)S(1)}, bf16[1,128,4096]{2,1,0:T(8,128)(2,1)}, u32[]{:S(2)}) copy-start(bf16[1,128,4096]{2,1,0:T(8,128)(2,1)} %param.10) | copy-start | bytes 3145732
  10.8 22.7 %copy-start.6 = (s32[1,4,4]{2,1,0:T(4,128)S(1)}, s32[1,4,4]{2,1,0:T(4,128)}, u32[]{:S(2)}) copy-start(s32[1,4,4]{2,1,0:T(4,128)} %route_ref.5) | copy-start | bytes 196
  10.8 12.9 %collective-permute-start.2 = (s32[2,128]{1,0:T(2,128)}, s32[2,128]{1,0:T(2,128)S(1)}, u32[]{:S(2)}, u32[]{:S(2)}) collective-permute-start(s32[2,128]{1,0:T(2,128)} %get-tuple-element.19), channel_id=1, source_target_pairs={{0,24},{8,0},{16,8},{24,16},{1,25},{9,1},{17,9},{25,17},{2,26},{10... | collective-permute-start | bytes 3080 | tf_op jit(solution)/shard_map/ppermute | solution.py:514
  14.4 9.3 %collective-permute-start.1 = (s32[2,128]{1,0:T(2,128)}, s32[2,128]{1,0:T(2,128)S(1)}, u32[]{:S(2)}, u32[]{:S(2)}) collective-permute-start(s32[2,128]{1,0:T(2,128)} %get-tuple-element.19), channel_id=1, source_target_pairs={{0,16},{8,24},{16,0},{24,8},{1,17},{9,25},{17,1},{25,9},{2,18},{10... | collective-permute-start | bytes 3080 | tf_op jit(solution)/shard_map/ppermute | solution.py:514
  14.8 9.0 %collective-permute-start = (s32[2,128]{1,0:T(2,128)}, s32[2,128]{1,0:T(2,128)S(1)}, u32[]{:S(2)}, u32[]{:S(2)}) collective-permute-start(s32[2,128]{1,0:T(2,128)} %get-tuple-element.19), channel_id=1, source_target_pairs={{0,8},{8,16},{16,24},{24,0},{1,9},{9,17},{17,25},{25,1},{2,10},{10... | collective-permute-start | bytes 3080 | tf_op jit(solution)/shard_map/ppermute | solution.py:514
  15.5 15.1 %all-to-all-start.1 = ((bf16[16,32,384]{2,1,0:T(8,128)(2,1)}), bf16[16,32,384]{2,1,0:T(8,128)(2,1)S(1)}, u32[]{:S(2)}, u32[]{:S(2)}) async-start(bf16[16,32,384]{2,1,0:T(8,128)(2,1)} %get-tuple-element.20), calls=%async_computation.1 | async-start | bytes 786432 | tf_op jit(solution)/shard_map/all_to_all | solution.py:522
  22.3 39.6 %all-gather.3.cloned.1.call-start = ((), (), s32[]{:S(2)}) async-start(), calls=%async_computation.5 | async-start | bytes 3538944 | tf_op jit(solution)/shard_map/all_gather | solution.py:531
  24.4 6.1 %copy-start.16 = (s32[4,2,128]{2,1,0:T(2,128)}, s32[4,2,128]{2,1,0:T(2,128)S(1)}, u32[]{:S(2)}) copy-start(s32[4,2,128]{2,1,0:T(2,128)S(1)} %pad_add_fusion.notes_ref) | copy-start | bytes 12292
  33.5 5.4 %copy-start.9 = (bf16[1,128,4096]{2,1,0:T(8,128)(2,1)S(1)}, bf16[1,128,4096]{2,1,0:T(8,128)(2,1)}, u32[]{:S(2)}) copy-start(bf16[1,128,4096]{2,1,0:T(8,128)(2,1)} %param.17) | copy-start | bytes 3145732
  35.2 26.8 %all-to-all-start = ((bf16[16,32,1024]{2,1,0:T(8,128)(2,1)}), bf16[16,32,1024]{2,1,0:T(8,128)(2,1)S(1)}, u32[]{:S(2)}, u32[]{:S(2)}) async-start(bf16[16,32,1024]{2,1,0:T(8,128)(2,1)} %shard_map.121), calls=%async_computation | async-start | bytes 2097152 | tf_op jit(solution)/shard_map/all_to_all | solution.py:532
  39.7 15.7 %collective-permute-start.5 = (bf16[128,1024]{1,0:T(8,128)(2,1)S(1)}, bf16[128,1024]{1,0:T(8,128)(2,1)S(1)}, u32[]{:S(2)}, u32[]{:S(2)}) collective-permute-start(bf16[128,1024]{1,0:T(8,128)(2,1)S(1)} %get-tuple-element.40), channel_id=1, source_target_pairs={{0,24},{8,0},{16,8},{24,16},{1,25},{9,1},{17,9},{25,17},{2,26},{10... | collective-permute-start | bytes 786440 | tf_op jit(solution)/shard_map/ppermute | solution.py:527
  42.1 17.8 %collective-permute-start.3 = (bf16[128,1024]{1,0:T(8,128)(2,1)S(1)}, bf16[128,1024]{1,0:T(8,128)(2,1)S(1)}, u32[]{:S(2)}, u32[]{:S(2)}) collective-permute-start(bf16[128,1024]{1,0:T(8,128)(2,1)S(1)} %get-tuple-element.41), channel_id=1, source_target_pairs={{0,8},{8,16},{16,24},{24,0},{1,9},{9,17},{17,25},{25,1},{2,10},{10... | collective-permute-start | bytes 786440 | tf_op jit(solution)/shard_map/ppermute | solution.py:527
  42.1 19.8 %collective-permute-start.4 = (bf16[128,1024]{1,0:T(8,128)(2,1)S(1)}, bf16[128,1024]{1,0:T(8,128)(2,1)S(1)}, u32[]{:S(2)}, u32[]{:S(2)}) collective-permute-start(bf16[128,1024]{1,0:T(8,128)(2,1)S(1)} %get-tuple-element.43), channel_id=1, source_target_pairs={{0,16},{8,24},{16,0},{24,8},{1,17},{9,25},{17,1},{25,9},{2,18},{10... | collective-permute-start | bytes 786440 | tf_op jit(solution)/shard_map/ppermute | solution.py:527
  55.4 6.5 %copy-start.17 = (bf16[128,1024]{1,0:T(8,128)(2,1)}, bf16[128,1024]{1,0:T(8,128)(2,1)S(1)}, u32[]{:S(2)}) copy-start(bf16[128,1024]{1,0:T(8,128)(2,1)S(1)} %collective-permute-done.5.d3) | copy-start | bytes 786436
  59.9 2.1 copy-start.18
  63.0 31.6 %copy-start.1 = (bf16[1,128,8192]{2,1,0:T(8,128)(2,1)S(1)}, bf16[1,128,8192]{2,1,0:T(8,128)(2,1)}, u32[]{:S(2)}) copy-start(bf16[1,128,8192]{2,1,0:T(8,128)(2,1)} %param.9) | copy-start | bytes 6291460
  90.4 5.9 %copy-start.12 = (bf16[64,32,128]{2,1,0:T(8,128)(2,1)S(1)}, bf16[64,32,128]{2,1,0:T(8,128)(2,1)}, u32[]{:S(2)}) copy-start(bf16[64,32,128]{2,1,0:T(8,128)(2,1)} %get-tuple-element.22) | copy-start | bytes 1572868
  90.4 25.9 %copy-start.20 = (bf16[288,128]{1,0:T(8,128)(2,1)S(1)}, bf16[288,128]{1,0:T(8,128)(2,1)}, u32[]{:S(2)}) copy-start(bf16[288,128]{1,0:T(8,128)(2,1)} %get-tuple-element.25) | copy-start | bytes 221188
  90.4 5.9 %collective-permute-start.7 = (bf16[64,32,128]{2,1,0:T(8,128)(2,1)}, bf16[64,32,128]{2,1,0:T(8,128)(2,1)S(1)}, u32[]{:S(2)}, u32[]{:S(2)}) collective-permute-start(bf16[64,32,128]{2,1,0:T(8,128)(2,1)} %get-tuple-element.23), channel_id=1, source_target_pairs={{0,1},{1,0},{2,3},{3,2},{4,5},{5,4},{6,7},{7,6},{8,9},{9,8},{10,11... | collective-permute-start | bytes 1572872 | tf_op jit(solution)/shard_map/ppermute | solution.py:542
  95.6 38.6 %copy-start.5 = (bf16[288,128]{1,0:T(8,128)(2,1)S(1)}, bf16[288,128]{1,0:T(8,128)(2,1)}, u32[]{:S(2)}) copy-start(bf16[288,128]{1,0:T(8,128)(2,1)} %get-tuple-element.24.up_ref) | copy-start | bytes 221188
  95.6 37.5 %collective-permute-start.6 = (bf16[128,4096]{1,0:T(8,128)(2,1)}, bf16[128,4096]{1,0:T(8,128)(2,1)}, u32[]{:S(2)}, u32[]{:S(2)}) collective-permute-start(bf16[128,4096]{1,0:T(8,128)(2,1)} %dynamic-slice_bitcast_fusion), channel_id=1, source_target_pairs={{0,1},{1,0},{2,3},{3,2},{4,5},{5,4},{6,7},{7,6},{8,9},{9,8},{10,11... | collective-permute-start | bytes 3145736 | tf_op jit(solution)/shard_map/ppermute | solution.py:535
  97.3 31.5 %all-to-all-start.2 = ((bf16[64,32,128]{2,1,0:T(8,128)(2,1)}), bf16[64,32,128]{2,1,0:T(8,128)(2,1)S(1)}, u32[]{:S(2)}, u32[]{:S(2)}) async-start(bf16[64,32,128]{2,1,0:T(8,128)(2,1)} %add_convert_fusion), calls=%async_computation.2 | async-start | bytes 1048576 | tf_op jit(solution)/shard_map/all_to_all | solution.py:544
  116.3 16.8 %collective-permute-start.9 = (bf16[288,128]{1,0:T(8,128)(2,1)S(1)}, bf16[288,128]{1,0:T(8,128)(2,1)S(1)}, u32[]{:S(2)}, u32[]{:S(2)}) collective-permute-start(bf16[288,128]{1,0:T(8,128)(2,1)S(1)} %copy-done.20), channel_id=1, source_target_pairs={{0,1},{1,0},{2,3},{3,2},{4,5},{5,4},{6,7},{7,6},{8,9},{9,8},{10,11... | collective-permute-start | bytes 221192 | tf_op jit(solution)/shard_map/ppermute | solution.py:541
  131.3 3.0 %collective-permute-start.8 = (bf16[128,128]{1,0:T(8,128)(2,1)}, bf16[128,128]{1,0:T(8,128)(2,1)S(1)}, u32[]{:S(2)}, u32[]{:S(2)}) collective-permute-start(bf16[128,128]{1,0:T(8,128)(2,1)} %shard_map.124.low_ref), channel_id=1, source_target_pairs={{0,1},{1,0},{2,3},{3,2},{4,5},{5,4},{6,7},{7,6},{8,9},{9,8},{10,11... | collective-permute-start | bytes 98312 | tf_op jit(solution)/shard_map/ppermute | solution.py:545
  138.3 4.8 %copy-start.11 = (bf16[4,128,1024]{2,1,0:T(8,128)(2,1)S(1)}, bf16[4,128,1024]{2,1,0:T(8,128)(2,1)}, u32[]{:S(2)}) copy-start(bf16[4,128,1024]{2,1,0:T(8,128)(2,1)} %get-tuple-element.21) | copy-start | bytes 3145732
  138.3 27.3 %all-to-all-start.3 = ((bf16[64,88,128]{2,1,0:T(8,128)(2,1)}), bf16[64,88,128]{2,1,0:T(8,128)(2,1)S(1)}, u32[]{:S(2)}, u32[]{:S(2)}) async-start(bf16[64,88,128]{2,1,0:T(8,128)(2,1)} %copy-done.2), calls=%async_computation.3 | async-start | bytes 2883584 | tf_op jit(solution)/shard_map/all_to_all | solution.py:547
  144.0 22.8 %collective-permute-start.10 = (bf16[128,1024]{1,0:T(8,128)(2,1)}, bf16[128,1024]{1,0:T(8,128)(2,1)S(1)}, u32[]{:S(2)}, u32[]{:S(2)}) collective-permute-start(bf16[128,1024]{1,0:T(8,128)(2,1)} %get-tuple-element.38), channel_id=1, source_target_pairs={{0,16},{8,24},{16,0},{24,8},{1,17},{9,25},{17,1},{25,9},{2,18},{10... | collective-permute-start | bytes 786440 | tf_op jit(solution)/shard_map/ppermute | solution.py:540
  168.1 33.9 %all-to-all-start.4 = ((bf16[64,88,128]{2,1,0:T(8,128)(2,1)}), bf16[64,88,128]{2,1,0:T(8,128)(2,1)S(1)}, u32[]{:S(2)}, u32[]{:S(2)}) async-start(bf16[64,88,128]{2,1,0:T(8,128)(2,1)} %broadcast_in_dim.2), calls=%async_computation.4 | async-start | bytes 2883584 | tf_op jit(solution)/shard_map/all_to_all | solution.py:550
  177.0 23.6 %collective-permute-start.12 = (bf16[128,1024]{1,0:T(8,128)(2,1)S(1)}, bf16[128,1024]{1,0:T(8,128)(2,1)S(1)}, u32[]{:S(2)}, u32[]{:S(2)}) collective-permute-start(bf16[128,1024]{1,0:T(8,128)(2,1)S(1)} %get-tuple-element.36), channel_id=1, source_target_pairs={{0,8},{8,16},{16,24},{24,0},{1,9},{9,17},{17,25},{25,1},{2,10},{10... | collective-permute-start | bytes 786440 | tf_op jit(solution)/shard_map/ppermute | solution.py:540
  178.1 22.5 %collective-permute-start.11 = (bf16[128,1024]{1,0:T(8,128)(2,1)S(1)}, bf16[128,1024]{1,0:T(8,128)(2,1)S(1)}, u32[]{:S(2)}, u32[]{:S(2)}) collective-permute-start(bf16[128,1024]{1,0:T(8,128)(2,1)S(1)} %get-tuple-element.37), channel_id=1, source_target_pairs={{0,24},{8,0},{16,8},{24,16},{1,25},{9,1},{17,9},{25,17},{2,26},{10... | collective-permute-start | bytes 786440 | tf_op jit(solution)/shard_map/ppermute | solution.py:540
  202.0 4.1 %collective-permute-start.13 = (bf16[64,88,128]{2,1,0:T(8,128)(2,1)S(1)}, bf16[64,88,128]{2,1,0:T(8,128)(2,1)S(1)}, u32[]{:S(2)}, u32[]{:S(2)}) collective-permute-start(bf16[64,88,128]{2,1,0:T(8,128)(2,1)S(1)} %all-to-all-done.4.own_ref), channel_id=1, source_target_pairs={{0,1},{1,0},{2,3},{3,2},{4,5},{5,4},{6,7},{7,6},{8,9},{9,8},{10,11... | collective-permute-start | bytes 4325384 | tf_op jit(solution)/shard_map/ppermute | solution.py:552
  (9 other events, 7.9 us)
Sparse Core Ops, SparseCore 0:
  33.6 27.8 all-gather.2

commit v4 on v3

--- a/solution.py
+++ b/solution.py
@@ -27,7 +27,6 @@
 VMEM = pltpu.VMEM
 CHIP = ("dp", "y", "x")
 ROWS = ("dp", "y")
-SHARD = 88
 
 
 def turn(d):
@@ -170,9 +169,9 @@
 def attention_kernel(
     scalar_ref, q_ref, got_ref, d0, d1, d2, d3, notes_ref, kv_ref, wv_ref, wq_ref,
     out_ref, send_ref, send_other_ref, up_ref, up_other_ref,
-    kv_s, s_s, w_s, t_s, m_s, acc_s, dq_s, dout_s, lg_s, qup_s, vup_s, send_s, up_s, below_s, sem,
+    q_s, kv_s, s_s, w_s, t_s, m_s, acc_s, dq_s, dout_s, lg_s, qup_s, vup_s, send_s, up_s, below_s, sem,
 ):
-    copies = []
+    copies = [pltpu.make_async_copy(q_ref, q_s, sem.at[32])]
     for c in range(32):
         copies.append(
             pltpu.make_async_copy(
@@ -219,7 +218,7 @@
 
         chunks = [scalar_ref[i * 4 + k] for k in range(4)]
         low = jnp.concatenate([got_ref[c, :, 256:384] for c in chunks], axis=0)
-        q_in = jnp.concatenate([q_ref[c] for c in chunks], axis=0).astype(F32)
+        q_in = jnp.concatenate([q_s[c] for c in chunks], axis=0).astype(F32)
         query = (
             q_in + SCALE * jnp.dot(low[:, 0:64], wq_ref[...], preferred_element_type=F32)
         ).astype(BF)
@@ -361,11 +360,12 @@
             jax.ShapeDtypeStruct((288, 128), BF),
             jax.ShapeDtypeStruct((288, 128), BF),
         ),
-        in_specs=[scalars()]
-        + [whole()] * 7
+        in_specs=[scalars(), pl.BlockSpec(memory_space=pl.ANY)]
+        + [whole()] * 6
         + [pl.BlockSpec(memory_space=pl.ANY), whole(), whole()],
         out_specs=(whole(),) * 5,
         scratch_shapes=[
+            VMEM((16, QUARTER, 1024), BF),
             VMEM((PAD + 4096, 384), BF),
             VMEM((chunks, ROWS_STEP, KEY_CHUNK), F32),
             VMEM((chunks, ROWS_STEP, KEY_CHUNK), BF),
@@ -380,7 +380,7 @@
             VMEM((2, 64, QUARTER, 128), BF),
             VMEM((2, 288, 128), BF),
             pltpu.SMEM((4,), jnp.int32),
-            pltpu.SemaphoreType.DMA((32,)),
+            pltpu.SemaphoreType.DMA((33,)),
         ],
         compiler_params=params(56),
         cost_estimate=pl.CostEstimate(flops=20 << 30, bytes_accessed=8 << 20, transcendentals=8 << 20),
@@ -394,71 +394,72 @@
         for c in range(1, 16):
             total = total + got_ref[r * 16 + c].astype(F32)
         sum_ref[r] = total
+    outgoing = route_ref[0, pl.ds(me, 1), :]
     for k in range(4):
-        low_ref[k * QUARTER : (k + 1) * QUARTER, :] = sum_ref[route_ref[0, me, k]].astype(BF)
+        low = jnp.zeros((QUARTER, 128), F32)
+        for r in range(4):
+            low = jnp.where(outgoing[:, k : k + 1] == r, sum_ref[r], low)
+        low_ref[k * QUARTER : (k + 1) * QUARTER, :] = low.astype(BF)
 
 
 def low_back_of(route, got):
     return pl.pallas_call(
         low_back_kernel,
         out_shape=jax.ShapeDtypeStruct((BLOCK, 128), BF),
-        in_specs=[scalars(), whole()],
-        out_specs=whole(),
+        grid=(1,),
+        in_specs=[
+            pl.BlockSpec((1, 4, 4), lambda i: (0, 0, 0)),
+            pl.BlockSpec((64, QUARTER, 128), lambda i: (0, 0, 0)),
+        ],
+        out_specs=pl.BlockSpec((BLOCK, 128), lambda i: (0, 0)),
         scratch_shapes=[VMEM((4, QUARTER, 128), F32)],
         cost_estimate=pl.CostEstimate(flops=1 << 19, bytes_accessed=1 << 20, transcendentals=0),
     )(route, got)
 
 
-def grad_kernel(x_ref, other_ref, low_ref, low_other_ref, up_ref, up_other_ref, out_ref, own_s, sem):
+def grad_kernel(x_ref, other_ref, low_ref, low_other_ref, out_ref, own_s, sem):
     half = pl.ds(pl.multiple_of(lax.axis_index("core") * 4096, 4096), 4096)
     copy = pltpu.make_async_copy(x_ref.at[:, half], own_s, sem)
     copy.start()
-    my_y = lax.axis_index("y")
     low = jnp.concatenate([low_ref[...], low_other_ref[...]], axis=0)
-    up = up_ref[...].astype(F32) + up_other_ref[...].astype(F32)
-    for d in range(64):
-        dp, y, x = d // 16, d // 4 % 4, d % 4
-        keep = jnp.where(my_y == y, 1.0, 0.0)
-        first = 256 + (dp * 4 + x) * 2
-        tail = jnp.concatenate([up[first : first + 2, :] * keep, jnp.zeros((SHARD - 82, 128), F32)], axis=0)
-        out_ref[d, 64:80, :] = (up[dp * 64 + x * 16 : dp * 64 + (x + 1) * 16, :] * keep).astype(BF)
-        out_ref[d, 80:SHARD, :] = tail.astype(BF)
     copy.wait()
     for j in range(4):
         span = slice(j * 1024, (j + 1) * 1024)
         rows = jnp.concatenate([own_s[:, span], other_ref[:, span]], axis=0)
         grad = lax.dot_general(rows, low, TN, preferred_element_type=F32).astype(BF)
         for d in range(16):
-            out_ref[j * 16 + d, 0:64, :] = grad[d * 64 : (d + 1) * 64, :]
-
-
-def grad_chunks(x, other, low, low_other, up, up_other):
+            out_ref[j * 16 + d] = grad[d * 64 : (d + 1) * 64, :]
+
+
+def grad_chunks(x, other, low, low_other):
     return pl.pallas_call(
         grad_kernel,
-        out_shape=jax.ShapeDtypeStruct((64, SHARD, 128), BF),
-        in_specs=[pl.BlockSpec(memory_space=pl.ANY)] + [whole()] * 5,
+        out_shape=jax.ShapeDtypeStruct((64, 64, 128), BF),
+        in_specs=[pl.BlockSpec(memory_space=pl.ANY)] + [whole()] * 3,
         out_specs=whole(),
         scratch_shapes=[VMEM((BLOCK, 4096), BF), pltpu.SemaphoreType.DMA],
         compiler_params=params(48),
         cost_estimate=pl.CostEstimate(flops=2 * 256 * 4096 * 128, bytes_accessed=4 << 20, transcendentals=0),
-    )(x, other, low, low_other, up, up_other)
-
-
-def gather_kernel(own_ref, other_ref, down_ref, query_ref, value_ref):
+    )(x, other, low, low_other)
+
+
+def gather_kernel(own_ref, other_ref, up_ref, up_other_ref, down_ref, query_ref, value_ref):
     zero = lax.axis_index("core") == 0
-    for chip in range(64):
-        dp, y, x = chip // 16, chip // 4 % 4, chip % 4
-        own, other = own_ref[chip].astype(F32), other_ref[chip].astype(F32)
-        for core in range(2):
+    for core in range(2):
+        for chip in range(64):
+            own, other = own_ref[chip].astype(F32), other_ref[chip].astype(F32)
             part = jnp.where(zero, own, other) if core == 0 else jnp.where(zero, other, own)
-            down_ref[core * 4096 + chip * 64 : core * 4096 + (chip + 1) * 64, :] = part[0:64, :]
-            column = (y * 8 + core * 4 + dp) * 128
-            query_ref[x * 16 : (x + 1) * 16, column : column + 128] = part[64:80, :]
-            row = core * 32 + (dp * 4 + x) * 2
-            value_ref[row : row + 2, y * 128 : (y + 1) * 128] = part[80:82, :]
-
-
-def gather_outputs(own, other):
+            down_ref[core * 4096 + chip * 64 : core * 4096 + (chip + 1) * 64, :] = part
+        for y in range(4):
+            own, other = up_ref[y].astype(F32), up_other_ref[y].astype(F32)
+            part = jnp.where(zero, own, other) if core == 0 else jnp.where(zero, other, own)
+            for h in range(4):
+                column = (y * 8 + core * 4 + h) * 128
+                query_ref[:, column : column + 128] = part[h * 64 : (h + 1) * 64, :]
+            value_ref[core * 32 : (core + 1) * 32, y * 128 : (y + 1) * 128] = part[256:288, :]
+
+
+def gather_outputs(own, other, up, up_other):
     return pl.pallas_call(
         gather_kernel,
         out_shape=(
@@ -466,11 +467,11 @@
             jax.ShapeDtypeStruct((64, 4096), F32),
             jax.ShapeDtypeStruct((64, 512), F32),
         ),
-        in_specs=[whole(), whole()],
+        in_specs=[whole()] * 4,
         out_specs=(whole(), whole(), whole()),
         compiler_params=params(32),
         cost_estimate=pl.CostEstimate(flops=1 << 20, bytes_accessed=8 << 20, transcendentals=0),
-    )(own, other)
+    )(own, other, up, up_other)
 
 
 def join_kernel(p0, p1, p2, p3, out_ref):
@@ -483,8 +484,10 @@
     return pl.pallas_call(
         join_kernel,
         out_shape=jax.ShapeDtypeStruct((1, BLOCK, 4096), BF),
-        in_specs=[whole()] * 4,
-        out_specs=whole(),
+        grid=(1,),
+        in_specs=[pl.BlockSpec((BLOCK, 1024), lambda i: (0, 0))] * 4,
+        out_specs=pl.BlockSpec((1, BLOCK, 4096), lambda i: (0, 0, 0)),
+        compiler_params=params(60),
         cost_estimate=pl.CostEstimate(flops=0, bytes_accessed=2 << 20, transcendentals=0),
     )(*pieces)
 
@@ -539,19 +542,24 @@
     out, send, send_other, up, up_other = attention(scalar, q, got, dout, notes, kv, wv, wq)
     pieces = [out[0]] + [lax.ppermute(out[i], "y", turn(-i)) for i in range(1, 4)]
     up_other = lax.ppermute(up_other, "core", swap)
+    up = (up.astype(F32) + up_other.astype(F32)).astype(BF)
+    up = sum([lax.ppermute(up, "dp", turn(d)).astype(F32) for d in range(1, 4)], up.astype(F32)).astype(BF)
+    up = lax.all_gather(up, ("y", "x"), axis=0, tiled=False)
+    up = jnp.sum(up.reshape(4, 4, 288, 128).astype(F32), axis=1).astype(BF)
+    up_other = lax.ppermute(up, "core", swap)
     send_other = lax.ppermute(send_other, "core", swap)
     send = (send.astype(F32) + send_other.astype(F32)).astype(BF)
     low_back = low_back_of(target_replica, lax.all_to_all(send, CHIP, 0, 0, tiled=True))
     low_other = lax.ppermute(low_back, "core", swap)
-    chunks = grad_chunks(rows, other_half, low_back, low_other, up, up_other)
+    chunks = grad_chunks(rows, other_half, low_back, low_other)
     parts = lax.all_to_all(chunks, CHIP, 0, 0, tiled=True)
     shard = jnp.sum(parts.astype(F32), axis=0).astype(BF)
-    shard, pieces[2] = lax.optimization_barrier((shard, pieces[2]))
+    shard, pieces[1], pieces[3] = lax.optimization_barrier((shard, pieces[1], pieces[3]))
     own = lax.all_to_all(jnp.broadcast_to(shard[None], parts.shape), CHIP, 0, 0, tiled=True)
-    own, pieces[1], pieces[3] = lax.optimization_barrier((own, pieces[1], pieces[3]))
+    own, pieces[2], up_other = lax.optimization_barrier((own, pieces[2], up_other))
     other = lax.ppermute(own, "core", swap)
     attn_out = join_heads(pieces)
-    grad_a, query_up_gradient, value_up_gradient = gather_outputs(own, other)
+    grad_a, query_up_gradient, value_up_gradient = gather_outputs(own, other, up, up_other)
 
     return (attn_out, grad_a, query_up_gradient, value_up_gradient)
 

time: 215 us -> 213 us (level)
  waiting for transfers between devices: 77.2 us -> 69.3 us
  Pallas kernels: 43.5 us -> 49.1 us
    all_to_all x1, starting transfers between devices: 19 us -> 12.3 us  [on_device(): lax.all_to_all(send, CHIP, 0, 0, tiled=True)]
    ppermute x0 -> x4, starting transfers between devices: none -> 6.49 us  [the longest x3 5.5 us: on_device(): lax.ppermute(up, 'dp', turn(d)).astype(F32)]
    pallas_call x1, Pallas kernels: 27.4 us -> 32.8 us  [attention(): pl.pallas_call(attention_kernel, out_shape=(jax.ShapeDtypeStruct((4, BLOC...]
    ppermute x1, starting transfers between devices: 4.16 us -> 0.09 us  [on_device(): send_other = lax.ppermute(send_other, 'core', swap)]
    all_to_all x1, waiting for transfers between devices: 19.2 us -> 15.8 us  [on_device(): parts = lax.all_to_all(chunks, CHIP, 0, 0, tiled=True)]
    ppermute x1, starting transfers between devices: 0.91 us -> 4.15 us  [on_device(): up_other = lax.ppermute(up_other, 'core', swap)]
    ppermute x3, waiting for transfers between devices: 21.8 us -> 18.8 us  [on_device(): lax.ppermute(out[i], 'y', turn(-i))]
    unnamed x42 -> x40, local copies, waits for them, and re-layouts: 5.87 us -> 4.34 us
  transfers between devices with their start and end apart: 20 -> 25, of which waited for: 11 -> 9; matrix products, arithmetic and copies ran while one was open for 4% -> 5% of each run, Pallas kernels for 3% -> 4%
where the time goes in v4:
time: 213 us; the launch traced here: 214 us
  waiting for transfers between devices  69.3 us (33%)
  starting transfers between devices  65.4 us (31%)
  Pallas kernels  49.1 us (23%)
  between operations  14.4 us (7%)
  local copies, waits for them, and re-layouts  11.3 us (5%)
  other arithmetic  4.12 us (2%)
    pallas_call x1, Pallas kernels, attention(): pl.pallas_call(attention_kernel, out_shape=(jax.ShapeDtypeStruct((4, BLOC...  32.8 us
    ppermute x3, waiting for transfers between devices, on_device(): lax.ppermute(out[i], 'y', turn(-i))  18.8 us
    ppermute x3, waiting for transfers between devices, on_device(): dout.append(lax.ppermute(part, 'y', turn(d)) if d else part)  17.4 us
    all_to_all x1, waiting for transfers between devices, on_device(): parts = lax.all_to_all(chunks, CHIP, 0, 0, tiled=True)  15.8 us
    all_to_all x1, starting transfers between devices, on_device(): lax.all_to_all(send, CHIP, 0, 0, tiled=True)  12.3 us
    all_to_all x1, waiting for transfers between devices, on_device(): lax.all_to_all(send, CHIP, 0, 0, tiled=True)  11.1 us
    all_to_all x1, starting transfers between devices, on_device(): lax.all_to_all(jnp.broadcast_to(shard[None], parts.shape), CHIP, 0, 0, ti...  8.65 us
    all_to_all x1, starting transfers between devices, on_device(): got = lax.all_to_all(sent, ROWS, 0, 0, tiled=True)  6.84 us
  transfers between devices with their start and end apart: 25, of which 9 were waited for; matrix products, arithmetic and copies ran while one was open for 5% of the time, Pallas kernels for 4%

profile of v4, /device:TPU:1, one launch (start us, length us, event | category | flops | bytes accessed | tf_op | source)
XLA Modules:
  0.0 213.6 jit_solution(11645649371075538764)
XLA Ops:
  7.2 3.6 %shard_map.120 = (bf16[16,32,384]{2,1,0:T(8,128)(2,1)}, s32[2,128]{1,0:T(2,128)}) custom-call(s32[1,4,4]{2,1,0:T(4,128)} %route_ref.5, bf16[128,8192]{1,0:T(8,128)(2,1)} %bitcast.28, bf16[8192,128]{1,0:T(8,128)(2,1)} %a_ref.1, bf16[128,1024]{1,0:T(8,128)(2,1)} %bitcast.32, s32[1,128]{1,0:T(1,128)} %resp_ref.1), custom_call_target="tpu_custom_call" | custom-call | flops 268435456 | bytes 5242880 | tf_op jit(solution)/shard_map/pallas_call | solution.py:85
  10.8 3.6 %collective-permute-start.2 = (s32[2,128]{1,0:T(2,128)}, s32[2,128]{1,0:T(2,128)S(1)}, u32[]{:S(2)}, u32[]{:S(2)}) collective-permute-start(s32[2,128]{1,0:T(2,128)} %get-tuple-element.20), channel_id=1, source_target_pairs={{0,24},{8,0},{16,8},{24,16},{1,25},{9,1},{17,9},{25,17},{2,26},{10... | collective-permute-start | bytes 3080 | tf_op jit(solution)/shard_map/ppermute | solution.py:517
  15.5 6.8 %all-to-all-start.1 = ((bf16[16,32,384]{2,1,0:T(8,128)(2,1)}), bf16[16,32,384]{2,1,0:T(8,128)(2,1)S(1)}, u32[]{:S(2)}, u32[]{:S(2)}) async-start(bf16[16,32,384]{2,1,0:T(8,128)(2,1)} %get-tuple-element.21), calls=%async_computation.1 | async-start | bytes 786432 | tf_op jit(solution)/shard_map/all_to_all | solution.py:525
  22.4 1.3 constant_dynamic-slice_fusion.1.wv_ref
  25.5 5.0 %all-to-all-done.1.got_ref = bf16[16,32,384]{2,1,0:T(8,128)(2,1)S(1)} async-done(((bf16[16,32,384]{2,1,0:T(8,128)(2,1)}), bf16[16,32,384]{2,1,0:T(8,128)(2,1)S(1)}, u32[]{:S(2)}, u32[]{:S(2)}) %all-to-all-start.1) | async-done | bytes 393248 | tf_op jit(solution)/shard_map/all_to_all | solution.py:525
  31.3 2.1 shard_map.122
  33.5 1.7 shard_map.121
  35.2 3.7 %all-to-all-start = ((bf16[16,32,1024]{2,1,0:T(8,128)(2,1)}), bf16[16,32,1024]{2,1,0:T(8,128)(2,1)S(1)}, u32[]{:S(2)}, u32[]{:S(2)}) async-start(bf16[16,32,1024]{2,1,0:T(8,128)(2,1)} %shard_map.121), calls=%async_computation | async-start | bytes 2097152 | tf_op jit(solution)/shard_map/all_to_all | solution.py:535
  39.7 2.4 %collective-permute-start.5 = (bf16[128,1024]{1,0:T(8,128)(2,1)S(1)}, bf16[128,1024]{1,0:T(8,128)(2,1)S(1)}, u32[]{:S(2)}, u32[]{:S(2)}) collective-permute-start(bf16[128,1024]{1,0:T(8,128)(2,1)S(1)} %get-tuple-element.42), channel_id=1, source_target_pairs={{0,24},{8,0},{16,8},{24,16},{1,25},{9,1},{17,9},{25,17},{2,26},{10... | collective-permute-start | bytes 786440 | tf_op jit(solution)/shard_map/ppermute | solution.py:530
  42.2 1.7 collective-permute-start.4
  44.6 10.9 %collective-permute-done.5.d3 = bf16[128,1024]{1,0:T(8,128)(2,1)S(1)} collective-permute-done((bf16[128,1024]{1,0:T(8,128)(2,1)S(1)}, bf16[128,1024]{1,0:T(8,128)(2,1)S(1)}, u32[]{:S(2)}, u32[]{:S(2)}) %collective-permute-start.5) | collective-permute-done | bytes 262176 | tf_op jit(solution)/shard_map/ppermute | solution.py:530
  55.4 4.5 %collective-permute-done.3.d1 = bf16[128,1024]{1,0:T(8,128)(2,1)S(1)} collective-permute-done((bf16[128,1024]{1,0:T(8,128)(2,1)S(1)}, bf16[128,1024]{1,0:T(8,128)(2,1)S(1)}, u32[]{:S(2)}, u32[]{:S(2)}) %collective-permute-start.3) | collective-permute-done | bytes 262176 | tf_op jit(solution)/shard_map/ppermute | solution.py:530
  59.9 2.0 collective-permute-done.4.d2
  63.0 32.8 %shard_map.123 = (bf16[4,128,1024]{2,1,0:T(8,128)(2,1)}, bf16[64,32,128]{2,1,0:T(8,128)(2,1)}, bf16[64,32,128]{2,1,0:T(8,128)(2,1)}, bf16[288,128]{1,0:T(8,128)(2,1)}, bf16[288,128]{1,0:T(8,128)(2,1)}) custom-call(s32[32]{0:T(128)} %concatenate.3.scalar_ref, bf16[16,32,1024]{2,1,0:T(8,128)(2,1)} %copy-done.9, bf16[16,32,384]{2,1,0:T(8,128)(2,1)} %copy-done.7, ...), custom_call_target="tpu_custom_call" | custom-call | flops 21474836480 | bytes 8388608 | tf_op jit(solution)/shard_map/pallas_call | solution.py:354
  95.8 4.2 %collective-permute-start.12 = (bf16[288,128]{1,0:T(8,128)(2,1)}, bf16[288,128]{1,0:T(8,128)(2,1)S(1)}, u32[]{:S(2)}, u32[]{:S(2)}) collective-permute-start(bf16[288,128]{1,0:T(8,128)(2,1)} %get-tuple-element.28), channel_id=1, source_target_pairs={{0,1},{1,0},{2,3},{3,2},{4,5},{5,4},{6,7},{7,6},{8,9},{9,8},{10,11... | collective-permute-start | bytes 221192 | tf_op jit(solution)/shard_map/ppermute | solution.py:544
  101.6 4.7 %collective-permute-start.14 = (bf16[288,128]{1,0:T(8,128)(2,1)S(1)}, bf16[288,128]{1,0:T(8,128)(2,1)S(1)}, u32[]{:S(2)}, u32[]{:S(2)}) collective-permute-start(bf16[288,128]{1,0:T(8,128)(2,1)S(1)} %add_convert_fusion.2), channel_id=1, source_target_pairs={{0,64},{32,96},{64,0},{96,32},{1,65},{33,97},{65,1},{97,33},{2,66}... | collective-permute-start | bytes 221192 | tf_op jit(solution)/shard_map/ppermute | solution.py:546
  108.0 12.3 %all-to-all-start.2 = ((bf16[64,32,128]{2,1,0:T(8,128)(2,1)}), bf16[64,32,128]{2,1,0:T(8,128)(2,1)S(1)}, u32[]{:S(2)}, u32[]{:S(2)}) async-start(bf16[64,32,128]{2,1,0:T(8,128)(2,1)} %add_convert_fusion), calls=%async_computation.2 | async-start | bytes 1048576 | tf_op jit(solution)/shard_map/all_to_all | solution.py:552
  121.1 11.1 %all-to-all-done.2.got_ref = bf16[64,32,128]{2,1,0:T(8,128)(2,1)S(1)} async-done(((bf16[64,32,128]{2,1,0:T(8,128)(2,1)}), bf16[64,32,128]{2,1,0:T(8,128)(2,1)S(1)}, u32[]{:S(2)}, u32[]{:S(2)}) %all-to-all-start.2) | async-done | bytes 524320 | tf_op jit(solution)/shard_map/all_to_all | solution.py:552
  133.0 1.8 shard_map.124.low_ref
  134.8 2.4 %collective-permute-start.8 = (bf16[128,128]{1,0:T(8,128)(2,1)}, bf16[128,128]{1,0:T(8,128)(2,1)S(1)}, u32[]{:S(2)}, u32[]{:S(2)}) collective-permute-start(bf16[128,128]{1,0:T(8,128)(2,1)} %shard_map.124.low_ref), channel_id=1, source_target_pairs={{0,1},{1,0},{2,3},{3,2},{4,5},{5,4},{6,7},{7,6},{8,9},{9,8},{10,11... | collective-permute-start | bytes 98312 | tf_op jit(solution)/shard_map/ppermute | solution.py:553
  139.1 2.1 shard_map.125
  142.1 4.8 %all-to-all-start.3 = ((bf16[64,64,128]{2,1,0:T(8,128)(2,1)}), bf16[64,64,128]{2,1,0:T(8,128)(2,1)S(1)}, u32[]{:S(2)}, u32[]{:S(2)}) async-start(bf16[64,64,128]{2,1,0:T(8,128)(2,1)} %copy-done.2), calls=%async_computation.3 | async-start | bytes 2097152 | tf_op jit(solution)/shard_map/all_to_all | solution.py:555
  148.8 1.8 collective-permute-start.9
  150.5 15.8 %all-to-all-done.3 = bf16[64,64,128]{2,1,0:T(8,128)(2,1)S(1)} async-done(((bf16[64,64,128]{2,1,0:T(8,128)(2,1)}), bf16[64,64,128]{2,1,0:T(8,128)(2,1)S(1)}, u32[]{:S(2)}, u32[]{:S(2)}) %all-to-all-start.3) | async-done | bytes 1048608 | tf_op jit(solution)/shard_map/all_to_all | solution.py:555
  166.5 4.3 %collective-permute-done.10.p3 = bf16[128,1024]{1,0:T(8,128)(2,1)S(1)} collective-permute-done((bf16[128,1024]{1,0:T(8,128)(2,1)}, bf16[128,1024]{1,0:T(8,128)(2,1)S(1)}, u32[]{:S(2)}, u32[]{:S(2)}) %collective-permute-start.10) | collective-permute-done | bytes 262176 | tf_op jit(solution)/shard_map/ppermute | solution.py:543
  170.8 1.2 broadcast_in_dim.2
  172.0 8.7 %all-to-all-start.4 = ((bf16[64,64,128]{2,1,0:T(8,128)(2,1)}), bf16[64,64,128]{2,1,0:T(8,128)(2,1)S(1)}, u32[]{:S(2)}, u32[]{:S(2)}) async-start(bf16[64,64,128]{2,1,0:T(8,128)(2,1)} %broadcast_in_dim.2), calls=%async_computation.4 | async-start | bytes 2097152 | tf_op jit(solution)/shard_map/all_to_all | solution.py:558
  180.7 1.5 reduce_sum.35.up_ref
  183.2 2.8 %collective-permute-start.11 = (bf16[128,1024]{1,0:T(8,128)(2,1)S(1)}, bf16[128,1024]{1,0:T(8,128)(2,1)S(1)}, u32[]{:S(2)}, u32[]{:S(2)}) collective-permute-start(bf16[128,1024]{1,0:T(8,128)(2,1)S(1)} %get-tuple-element.38), channel_id=1, source_target_pairs={{0,16},{8,24},{16,0},{24,8},{1,17},{9,25},{17,1},{25,9},{2,18},{10... | collective-permute-start | bytes 786440 | tf_op jit(solution)/shard_map/ppermute | solution.py:543
  186.0 14.5 %collective-permute-done.11.p2 = bf16[128,1024]{1,0:T(8,128)(2,1)S(1)} collective-permute-done((bf16[128,1024]{1,0:T(8,128)(2,1)S(1)}, bf16[128,1024]{1,0:T(8,128)(2,1)S(1)}, u32[]{:S(2)}, u32[]{:S(2)}) %collective-permute-start.11) | collective-permute-done | bytes 262176 | tf_op jit(solution)/shard_map/ppermute | solution.py:543
  201.6 2.2 %shard_map.126 = bf16[1,128,4096]{2,1,0:T(8,128)(2,1)} custom-call(bf16[128,1024]{1,0:T(8,128)(2,1)} %get-tuple-element.41.p0, bf16[128,1024]{1,0:T(8,128)(2,1)} %copy-done.13, bf16[128,1024]{1,0:T(8,128)(2,1)} %copy-done.14, bf16[128,1024]{1,0:T(8,128)(2,1)} %copy-done.12), custom_call_target="tpu_custom_call" | custom-call | bytes 2097152 | tf_op jit(solution)/shard_map/pallas_call | solution.py:484
  203.9 2.8 %shard_map.127 = (f32[8192,128]{1,0:T(8,128)}, f32[64,4096]{1,0:T(8,128)}, f32[64,512]{1,0:T(8,128)}) custom-call(bf16[64,64,128]{2,1,0:T(8,128)(2,1)S(1)} %all-to-all-done.4.own_ref, bf16[64,64,128]{2,1,0:T(8,128)(2,1)S(1)} %collective-permute-done.17.other_ref, bf16[4,288,128]{2,1,0:T(8,128)(2,1)S(1)} %reduce_sum.35.up_ref, ...), custom_call_target="tpu_custom_call" | custom-call | flops 1048576 | bytes 8388608 | tf_op jit(solution)/shard_map/pallas_call | solution.py:463
  (89 shorter events, 18.1 us)
Async XLA Ops:
  7.2 36.7 %copy-start = (bf16[64,4096]{1,0:T(8,128)(2,1)S(1)}, bf16[64,4096]{1,0:T(8,128)(2,1)}, u32[]{:S(2)}) copy-start(bf16[64,4096]{1,0:T(8,128)(2,1)} %param.13) | copy-start | bytes 1572868
  10.8 22.7 %copy-start.3 = (bf16[1,128,4096]{2,1,0:T(8,128)(2,1)S(1)}, bf16[1,128,4096]{2,1,0:T(8,128)(2,1)}, u32[]{:S(2)}) copy-start(bf16[1,128,4096]{2,1,0:T(8,128)(2,1)} %param.10) | copy-start | bytes 3145732
  10.8 22.7 %copy-start.5 = (s32[1,4,4]{2,1,0:T(4,128)S(1)}, s32[1,4,4]{2,1,0:T(4,128)}, u32[]{:S(2)}) copy-start(s32[1,4,4]{2,1,0:T(4,128)} %route_ref.5) | copy-start | bytes 196
  10.8 12.9 %collective-permute-start.2 = (s32[2,128]{1,0:T(2,128)}, s32[2,128]{1,0:T(2,128)S(1)}, u32[]{:S(2)}, u32[]{:S(2)}) collective-permute-start(s32[2,128]{1,0:T(2,128)} %get-tuple-element.20), channel_id=1, source_target_pairs={{0,24},{8,0},{16,8},{24,16},{1,25},{9,1},{17,9},{25,17},{2,26},{10... | collective-permute-start | bytes 3080 | tf_op jit(solution)/shard_map/ppermute | solution.py:517
  14.4 9.3 %collective-permute-start.1 = (s32[2,128]{1,0:T(2,128)}, s32[2,128]{1,0:T(2,128)S(1)}, u32[]{:S(2)}, u32[]{:S(2)}) collective-permute-start(s32[2,128]{1,0:T(2,128)} %get-tuple-element.20), channel_id=1, source_target_pairs={{0,16},{8,24},{16,0},{24,8},{1,17},{9,25},{17,1},{25,9},{2,18},{10... | collective-permute-start | bytes 3080 | tf_op jit(solution)/shard_map/ppermute | solution.py:517
  14.8 9.0 %collective-permute-start = (s32[2,128]{1,0:T(2,128)}, s32[2,128]{1,0:T(2,128)S(1)}, u32[]{:S(2)}, u32[]{:S(2)}) collective-permute-start(s32[2,128]{1,0:T(2,128)} %get-tuple-element.20), channel_id=1, source_target_pairs={{0,8},{8,16},{16,24},{24,0},{1,9},{9,17},{17,25},{25,1},{2,10},{10... | collective-permute-start | bytes 3080 | tf_op jit(solution)/shard_map/ppermute | solution.py:517
  15.5 15.1 %all-to-all-start.1 = ((bf16[16,32,384]{2,1,0:T(8,128)(2,1)}), bf16[16,32,384]{2,1,0:T(8,128)(2,1)S(1)}, u32[]{:S(2)}, u32[]{:S(2)}) async-start(bf16[16,32,384]{2,1,0:T(8,128)(2,1)} %get-tuple-element.21), calls=%async_computation.1 | async-start | bytes 786432 | tf_op jit(solution)/shard_map/all_to_all | solution.py:525
  22.3 39.7 %all-gather.5.cloned.1.call-start = ((), (), s32[]{:S(2)}) async-start(), calls=%async_computation.5 | async-start | bytes 3538944 | tf_op jit(solution)/shard_map/all_gather | solution.py:534
  35.2 26.8 %all-to-all-start = ((bf16[16,32,1024]{2,1,0:T(8,128)(2,1)}), bf16[16,32,1024]{2,1,0:T(8,128)(2,1)S(1)}, u32[]{:S(2)}, u32[]{:S(2)}) async-start(bf16[16,32,1024]{2,1,0:T(8,128)(2,1)} %shard_map.121), calls=%async_computation | async-start | bytes 2097152 | tf_op jit(solution)/shard_map/all_to_all | solution.py:535
  39.7 15.7 %collective-permute-start.5 = (bf16[128,1024]{1,0:T(8,128)(2,1)S(1)}, bf16[128,1024]{1,0:T(8,128)(2,1)S(1)}, u32[]{:S(2)}, u32[]{:S(2)}) collective-permute-start(bf16[128,1024]{1,0:T(8,128)(2,1)S(1)} %get-tuple-element.42), channel_id=1, source_target_pairs={{0,24},{8,0},{16,8},{24,16},{1,25},{9,1},{17,9},{25,17},{2,26},{10... | collective-permute-start | bytes 786440 | tf_op jit(solution)/shard_map/ppermute | solution.py:530
  42.2 17.8 %collective-permute-start.3 = (bf16[128,1024]{1,0:T(8,128)(2,1)S(1)}, bf16[128,1024]{1,0:T(8,128)(2,1)S(1)}, u32[]{:S(2)}, u32[]{:S(2)}) collective-permute-start(bf16[128,1024]{1,0:T(8,128)(2,1)S(1)} %get-tuple-element.43), channel_id=1, source_target_pairs={{0,8},{8,16},{16,24},{24,0},{1,9},{9,17},{17,25},{25,1},{2,10},{10... | collective-permute-start | bytes 786440 | tf_op jit(solution)/shard_map/ppermute | solution.py:530
  42.2 19.8 %collective-permute-start.4 = (bf16[128,1024]{1,0:T(8,128)(2,1)S(1)}, bf16[128,1024]{1,0:T(8,128)(2,1)S(1)}, u32[]{:S(2)}, u32[]{:S(2)}) collective-permute-start(bf16[128,1024]{1,0:T(8,128)(2,1)S(1)} %get-tuple-element.45), channel_id=1, source_target_pairs={{0,16},{8,24},{16,0},{24,8},{1,17},{9,25},{17,1},{25,9},{2,18},{10... | collective-permute-start | bytes 786440 | tf_op jit(solution)/shard_map/ppermute | solution.py:530
  63.0 37.0 %copy-start.1 = (bf16[1,128,8192]{2,1,0:T(8,128)(2,1)S(1)}, bf16[1,128,8192]{2,1,0:T(8,128)(2,1)}, u32[]{:S(2)}) copy-start(bf16[1,128,8192]{2,1,0:T(8,128)(2,1)} %param.9) | copy-start | bytes 6291460
  95.8 11.3 %copy-start.11 = (bf16[64,32,128]{2,1,0:T(8,128)(2,1)S(1)}, bf16[64,32,128]{2,1,0:T(8,128)(2,1)}, u32[]{:S(2)}) copy-start(bf16[64,32,128]{2,1,0:T(8,128)(2,1)} %get-tuple-element.23) | copy-start | bytes 1572868
  95.8 5.7 %collective-permute-start.12 = (bf16[288,128]{1,0:T(8,128)(2,1)}, bf16[288,128]{1,0:T(8,128)(2,1)S(1)}, u32[]{:S(2)}, u32[]{:S(2)}) collective-permute-start(bf16[288,128]{1,0:T(8,128)(2,1)} %get-tuple-element.28), channel_id=1, source_target_pairs={{0,1},{1,0},{2,3},{3,2},{4,5},{5,4},{6,7},{7,6},{8,9},{9,8},{10,11... | collective-permute-start | bytes 221192 | tf_op jit(solution)/shard_map/ppermute | solution.py:544
  100.0 7.1 %collective-permute-start.7 = (bf16[64,32,128]{2,1,0:T(8,128)(2,1)}, bf16[64,32,128]{2,1,0:T(8,128)(2,1)S(1)}, u32[]{:S(2)}, u32[]{:S(2)}) collective-permute-start(bf16[64,32,128]{2,1,0:T(8,128)(2,1)} %get-tuple-element.24), channel_id=1, source_target_pairs={{0,1},{1,0},{2,3},{3,2},{4,5},{5,4},{6,7},{7,6},{8,9},{9,8},{10,11... | collective-permute-start | bytes 1572872 | tf_op jit(solution)/shard_map/ppermute | solution.py:550
  101.1 36.1 %collective-permute-start.6 = (bf16[128,4096]{1,0:T(8,128)(2,1)}, bf16[128,4096]{1,0:T(8,128)(2,1)}, u32[]{:S(2)}, u32[]{:S(2)}) collective-permute-start(bf16[128,4096]{1,0:T(8,128)(2,1)} %dynamic-slice_bitcast_fusion), channel_id=1, source_target_pairs={{0,1},{1,0},{2,3},{3,2},{4,5},{5,4},{6,7},{7,6},{8,9},{9,8},{10,11... | collective-permute-start | bytes 3145736 | tf_op jit(solution)/shard_map/ppermute | solution.py:538
  101.5 18.8 %collective-permute-start.15 = (bf16[288,128]{1,0:T(8,128)(2,1)S(1)}, bf16[288,128]{1,0:T(8,128)(2,1)S(1)}, u32[]{:S(2)}, u32[]{:S(2)}) collective-permute-start(bf16[288,128]{1,0:T(8,128)(2,1)S(1)} %add_convert_fusion.2), channel_id=1, source_target_pairs={{0,96},{32,0},{64,32},{96,64},{1,97},{33,1},{65,33},{97,65},{2,98}... | collective-permute-start | bytes 221192 | tf_op jit(solution)/shard_map/ppermute | solution.py:546
  101.6 18.8 %collective-permute-start.14 = (bf16[288,128]{1,0:T(8,128)(2,1)S(1)}, bf16[288,128]{1,0:T(8,128)(2,1)S(1)}, u32[]{:S(2)}, u32[]{:S(2)}) collective-permute-start(bf16[288,128]{1,0:T(8,128)(2,1)S(1)} %add_convert_fusion.2), channel_id=1, source_target_pairs={{0,64},{32,96},{64,0},{96,32},{1,65},{33,97},{65,1},{97,33},{2,66}... | collective-permute-start | bytes 221192 | tf_op jit(solution)/shard_map/ppermute | solution.py:546
  106.3 14.1 %collective-permute-start.13 = (bf16[288,128]{1,0:T(8,128)(2,1)S(1)}, bf16[288,128]{1,0:T(8,128)(2,1)S(1)}, u32[]{:S(2)}, u32[]{:S(2)}) collective-permute-start(bf16[288,128]{1,0:T(8,128)(2,1)S(1)} %add_convert_fusion.2), channel_id=1, source_target_pairs={{0,32},{32,64},{64,96},{96,0},{1,33},{33,65},{65,97},{97,1},{2,34}... | collective-permute-start | bytes 221192 | tf_op jit(solution)/shard_map/ppermute | solution.py:546
  108.0 24.3 %all-to-all-start.2 = ((bf16[64,32,128]{2,1,0:T(8,128)(2,1)}), bf16[64,32,128]{2,1,0:T(8,128)(2,1)S(1)}, u32[]{:S(2)}, u32[]{:S(2)}) async-start(bf16[64,32,128]{2,1,0:T(8,128)(2,1)} %add_convert_fusion), calls=%async_computation.2 | async-start | bytes 1048576 | tf_op jit(solution)/shard_map/all_to_all | solution.py:552
  120.3 60.4 %all-gather.7.cloned.1.call-start = ((), (), s32[]{:S(2)}) async-start(), calls=%async_computation.6 | async-start | bytes 1253376 | tf_op jit(solution)/shard_map/all_gather | solution.py:547
  134.8 3.5 %collective-permute-start.8 = (bf16[128,128]{1,0:T(8,128)(2,1)}, bf16[128,128]{1,0:T(8,128)(2,1)S(1)}, u32[]{:S(2)}, u32[]{:S(2)}) collective-permute-start(bf16[128,128]{1,0:T(8,128)(2,1)} %shard_map.124.low_ref), channel_id=1, source_target_pairs={{0,1},{1,0},{2,3},{3,2},{4,5},{5,4},{6,7},{7,6},{8,9},{9,8},{10,11... | collective-permute-start | bytes 98312 | tf_op jit(solution)/shard_map/ppermute | solution.py:553
  142.1 24.2 %all-to-all-start.3 = ((bf16[64,64,128]{2,1,0:T(8,128)(2,1)}), bf16[64,64,128]{2,1,0:T(8,128)(2,1)S(1)}, u32[]{:S(2)}, u32[]{:S(2)}) async-start(bf16[64,64,128]{2,1,0:T(8,128)(2,1)} %copy-done.2), calls=%async_computation.3 | async-start | bytes 2097152 | tf_op jit(solution)/shard_map/all_to_all | solution.py:555
  147.8 22.9 %collective-permute-start.10 = (bf16[128,1024]{1,0:T(8,128)(2,1)}, bf16[128,1024]{1,0:T(8,128)(2,1)S(1)}, u32[]{:S(2)}, u32[]{:S(2)}) collective-permute-start(bf16[128,1024]{1,0:T(8,128)(2,1)} %get-tuple-element.39), channel_id=1, source_target_pairs={{0,8},{8,16},{16,24},{24,0},{1,9},{9,17},{17,25},{25,1},{2,10},{10... | collective-permute-start | bytes 786440 | tf_op jit(solution)/shard_map/ppermute | solution.py:543
  148.8 22.0 %collective-permute-start.9 = (bf16[128,1024]{1,0:T(8,128)(2,1)S(1)}, bf16[128,1024]{1,0:T(8,128)(2,1)S(1)}, u32[]{:S(2)}, u32[]{:S(2)}) collective-permute-start(bf16[128,1024]{1,0:T(8,128)(2,1)S(1)} %get-tuple-element.40), channel_id=1, source_target_pairs={{0,24},{8,0},{16,8},{24,16},{1,25},{9,1},{17,9},{25,17},{2,26},{10... | collective-permute-start | bytes 786440 | tf_op jit(solution)/shard_map/ppermute | solution.py:543
  170.8 11.4 %copy-start.12 = (bf16[128,1024]{1,0:T(8,128)(2,1)}, bf16[128,1024]{1,0:T(8,128)(2,1)S(1)}, u32[]{:S(2)}) copy-start(bf16[128,1024]{1,0:T(8,128)(2,1)S(1)} %collective-permute-done.10.p3) | copy-start | bytes 786436
  170.8 9.9 %copy-start.13 = (bf16[128,1024]{1,0:T(8,128)(2,1)}, bf16[128,1024]{1,0:T(8,128)(2,1)S(1)}, u32[]{:S(2)}) copy-start(bf16[128,1024]{1,0:T(8,128)(2,1)S(1)} %collective-permute-done.9.p1) | copy-start | bytes 786436
  172.0 28.5 %all-to-all-start.4 = ((bf16[64,64,128]{2,1,0:T(8,128)(2,1)}), bf16[64,64,128]{2,1,0:T(8,128)(2,1)S(1)}, u32[]{:S(2)}, u32[]{:S(2)}) async-start(bf16[64,64,128]{2,1,0:T(8,128)(2,1)} %broadcast_in_dim.2), calls=%async_computation.4 | async-start | bytes 2097152 | tf_op jit(solution)/shard_map/all_to_all | solution.py:558
  182.2 18.3 %collective-permute-start.16 = (bf16[4,288,128]{2,1,0:T(8,128)(2,1)S(1)}, bf16[4,288,128]{2,1,0:T(8,128)(2,1)S(1)}, u32[]{:S(2)}, u32[]{:S(2)}) collective-permute-start(bf16[4,288,128]{2,1,0:T(8,128)(2,1)S(1)} %reduce_sum.35.up_ref), channel_id=1, source_target_pairs={{0,1},{1,0},{2,3},{3,2},{4,5},{5,4},{6,7},{7,6},{8,9},{9,8},{10,11... | collective-permute-start | bytes 884744 | tf_op jit(solution)/shard_map/ppermute | solution.py:549
  183.2 17.3 %collective-permute-start.11 = (bf16[128,1024]{1,0:T(8,128)(2,1)S(1)}, bf16[128,1024]{1,0:T(8,128)(2,1)S(1)}, u32[]{:S(2)}, u32[]{:S(2)}) collective-permute-start(bf16[128,1024]{1,0:T(8,128)(2,1)S(1)} %get-tuple-element.38), channel_id=1, source_target_pairs={{0,16},{8,24},{16,0},{24,8},{1,17},{9,25},{17,1},{25,9},{2,18},{10... | collective-permute-start | bytes 786440 | tf_op jit(solution)/shard_map/ppermute | solution.py:543
  200.5 3.4 %collective-permute-start.17 = (bf16[64,64,128]{2,1,0:T(8,128)(2,1)S(1)}, bf16[64,64,128]{2,1,0:T(8,128)(2,1)S(1)}, u32[]{:S(2)}, u32[]{:S(2)}) collective-permute-start(bf16[64,64,128]{2,1,0:T(8,128)(2,1)S(1)} %all-to-all-done.4.own_ref), channel_id=1, source_target_pairs={{0,1},{1,0},{2,3},{3,2},{4,5},{5,4},{6,7},{7,6},{8,9},{9,8},{10,11... | collective-permute-start | bytes 3145736 | tf_op jit(solution)/shard_map/ppermute | solution.py:560
  (13 other events, 36.9 us)
Sparse Core Ops, SparseCore 0:
  33.6 27.8 all-gather.4
  123.9 48.6 all-gather.6

commit v5 on v4

--- a/solution.py
+++ b/solution.py
@@ -552,9 +552,9 @@
     low_back = low_back_of(target_replica, lax.all_to_all(send, CHIP, 0, 0, tiled=True))
     low_other = lax.ppermute(low_back, "core", swap)
     chunks = grad_chunks(rows, other_half, low_back, low_other)
+    chunks, pieces[1], pieces[3] = lax.optimization_barrier((chunks, pieces[1], pieces[3]))
     parts = lax.all_to_all(chunks, CHIP, 0, 0, tiled=True)
     shard = jnp.sum(parts.astype(F32), axis=0).astype(BF)
-    shard, pieces[1], pieces[3] = lax.optimization_barrier((shard, pieces[1], pieces[3]))
     own = lax.all_to_all(jnp.broadcast_to(shard[None], parts.shape), CHIP, 0, 0, tiled=True)
     own, pieces[2], up_other = lax.optimization_barrier((own, pieces[2], up_other))
     other = lax.ppermute(own, "core", swap)

time: 213 us -> 202 us (0.948); the launches traced: 214 us -> 200 us
  waiting for transfers between devices: 69.3 us -> 42.5 us
  blocking collectives: 0 us -> 22.2 us
  Pallas kernels: 49.1 us -> 43.7 us
  starting transfers between devices: 65.4 us -> 61.4 us
    all_to_all x0 -> x1, blocking collectives: none -> 22.2 us  [on_device(): parts = lax.all_to_all(chunks, CHIP, 0, 0, tiled=True)]
    all_to_all x1 -> x0, waiting for transfers between devices: 15.8 us -> none  [on_device(): parts = lax.all_to_all(chunks, CHIP, 0, 0, tiled=True)]
    ppermute x3, waiting for transfers between devices: 18.8 us -> 12.6 us  [on_device(): lax.ppermute(out[i], 'y', turn(-i))]
    pallas_call x1, Pallas kernels: 32.8 us -> 27.3 us  [attention(): pl.pallas_call(attention_kernel, out_shape=(jax.ShapeDtypeStruct((4, BLOC...]
    ppermute x3, starting transfers between devices: 5.5 us -> 10.3 us  [on_device(): lax.ppermute(up, 'dp', turn(d)).astype(F32)]
    all_to_all x1 -> x0, starting transfers between devices: 4.79 us -> none  [on_device(): parts = lax.all_to_all(chunks, CHIP, 0, 0, tiled=True)]
    all_to_all x1, waiting for transfers between devices: 11.1 us -> 6.41 us  [on_device(): lax.all_to_all(send, CHIP, 0, 0, tiled=True)]
    all_to_all x1, starting transfers between devices: 8.65 us -> 4.65 us  [on_device(): lax.all_to_all(jnp.broadcast_to(shard[None], parts.shape), CHIP, 0, 0, ti...]
  transfers between devices with their start and end apart: 25 -> 24, of which waited for: 9 -> 7; matrix products, arithmetic and copies ran while one was open for 5% -> 6% of each run, Pallas kernels for 4% -> 4%
where the time goes in v5:
time: 202 us; the launch traced here: 200 us
  starting transfers between devices  61.4 us (30%)
  Pallas kernels  43.7 us (22%)
  waiting for transfers between devices  42.5 us (21%)
  blocking collectives  22.2 us (11%)
  between operations  14.4 us (7%)
  local copies, waits for them, and re-layouts  11.7 us (6%)
  other arithmetic  4.12 us (2%)
    pallas_call x1, Pallas kernels, attention(): pl.pallas_call(attention_kernel, out_shape=(jax.ShapeDtypeStruct((4, BLOC...  27.3 us
    all_to_all x1, blocking collectives, on_device(): parts = lax.all_to_all(chunks, CHIP, 0, 0, tiled=True)  22.2 us
    ppermute x3, waiting for transfers between devices, on_device(): dout.append(lax.ppermute(part, 'y', turn(d)) if d else part)  17.4 us
    ppermute x3, waiting for transfers between devices, on_device(): lax.ppermute(out[i], 'y', turn(-i))  12.6 us
    ppermute x3, starting transfers between devices, on_device(): lax.ppermute(up, 'dp', turn(d)).astype(F32)  10.3 us
    all_to_all x1, starting transfers between devices, on_device(): lax.all_to_all(send, CHIP, 0, 0, tiled=True)  9.52 us
    all_to_all x1, starting transfers between devices, on_device(): got = lax.all_to_all(sent, ROWS, 0, 0, tiled=True)  6.84 us
    all_to_all x1, waiting for transfers between devices, on_device(): lax.all_to_all(send, CHIP, 0, 0, tiled=True)  6.41 us
  transfers between devices with their start and end apart: 24, of which 7 were waited for; matrix products, arithmetic and copies ran while one was open for 6% of the time, Pallas kernels for 4%

profile of v5, /device:TPU:1, one launch (start us, length us, event | category | flops | bytes accessed | tf_op | source)
XLA Modules:
  0.0 200.0 jit_solution(3273182630644188579)
XLA Ops:
  7.2 3.6 %shard_map.120 = (bf16[16,32,384]{2,1,0:T(8,128)(2,1)}, s32[2,128]{1,0:T(2,128)}) custom-call(s32[1,4,4]{2,1,0:T(4,128)} %route_ref.5, bf16[128,8192]{1,0:T(8,128)(2,1)} %bitcast.28, bf16[8192,128]{1,0:T(8,128)(2,1)} %a_ref.1, bf16[128,1024]{1,0:T(8,128)(2,1)} %bitcast.32, s32[1,128]{1,0:T(1,128)} %resp_ref.1), custom_call_target="tpu_custom_call" | custom-call | flops 268435456 | bytes 5242880 | tf_op jit(solution)/shard_map/pallas_call | solution.py:85
  10.8 3.6 %collective-permute-start.2 = (s32[2,128]{1,0:T(2,128)}, s32[2,128]{1,0:T(2,128)S(1)}, u32[]{:S(2)}, u32[]{:S(2)}) collective-permute-start(s32[2,128]{1,0:T(2,128)} %get-tuple-element.20), channel_id=1, source_target_pairs={{0,24},{8,0},{16,8},{24,16},{1,25},{9,1},{17,9},{25,17},{2,26},{10... | collective-permute-start | bytes 3080 | tf_op jit(solution)/shard_map/ppermute | solution.py:517
  15.5 6.8 %all-to-all-start.1 = ((bf16[16,32,384]{2,1,0:T(8,128)(2,1)}), bf16[16,32,384]{2,1,0:T(8,128)(2,1)S(1)}, u32[]{:S(2)}, u32[]{:S(2)}) async-start(bf16[16,32,384]{2,1,0:T(8,128)(2,1)} %get-tuple-element.21), calls=%async_computation.1 | async-start | bytes 786432 | tf_op jit(solution)/shard_map/all_to_all | solution.py:525
  25.6 5.0 %all-to-all-done.1.got_ref = bf16[16,32,384]{2,1,0:T(8,128)(2,1)S(1)} async-done(((bf16[16,32,384]{2,1,0:T(8,128)(2,1)}), bf16[16,32,384]{2,1,0:T(8,128)(2,1)S(1)}, u32[]{:S(2)}, u32[]{:S(2)}) %all-to-all-start.1) | async-done | bytes 393248 | tf_op jit(solution)/shard_map/all_to_all | solution.py:525
  31.3 2.1 %shard_map.122 = bf16[4,128,384]{2,1,0:T(8,128)(2,1)} custom-call(s32[32]{0:T(128)} %concatenate.3.scalar_ref, bf16[16,32,384]{2,1,0:T(8,128)(2,1)} %copy-done.6, s32[4,2,128]{2,1,0:T(2,128)} %copy-done.14, bf16[64,128]{1,0:T(8,128)(2,1)} %constant_dynamic-slice_fusion.1.wv_ref), custom_call_target="tpu_custom_call" | custom-call | flops 8388608 | bytes 1048576 | tf_op jit(solution)/shard_map/pallas_call | solution.py:160
  33.5 1.7 shard_map.121
  35.2 3.7 %all-to-all-start = ((bf16[16,32,1024]{2,1,0:T(8,128)(2,1)}), bf16[16,32,1024]{2,1,0:T(8,128)(2,1)S(1)}, u32[]{:S(2)}, u32[]{:S(2)}) async-start(bf16[16,32,1024]{2,1,0:T(8,128)(2,1)} %shard_map.121), calls=%async_computation | async-start | bytes 2097152 | tf_op jit(solution)/shard_map/all_to_all | solution.py:535
  39.7 2.4 %collective-permute-start.5 = (bf16[128,1024]{1,0:T(8,128)(2,1)S(1)}, bf16[128,1024]{1,0:T(8,128)(2,1)S(1)}, u32[]{:S(2)}, u32[]{:S(2)}) collective-permute-start(bf16[128,1024]{1,0:T(8,128)(2,1)S(1)} %get-tuple-element.42), channel_id=1, source_target_pairs={{0,24},{8,0},{16,8},{24,16},{1,25},{9,1},{17,9},{25,17},{2,26},{10... | collective-permute-start | bytes 786440 | tf_op jit(solution)/shard_map/ppermute | solution.py:530
  42.1 1.7 collective-permute-start.4
  44.6 10.9 %collective-permute-done.5.d3 = bf16[128,1024]{1,0:T(8,128)(2,1)S(1)} collective-permute-done((bf16[128,1024]{1,0:T(8,128)(2,1)S(1)}, bf16[128,1024]{1,0:T(8,128)(2,1)S(1)}, u32[]{:S(2)}, u32[]{:S(2)}) %collective-permute-start.5) | collective-permute-done | bytes 262176 | tf_op jit(solution)/shard_map/ppermute | solution.py:530
  55.4 4.5 %collective-permute-done.3.d1 = bf16[128,1024]{1,0:T(8,128)(2,1)S(1)} collective-permute-done((bf16[128,1024]{1,0:T(8,128)(2,1)S(1)}, bf16[128,1024]{1,0:T(8,128)(2,1)S(1)}, u32[]{:S(2)}, u32[]{:S(2)}) %collective-permute-start.3) | collective-permute-done | bytes 262176 | tf_op jit(solution)/shard_map/ppermute | solution.py:530
  59.9 2.0 %collective-permute-done.4.d2 = bf16[128,1024]{1,0:T(8,128)(2,1)S(1)} collective-permute-done((bf16[128,1024]{1,0:T(8,128)(2,1)S(1)}, bf16[128,1024]{1,0:T(8,128)(2,1)S(1)}, u32[]{:S(2)}, u32[]{:S(2)}) %collective-permute-start.4) | collective-permute-done | bytes 262176 | tf_op jit(solution)/shard_map/ppermute | solution.py:530
  63.0 27.3 %shard_map.123 = (bf16[4,128,1024]{2,1,0:T(8,128)(2,1)}, bf16[64,32,128]{2,1,0:T(8,128)(2,1)}, bf16[64,32,128]{2,1,0:T(8,128)(2,1)}, bf16[288,128]{1,0:T(8,128)(2,1)}, bf16[288,128]{1,0:T(8,128)(2,1)}) custom-call(s32[32]{0:T(128)} %concatenate.3.scalar_ref, bf16[16,32,1024]{2,1,0:T(8,128)(2,1)} %copy-done.8, bf16[16,32,384]{2,1,0:T(8,128)(2,1)} %copy-done.6, ...), custom_call_target="tpu_custom_call" | custom-call | flops 21474836480 | bytes 8388608 | tf_op jit(solution)/shard_map/pallas_call | solution.py:354
  90.4 4.2 %collective-permute-start.12 = (bf16[288,128]{1,0:T(8,128)(2,1)}, bf16[288,128]{1,0:T(8,128)(2,1)S(1)}, u32[]{:S(2)}, u32[]{:S(2)}) collective-permute-start(bf16[288,128]{1,0:T(8,128)(2,1)} %get-tuple-element.28), channel_id=1, source_target_pairs={{0,1},{1,0},{2,3},{3,2},{4,5},{5,4},{6,7},{7,6},{8,9},{9,8},{10,11... | collective-permute-start | bytes 221192 | tf_op jit(solution)/shard_map/ppermute | solution.py:544
  96.1 4.4 %collective-permute-start.15 = (bf16[288,128]{1,0:T(8,128)(2,1)S(1)}, bf16[288,128]{1,0:T(8,128)(2,1)S(1)}, u32[]{:S(2)}, u32[]{:S(2)}) collective-permute-start(bf16[288,128]{1,0:T(8,128)(2,1)S(1)} %add_convert_fusion.2), channel_id=1, source_target_pairs={{0,96},{32,0},{64,32},{96,64},{1,97},{33,1},{65,33},{97,65},{2,98}... | collective-permute-start | bytes 221192 | tf_op jit(solution)/shard_map/ppermute | solution.py:546
  100.5 5.9 %collective-permute-start.14 = (bf16[288,128]{1,0:T(8,128)(2,1)S(1)}, bf16[288,128]{1,0:T(8,128)(2,1)S(1)}, u32[]{:S(2)}, u32[]{:S(2)}) collective-permute-start(bf16[288,128]{1,0:T(8,128)(2,1)S(1)} %add_convert_fusion.2), channel_id=1, source_target_pairs={{0,64},{32,96},{64,0},{96,32},{1,65},{33,97},{65,1},{97,33},{2,66}... | collective-permute-start | bytes 221192 | tf_op jit(solution)/shard_map/ppermute | solution.py:546
  107.4 9.5 %all-to-all-start.2 = ((bf16[64,32,128]{2,1,0:T(8,128)(2,1)}), bf16[64,32,128]{2,1,0:T(8,128)(2,1)S(1)}, u32[]{:S(2)}, u32[]{:S(2)}) async-start(bf16[64,32,128]{2,1,0:T(8,128)(2,1)} %add_convert_fusion), calls=%async_computation.2 | async-start | bytes 1048576 | tf_op jit(solution)/shard_map/all_to_all | solution.py:552
  117.7 2.2 %slice_bitcast_fusion = (bf16[128,1024]{1,0:T(8,128)(2,1)}, bf16[128,1024]{1,0:T(8,128)(2,1)}, bf16[128,1024]{1,0:T(8,128)(2,1)}, bf16[128,1024]{1,0:T(8,128)(2,1)}) fusion(bf16[4,128,1024]{2,1,0:T(8,128)(2,1)} %get-tuple-element.22), kind=kLoop, calls=%fused_computation.2 | loop fusion | bytes 2097152 | tf_op jit(solution)/shard_map/squeeze | solution.py:543
  120.9 1.7 collective-permute-start.9
  122.5 6.4 %all-to-all-done.2.got_ref = bf16[64,32,128]{2,1,0:T(8,128)(2,1)S(1)} async-done(((bf16[64,32,128]{2,1,0:T(8,128)(2,1)}), bf16[64,32,128]{2,1,0:T(8,128)(2,1)S(1)}, u32[]{:S(2)}, u32[]{:S(2)}) %all-to-all-start.2) | async-done | bytes 524320 | tf_op jit(solution)/shard_map/all_to_all | solution.py:552
  129.7 1.8 shard_map.124.low_ref
  131.5 2.3 %collective-permute-start.8 = (bf16[128,128]{1,0:T(8,128)(2,1)}, bf16[128,128]{1,0:T(8,128)(2,1)S(1)}, u32[]{:S(2)}, u32[]{:S(2)}) collective-permute-start(bf16[128,128]{1,0:T(8,128)(2,1)} %shard_map.124.low_ref), channel_id=1, source_target_pairs={{0,1},{1,0},{2,3},{3,2},{4,5},{5,4},{6,7},{7,6},{8,9},{9,8},{10,11... | collective-permute-start | bytes 98312 | tf_op jit(solution)/shard_map/ppermute | solution.py:553
  135.7 2.1 %shard_map.125 = bf16[64,64,128]{2,1,0:T(8,128)(2,1)S(1)} custom-call(bf16[128,8192]{1,0:T(8,128)(2,1)S(1)} %bitcast.29, bf16[128,4096]{1,0:T(8,128)(2,1)} %collective-permute-done.6.other_ref, bf16[128,128]{1,0:T(8,128)(2,1)S(1)} %copy-done.3, bf16[128,128]{1,0:T(8,128)(2,1)S(1)} %collective-permute-done.8.low_other_ref), custom_call_target="tpu_custom_call" | custom-call | flops 268435456 | bytes 4194304 | tf_op jit(solution)/shard_map/pallas_call | solution.py:435
  137.8 22.2 %all_to_all.25 = bf16[64,64,128]{2,1,0:T(8,128)(2,1)S(1)} all-to-all(bf16[64,64,128]{2,1,0:T(8,128)(2,1)S(1)} %shard_map.125), channel_id=1, replica_groups=mesh['dp'=4,'y'=4,'x'=4,'core'=2] {'dp','y','x'}, dimensions={0} | all-to-all | bytes 2097152 | tf_op jit(solution)/shard_map/all_to_all | solution.py:556
  161.4 4.7 %all-to-all-start.4 = ((bf16[64,64,128]{2,1,0:T(8,128)(2,1)}), bf16[64,64,128]{2,1,0:T(8,128)(2,1)S(1)}, u32[]{:S(2)}, u32[]{:S(2)}) async-start(bf16[64,64,128]{2,1,0:T(8,128)(2,1)} %broadcast_in_dim.2), calls=%async_computation.4 | async-start | bytes 2097152 | tf_op jit(solution)/shard_map/all_to_all | solution.py:558
  166.1 1.5 reduce_sum.35.up_ref
  167.6 3.6 %collective-permute-start.16 = (bf16[4,288,128]{2,1,0:T(8,128)(2,1)S(1)}, bf16[4,288,128]{2,1,0:T(8,128)(2,1)S(1)}, u32[]{:S(2)}, u32[]{:S(2)}) collective-permute-start(bf16[4,288,128]{2,1,0:T(8,128)(2,1)S(1)} %reduce_sum.35.up_ref), channel_id=1, source_target_pairs={{0,1},{1,0},{2,3},{3,2},{4,5},{5,4},{6,7},{7,6},{8,9},{9,8},{10,11... | collective-permute-start | bytes 884744 | tf_op jit(solution)/shard_map/ppermute | solution.py:549
  171.1 2.7 %collective-permute-start.11 = (bf16[128,1024]{1,0:T(8,128)(2,1)S(1)}, bf16[128,1024]{1,0:T(8,128)(2,1)S(1)}, u32[]{:S(2)}, u32[]{:S(2)}) collective-permute-start(bf16[128,1024]{1,0:T(8,128)(2,1)S(1)} %copy-done.11), channel_id=1, source_target_pairs={{0,16},{8,24},{16,0},{24,8},{1,17},{9,25},{17,1},{25,9},{2,18},{10... | collective-permute-start | bytes 786440 | tf_op jit(solution)/shard_map/ppermute | solution.py:543
  173.9 12.5 %collective-permute-done.11.p2 = bf16[128,1024]{1,0:T(8,128)(2,1)S(1)} collective-permute-done((bf16[128,1024]{1,0:T(8,128)(2,1)S(1)}, bf16[128,1024]{1,0:T(8,128)(2,1)S(1)}, u32[]{:S(2)}, u32[]{:S(2)}) %collective-permute-start.11) | collective-permute-done | bytes 262176 | tf_op jit(solution)/shard_map/ppermute | solution.py:543
  186.4 1.6 collective-permute-start.17
  188.0 2.2 %shard_map.126 = bf16[1,128,4096]{2,1,0:T(8,128)(2,1)} custom-call(bf16[128,1024]{1,0:T(8,128)(2,1)} %get-tuple-element.41.p0, bf16[128,1024]{1,0:T(8,128)(2,1)} %collective-permute-done.9.p1, bf16[128,1024]{1,0:T(8,128)(2,1)} %copy-done.12, bf16[128,1024]{1,0:T(8,128)(2,1)} %copy-done.10), custom_call_target="tpu_custom_call" | custom-call | bytes 2097152 | tf_op jit(solution)/shard_map/pallas_call | solution.py:484
  190.3 2.8 %shard_map.127 = (f32[8192,128]{1,0:T(8,128)}, f32[64,4096]{1,0:T(8,128)}, f32[64,512]{1,0:T(8,128)}) custom-call(bf16[64,64,128]{2,1,0:T(8,128)(2,1)S(1)} %all-to-all-done.4.own_ref, bf16[64,64,128]{2,1,0:T(8,128)(2,1)S(1)} %collective-permute-done.17.other_ref, bf16[4,288,128]{2,1,0:T(8,128)(2,1)S(1)} %reduce_sum.35.up_ref, ...), custom_call_target="tpu_custom_call" | custom-call | flops 1048576 | bytes 8388608 | tf_op jit(solution)/shard_map/pallas_call | solution.py:463
  (84 shorter events, 16.0 us)
Async XLA Ops:
  7.2 36.7 %copy-start = (bf16[64,4096]{1,0:T(8,128)(2,1)S(1)}, bf16[64,4096]{1,0:T(8,128)(2,1)}, u32[]{:S(2)}) copy-start(bf16[64,4096]{1,0:T(8,128)(2,1)} %param.13) | copy-start | bytes 1572868
  10.8 22.7 %copy-start.2 = (bf16[1,128,4096]{2,1,0:T(8,128)(2,1)S(1)}, bf16[1,128,4096]{2,1,0:T(8,128)(2,1)}, u32[]{:S(2)}) copy-start(bf16[1,128,4096]{2,1,0:T(8,128)(2,1)} %param.10) | copy-start | bytes 3145732
  10.8 22.7 %copy-start.4 = (s32[1,4,4]{2,1,0:T(4,128)S(1)}, s32[1,4,4]{2,1,0:T(4,128)}, u32[]{:S(2)}) copy-start(s32[1,4,4]{2,1,0:T(4,128)} %route_ref.5) | copy-start | bytes 196
  10.8 12.9 %collective-permute-start.2 = (s32[2,128]{1,0:T(2,128)}, s32[2,128]{1,0:T(2,128)S(1)}, u32[]{:S(2)}, u32[]{:S(2)}) collective-permute-start(s32[2,128]{1,0:T(2,128)} %get-tuple-element.20), channel_id=1, source_target_pairs={{0,24},{8,0},{16,8},{24,16},{1,25},{9,1},{17,9},{25,17},{2,26},{10... | collective-permute-start | bytes 3080 | tf_op jit(solution)/shard_map/ppermute | solution.py:517
  14.4 9.3 %collective-permute-start.1 = (s32[2,128]{1,0:T(2,128)}, s32[2,128]{1,0:T(2,128)S(1)}, u32[]{:S(2)}, u32[]{:S(2)}) collective-permute-start(s32[2,128]{1,0:T(2,128)} %get-tuple-element.20), channel_id=1, source_target_pairs={{0,16},{8,24},{16,0},{24,8},{1,17},{9,25},{17,1},{25,9},{2,18},{10... | collective-permute-start | bytes 3080 | tf_op jit(solution)/shard_map/ppermute | solution.py:517
  14.8 9.0 %collective-permute-start = (s32[2,128]{1,0:T(2,128)}, s32[2,128]{1,0:T(2,128)S(1)}, u32[]{:S(2)}, u32[]{:S(2)}) collective-permute-start(s32[2,128]{1,0:T(2,128)} %get-tuple-element.20), channel_id=1, source_target_pairs={{0,8},{8,16},{16,24},{24,0},{1,9},{9,17},{17,25},{25,1},{2,10},{10... | collective-permute-start | bytes 3080 | tf_op jit(solution)/shard_map/ppermute | solution.py:517
  15.5 15.1 %all-to-all-start.1 = ((bf16[16,32,384]{2,1,0:T(8,128)(2,1)}), bf16[16,32,384]{2,1,0:T(8,128)(2,1)S(1)}, u32[]{:S(2)}, u32[]{:S(2)}) async-start(bf16[16,32,384]{2,1,0:T(8,128)(2,1)} %get-tuple-element.21), calls=%async_computation.1 | async-start | bytes 786432 | tf_op jit(solution)/shard_map/all_to_all | solution.py:525
  22.3 39.6 %all-gather.5.cloned.1.call-start = ((), (), s32[]{:S(2)}) async-start(), calls=%async_computation.5 | async-start | bytes 3538944 | tf_op jit(solution)/shard_map/all_gather | solution.py:534
  35.2 26.8 %all-to-all-start = ((bf16[16,32,1024]{2,1,0:T(8,128)(2,1)}), bf16[16,32,1024]{2,1,0:T(8,128)(2,1)S(1)}, u32[]{:S(2)}, u32[]{:S(2)}) async-start(bf16[16,32,1024]{2,1,0:T(8,128)(2,1)} %shard_map.121), calls=%async_computation | async-start | bytes 2097152 | tf_op jit(solution)/shard_map/all_to_all | solution.py:535
  39.7 15.7 %collective-permute-start.5 = (bf16[128,1024]{1,0:T(8,128)(2,1)S(1)}, bf16[128,1024]{1,0:T(8,128)(2,1)S(1)}, u32[]{:S(2)}, u32[]{:S(2)}) collective-permute-start(bf16[128,1024]{1,0:T(8,128)(2,1)S(1)} %get-tuple-element.42), channel_id=1, source_target_pairs={{0,24},{8,0},{16,8},{24,16},{1,25},{9,1},{17,9},{25,17},{2,26},{10... | collective-permute-start | bytes 786440 | tf_op jit(solution)/shard_map/ppermute | solution.py:530
  42.1 17.8 %collective-permute-start.3 = (bf16[128,1024]{1,0:T(8,128)(2,1)S(1)}, bf16[128,1024]{1,0:T(8,128)(2,1)S(1)}, u32[]{:S(2)}, u32[]{:S(2)}) collective-permute-start(bf16[128,1024]{1,0:T(8,128)(2,1)S(1)} %get-tuple-element.43), channel_id=1, source_target_pairs={{0,8},{8,16},{16,24},{24,0},{1,9},{9,17},{17,25},{25,1},{2,10},{10... | collective-permute-start | bytes 786440 | tf_op jit(solution)/shard_map/ppermute | solution.py:530
  42.1 19.8 %collective-permute-start.4 = (bf16[128,1024]{1,0:T(8,128)(2,1)S(1)}, bf16[128,1024]{1,0:T(8,128)(2,1)S(1)}, u32[]{:S(2)}, u32[]{:S(2)}) collective-permute-start(bf16[128,1024]{1,0:T(8,128)(2,1)S(1)} %get-tuple-element.45), channel_id=1, source_target_pairs={{0,16},{8,24},{16,0},{24,8},{1,17},{9,25},{17,1},{25,9},{2,18},{10... | collective-permute-start | bytes 786440 | tf_op jit(solution)/shard_map/ppermute | solution.py:530
  55.4 6.5 %copy-start.15 = (bf16[128,1024]{1,0:T(8,128)(2,1)}, bf16[128,1024]{1,0:T(8,128)(2,1)S(1)}, u32[]{:S(2)}) copy-start(bf16[128,1024]{1,0:T(8,128)(2,1)S(1)} %collective-permute-done.5.d3) | copy-start | bytes 786436
  63.0 31.6 %copy-start.1 = (bf16[1,128,8192]{2,1,0:T(8,128)(2,1)S(1)}, bf16[1,128,8192]{2,1,0:T(8,128)(2,1)}, u32[]{:S(2)}) copy-start(bf16[1,128,8192]{2,1,0:T(8,128)(2,1)} %param.9) | copy-start | bytes 6291460
  90.3 16.1 %copy-start.9 = (bf16[64,32,128]{2,1,0:T(8,128)(2,1)S(1)}, bf16[64,32,128]{2,1,0:T(8,128)(2,1)}, u32[]{:S(2)}) copy-start(bf16[64,32,128]{2,1,0:T(8,128)(2,1)} %get-tuple-element.23) | copy-start | bytes 1572868
  90.4 5.7 %collective-permute-start.12 = (bf16[288,128]{1,0:T(8,128)(2,1)}, bf16[288,128]{1,0:T(8,128)(2,1)S(1)}, u32[]{:S(2)}, u32[]{:S(2)}) collective-permute-start(bf16[288,128]{1,0:T(8,128)(2,1)} %get-tuple-element.28), channel_id=1, source_target_pairs={{0,1},{1,0},{2,3},{3,2},{4,5},{5,4},{6,7},{7,6},{8,9},{9,8},{10,11... | collective-permute-start | bytes 221192 | tf_op jit(solution)/shard_map/ppermute | solution.py:544
  94.5 11.9 %collective-permute-start.7 = (bf16[64,32,128]{2,1,0:T(8,128)(2,1)}, bf16[64,32,128]{2,1,0:T(8,128)(2,1)S(1)}, u32[]{:S(2)}, u32[]{:S(2)}) collective-permute-start(bf16[64,32,128]{2,1,0:T(8,128)(2,1)} %get-tuple-element.24), channel_id=1, source_target_pairs={{0,1},{1,0},{2,3},{3,2},{4,5},{5,4},{6,7},{7,6},{8,9},{9,8},{10,11... | collective-permute-start | bytes 1572872 | tf_op jit(solution)/shard_map/ppermute | solution.py:550
  95.7 38.2 %collective-permute-start.6 = (bf16[128,4096]{1,0:T(8,128)(2,1)}, bf16[128,4096]{1,0:T(8,128)(2,1)}, u32[]{:S(2)}, u32[]{:S(2)}) collective-permute-start(bf16[128,4096]{1,0:T(8,128)(2,1)} %dynamic-slice_bitcast_fusion), channel_id=1, source_target_pairs={{0,1},{1,0},{2,3},{3,2},{4,5},{5,4},{6,7},{7,6},{8,9},{9,8},{10,11... | collective-permute-start | bytes 3145736 | tf_op jit(solution)/shard_map/ppermute | solution.py:538
  96.1 20.8 %collective-permute-start.15 = (bf16[288,128]{1,0:T(8,128)(2,1)S(1)}, bf16[288,128]{1,0:T(8,128)(2,1)S(1)}, u32[]{:S(2)}, u32[]{:S(2)}) collective-permute-start(bf16[288,128]{1,0:T(8,128)(2,1)S(1)} %add_convert_fusion.2), channel_id=1, source_target_pairs={{0,96},{32,0},{64,32},{96,64},{1,97},{33,1},{65,33},{97,65},{2,98}... | collective-permute-start | bytes 221192 | tf_op jit(solution)/shard_map/ppermute | solution.py:546
  100.5 16.5 %collective-permute-start.14 = (bf16[288,128]{1,0:T(8,128)(2,1)S(1)}, bf16[288,128]{1,0:T(8,128)(2,1)S(1)}, u32[]{:S(2)}, u32[]{:S(2)}) collective-permute-start(bf16[288,128]{1,0:T(8,128)(2,1)S(1)} %add_convert_fusion.2), channel_id=1, source_target_pairs={{0,64},{32,96},{64,0},{96,32},{1,65},{33,97},{65,1},{97,33},{2,66}... | collective-permute-start | bytes 221192 | tf_op jit(solution)/shard_map/ppermute | solution.py:546
  106.4 10.5 %collective-permute-start.13 = (bf16[288,128]{1,0:T(8,128)(2,1)S(1)}, bf16[288,128]{1,0:T(8,128)(2,1)S(1)}, u32[]{:S(2)}, u32[]{:S(2)}) collective-permute-start(bf16[288,128]{1,0:T(8,128)(2,1)S(1)} %add_convert_fusion.2), channel_id=1, source_target_pairs={{0,32},{32,64},{64,96},{96,0},{1,33},{33,65},{65,97},{97,1},{2,34}... | collective-permute-start | bytes 221192 | tf_op jit(solution)/shard_map/ppermute | solution.py:546
  107.4 21.6 %all-to-all-start.2 = ((bf16[64,32,128]{2,1,0:T(8,128)(2,1)}), bf16[64,32,128]{2,1,0:T(8,128)(2,1)S(1)}, u32[]{:S(2)}, u32[]{:S(2)}) async-start(bf16[64,32,128]{2,1,0:T(8,128)(2,1)} %add_convert_fusion), calls=%async_computation.2 | async-start | bytes 1048576 | tf_op jit(solution)/shard_map/all_to_all | solution.py:552
  116.9 49.2 %all-gather.7.cloned.1.call-start = ((), (), s32[]{:S(2)}) async-start(), calls=%async_computation.6 | async-start | bytes 1253376 | tf_op jit(solution)/shard_map/all_gather | solution.py:547
  119.9 17.9 %collective-permute-start.10 = (bf16[128,1024]{1,0:T(8,128)(2,1)}, bf16[128,1024]{1,0:T(8,128)(2,1)S(1)}, u32[]{:S(2)}, u32[]{:S(2)}) collective-permute-start(bf16[128,1024]{1,0:T(8,128)(2,1)} %get-tuple-element.39), channel_id=1, source_target_pairs={{0,8},{8,16},{16,24},{24,0},{1,9},{9,17},{17,25},{25,1},{2,10},{10... | collective-permute-start | bytes 786440 | tf_op jit(solution)/shard_map/ppermute | solution.py:543
  120.9 16.9 %collective-permute-start.9 = (bf16[128,1024]{1,0:T(8,128)(2,1)}, bf16[128,1024]{1,0:T(8,128)(2,1)}, u32[]{:S(2)}, u32[]{:S(2)}) collective-permute-start(bf16[128,1024]{1,0:T(8,128)(2,1)} %get-tuple-element.40), channel_id=1, source_target_pairs={{0,24},{8,0},{16,8},{24,16},{1,25},{9,1},{17,9},{25,17},{2,26},{10... | collective-permute-start | bytes 786440 | tf_op jit(solution)/shard_map/ppermute | solution.py:543
  131.5 3.4 %collective-permute-start.8 = (bf16[128,128]{1,0:T(8,128)(2,1)}, bf16[128,128]{1,0:T(8,128)(2,1)S(1)}, u32[]{:S(2)}, u32[]{:S(2)}) collective-permute-start(bf16[128,128]{1,0:T(8,128)(2,1)} %shard_map.124.low_ref), channel_id=1, source_target_pairs={{0,1},{1,0},{2,3},{3,2},{4,5},{5,4},{6,7},{7,6},{8,9},{9,8},{10,11... | collective-permute-start | bytes 98312 | tf_op jit(solution)/shard_map/ppermute | solution.py:553
  137.8 23.6 %copy-start.10 = (bf16[128,1024]{1,0:T(8,128)(2,1)}, bf16[128,1024]{1,0:T(8,128)(2,1)S(1)}, u32[]{:S(2)}) copy-start(bf16[128,1024]{1,0:T(8,128)(2,1)S(1)} %collective-permute-done.10.p3) | copy-start | bytes 786436
  160.2 11.0 %copy-start.11 = (bf16[128,1024]{1,0:T(8,128)(2,1)S(1)}, bf16[128,1024]{1,0:T(8,128)(2,1)}, u32[]{:S(2)}) copy-start(bf16[128,1024]{1,0:T(8,128)(2,1)} %get-tuple-element.38) | copy-start | bytes 786436
  161.4 25.0 %all-to-all-start.4 = ((bf16[64,64,128]{2,1,0:T(8,128)(2,1)}), bf16[64,64,128]{2,1,0:T(8,128)(2,1)S(1)}, u32[]{:S(2)}, u32[]{:S(2)}) async-start(bf16[64,64,128]{2,1,0:T(8,128)(2,1)} %broadcast_in_dim.2), calls=%async_computation.4 | async-start | bytes 2097152 | tf_op jit(solution)/shard_map/all_to_all | solution.py:558
  167.6 18.9 %collective-permute-start.16 = (bf16[4,288,128]{2,1,0:T(8,128)(2,1)S(1)}, bf16[4,288,128]{2,1,0:T(8,128)(2,1)S(1)}, u32[]{:S(2)}, u32[]{:S(2)}) collective-permute-start(bf16[4,288,128]{2,1,0:T(8,128)(2,1)S(1)} %reduce_sum.35.up_ref), channel_id=1, source_target_pairs={{0,1},{1,0},{2,3},{3,2},{4,5},{5,4},{6,7},{7,6},{8,9},{9,8},{10,11... | collective-permute-start | bytes 884744 | tf_op jit(solution)/shard_map/ppermute | solution.py:549
  171.1 15.3 %collective-permute-start.11 = (bf16[128,1024]{1,0:T(8,128)(2,1)S(1)}, bf16[128,1024]{1,0:T(8,128)(2,1)S(1)}, u32[]{:S(2)}, u32[]{:S(2)}) collective-permute-start(bf16[128,1024]{1,0:T(8,128)(2,1)S(1)} %copy-done.11), channel_id=1, source_target_pairs={{0,16},{8,24},{16,0},{24,8},{1,17},{9,25},{17,1},{25,9},{2,18},{10... | collective-permute-start | bytes 786440 | tf_op jit(solution)/shard_map/ppermute | solution.py:543
  186.4 3.9 %collective-permute-start.17 = (bf16[64,64,128]{2,1,0:T(8,128)(2,1)S(1)}, bf16[64,64,128]{2,1,0:T(8,128)(2,1)S(1)}, u32[]{:S(2)}, u32[]{:S(2)}) collective-permute-start(bf16[64,64,128]{2,1,0:T(8,128)(2,1)S(1)} %all-to-all-done.4.own_ref), channel_id=1, source_target_pairs={{0,1},{1,0},{2,3},{3,2},{4,5},{5,4},{6,7},{7,6},{8,9},{9,8},{10,11... | collective-permute-start | bytes 3145736 | tf_op jit(solution)/shard_map/ppermute | solution.py:560
  (10 other events, 25.1 us)
Sparse Core Ops, SparseCore 0:
  33.6 27.8 all-gather.4
  120.4 45.0 all-gather.6
